TPU v7x, 512 devices: a whole 4x8x8 slice. The times are simulated.
512 devices in a mesh: state: 64 (over z, y), seq: 8 (over x, core).
Axes of the slice: x: 4, y: 8, z: 8, core: 2. Of those that a mesh axis runs over, the one named last changes fastest.
Arguments:
- emit_states: bfloat16 [32768, 512], P('state'), may hold values from -7 to 7
- trans_out: bfloat16 [32768, 512], P('state'), may hold values from -7 to 7
- trans_in: bfloat16 [32768, 512], P('state'), may hold values from -0.25 to 0.25
- word_emb: bfloat16 [131072, 512], P('state'), may hold values from -0.25 to 0.25
- word_cluster: int32 [131072], replicated, may hold values from 0 to 127, as said below
- cluster_block: int32 [128], replicated, may hold values from 0 to 127, as said below
- kept_parts: int32 [128, 2], replicated, may hold values from 0 to 7, as said below
- tokens: int32 [512, 128], P(('state', 'seq')), may hold values from 0 to 131071, as said below
Outputs:
- token_loglik: float32 [512], P(('state', 'seq'))
- trans_norm: float32 [8192], P('state')
- emit_norm: float32 [8192], P('state')
Inputs may be any that keep to these rules, and one draw needn't show every extreme that they name: `word_cluster`: within each shard of 2048 consecutive words every cluster holds at least 2 and at most 24 words, and some cluster holds exactly 24. `cluster_block`: A permutation of the blocks. `kept_parts`: each row holds 2 different parts in increasing order. Of the 128 tokens of one device, at most 2 have their word in the clusters of one block, and some block has exactly 2.
All inputs are finite; a program needn't handle non-finite values.
Results may differ from a plain program's by a relative error of at most 0.0003.
Values may be sent and summed in bfloat16 or wider, within the bound.
No kernel may reach another device: no remote copies, remote signals or barrier semaphores. Data moves between devices by JAX's collectives and lax.ppermute only.
A program may use at most 64 MiB of HBM per device.

v0:
```python
import jax
import jax.numpy as jnp
from jax import lax
from jax.experimental import pallas as pl
from jax.experimental.pallas import tpu as pltpu
from jax.sharding import PartitionSpec as P

BS = 256
PART = 32
KP = 2
KW = KP * PART
LANES = 128
RANKS = 3
f32 = jnp.float32
bf16 = jnp.bfloat16


def iota(shape, axis):
    return lax.broadcasted_iota(jnp.int32, shape, axis)


def one_hot(mask):
    return jnp.where(mask, 1.0, 0.0).astype(bf16)


def prep_kernel(
    scal_ref, emit_ref, out_ref, in_ref, word_ref, cluster_ref, table_ref,
    msg_ref, out_kept_ref, emit_kept_ref, in_kept, slot_of,
):
    share = scal_ref[4]
    for blk in range(2):
        for part in range(2):
            src = pl.ds(pl.multiple_of(blk * BS + scal_ref[blk * 2 + part] * PART, PART), PART)
            dst = pl.ds((blk * 2 + part) * PART, PART)
            emit_kept_ref[dst, :] = emit_ref[src, :]
            out_kept_ref[dst, :] = out_ref[src, :]
            in_kept[dst, :] = in_ref[src, :]
    row = iota((16, LANES), 0)
    want = ((row >> 2) & 1) * KW + (row & 3) * 16 + (row >> 3) * 8 + share
    targets = jnp.dot(
        one_hot(iota((16, LANES), 1) == want), in_kept[...], preferred_element_type=f32
    )
    sub = iota((LANES, LANES), 0)
    lane = iota((LANES, LANES), 1)
    sums = jnp.concatenate([one_hot(sub < lane), jnp.ones((LANES, LANES), bf16)], axis=1)
    table = table_ref[...].astype(f32)
    carry = jnp.zeros((LANES, LANES), f32)
    chunks = cluster_ref.shape[0]
    for c in range(chunks):
        hit = sub == cluster_ref[c : c + 1, :]
        counts = jnp.dot(one_hot(hit), sums, preferred_element_type=f32)
        before = counts[:, :LANES] + carry
        carry = carry + counts[:, LANES:]
        rank = jnp.sum(jnp.where(hit, before, 0.0), axis=0, keepdims=True).astype(jnp.int32)
        block = jnp.sum(jnp.where(hit, table, 0.0), axis=0, keepdims=True).astype(jnp.int32)
        x = rank - RANKS * share
        slot = (block >> 1) * 8 + x * 2 + (block & 1)
        slot_of[c : c + 1, :] = jnp.where((x >= 0) & (x < RANKS), slot, -1)
    for tile in range(4):
        rows = sub + tile * LANES
        chosen = jnp.concatenate(
            [one_hot(rows == slot_of[c : c + 1, :]) for c in range(chunks)], axis=1
        )
        words = jnp.dot(chosen, word_ref[...], preferred_element_type=f32)
        for d in range(16):
            both = jnp.concatenate(
                [targets[(d & 1) * 8 : (d & 1) * 8 + 8, :], words[d * 8 : d * 8 + 8, :]], axis=0
            )
            msg_ref[tile * 16 + d] = both.astype(bf16)


def prep(scal, emit_states, trans_out, trans_in, word_emb, clusters, table):
    width = emit_states.shape[1]
    vmem = pl.BlockSpec(memory_space=pltpu.VMEM)
    return pl.pallas_call(
        prep_kernel,
        out_shape=(
            jax.ShapeDtypeStruct((64, 16, width), bf16),
            jax.ShapeDtypeStruct((2 * KW, width), bf16),
            jax.ShapeDtypeStruct((2 * KW, width), bf16),
        ),
        in_specs=[pl.BlockSpec(memory_space=pltpu.SMEM)] + [vmem] * 6,
        out_specs=(vmem, vmem, vmem),
        scratch_shapes=[pltpu.VMEM((2 * KW, width), bf16), pltpu.VMEM((16, LANES), jnp.int32)],
        compiler_params=pltpu.CompilerParams(vmem_limit_bytes=40 * 1024 * 1024),
        name="prep",
    )(scal, emit_states, trans_out, trans_in, word_emb, clusters, table)


def pick_kernel(msg_ref, mat_ref, next_ref, panel_ref, z_ref, ws_ref, sa, sb, words, table):
    for tile in range(4):
        got = msg_ref[tile * 16 : tile * 16 + 16].reshape(256, msg_ref.shape[2])
        res = lax.dot_general(
            got, mat_ref[...], (((1,), (1,)), ((), ())), preferred_element_type=f32
        ).reshape(16, 16, 3 * LANES)
        rows = pl.ds(tile * LANES, LANES)
        sa[rows, :] = jnp.exp(res[:, :8, :LANES]).reshape(LANES, LANES)
        sb[rows, :] = jnp.exp(res[:, :8, LANES : 2 * LANES]).reshape(LANES, LANES)
        words[rows, :] = res[:, 8:, 2 * LANES :].reshape(LANES, LANES)
    low = iota((LANES, LANES), 1) < KW
    for part, ref in enumerate((sa, sb)):
        cols = [ref[pl.ds(j, LANES, stride=4), :] for j in range(4)]
        total = jnp.sum(cols[0] + cols[1] + cols[2] + cols[3], axis=0, keepdims=True)
        z_ref[:, part * LANES : (part + 1) * LANES] = jnp.broadcast_to(total, (8, LANES))
        for pair in range(2):
            first, second = cols[2 * pair], cols[2 * pair + 1]
            left = jnp.where(low, first, pltpu.roll(second, KW, 1))
            right = jnp.where(low, pltpu.roll(first, KW, 1), second)
            lanes = slice(pair * LANES, (pair + 1) * LANES)
            table[(2 * part) * LANES : (2 * part + 1) * LANES, lanes] = left.astype(bf16)
            table[(2 * part + 1) * LANES : (2 * part + 2) * LANES, lanes] = right.astype(bf16)
    ws_ref[...] = jnp.where(
        iota((256, LANES), 1) < KW,
        words[pl.ds(0, 256, stride=2), :],
        words[pl.ds(1, 256, stride=2), :],
    )
    eye = iota((64, 64), 0) == iota((64, 64), 1)
    ones = jnp.ones((64, LANES), bf16)
    lane = iota((512, LANES), 1).astype(f32)
    block_of = (iota((512, LANES), 0) & 7) >> 1

    def step(tile, _):
        asked = next_ref[pl.ds(pl.multiple_of(tile * 8, 8), 8), :]
        spread = jnp.concatenate(
            [jnp.where(eye, asked[d : d + 1, :64], 0.0) for d in range(8)], axis=0
        )
        wanted = jnp.dot(spread.astype(bf16), ones, preferred_element_type=f32)
        hit = wanted == lane
        chosen = jnp.concatenate([one_hot(hit & (block_of == b)) for b in range(4)], axis=1)
        got = jnp.dot(chosen, table[...], preferred_element_type=f32)
        panel_ref[pl.ds(pl.multiple_of(tile * 512, 512), 512), :] = got.astype(bf16)
        return 0

    lax.fori_loop(0, 8, step, 0)


def pick(msg, mat, next_blocks):
    vmem = pl.BlockSpec(memory_space=pltpu.VMEM)
    return pl.pallas_call(
        pick_kernel,
        out_shape=(
            jax.ShapeDtypeStruct((4096, 256), bf16),
            jax.ShapeDtypeStruct((8, 256), f32),
            jax.ShapeDtypeStruct((256, LANES), f32),
        ),
        in_specs=[vmem] * 3,
        out_specs=(vmem, vmem, vmem),
        scratch_shapes=[
            pltpu.VMEM((512, LANES), f32),
            pltpu.VMEM((512, LANES), f32),
            pltpu.VMEM((512, LANES), f32),
            pltpu.VMEM((512, 256), bf16),
        ],
        compiler_params=pltpu.CompilerParams(vmem_limit_bytes=40 * 1024 * 1024),
        name="pick",
    )(msg, mat, next_blocks)


def chain_kernel(slot_ref, panel_ref, ez_ref, out_ref, ya, yb, ge, ga, ping, pong, logs):
    length = slot_ref.shape[0]

    def widen(i, _):
        rows = pl.ds(pl.multiple_of(i * 256, 256), 256)
        got = panel_ref[rows, :].astype(f32)
        ya[rows, :] = got[:, :LANES]
        yb[rows, :] = got[:, LANES:]
        return 0

    lax.fori_loop(0, panel_ref.shape[0] // 256, widen, 0)

    def pull(i, _):
        for u in range(8):
            t = i * 8 + u
            ge[pl.ds(t, 1), :] = ez_ref[pl.ds(slot_ref[t], 1), :]
        return 0

    lax.fori_loop(0, length // 8, pull, 0)
    low = iota((length, LANES), 1) < KW
    raw = ge[...]
    peak = jnp.max(jnp.where(low, raw, -jnp.inf), axis=1, keepdims=True)
    ga[...] = jnp.exp(-0.5 * pltpu.roll(raw, KW, 1))
    ge[...] = jnp.where(low, jnp.exp(jnp.where(low, raw - peak, 0.0)), 0.0)
    shift = jnp.sum(peak, axis=0, keepdims=True)

    def build(i, _):
        for u in range(4):
            t = i * 4 + u
            slot = slot_ref[t]
            rows = pl.ds((slot >> 3) * LANES + (slot & 7), 16, stride=8)
            a, b = ya[rows, :], yb[rows, :]
            norm, emit = ga[pl.ds(t, 1), :], ge[pl.ds(t, 1), :]
            move = jnp.concatenate([a, pltpu.roll(a, KW, 1), b, pltpu.roll(b, KW, 1)], axis=0)
            ping[t] = (((move * norm) * norm) * emit).astype(bf16)
        return 0

    lax.fori_loop(0, length // 4, build, 0)
    last = ge[length - 1 : length, :]
    ping[length - 1] = jnp.where(
        iota((KW, LANES), 0) == iota((KW, LANES), 1), last, 0.0
    ).astype(bf16)

    logs[...] = jnp.ones_like(logs)
    src, dst, count, base = ping, pong, length // 2, 0
    while count >= 1:
        unroll = min(count, 8)

        def level(i, _, src=src, dst=dst, unroll=unroll, base=base):
            for u in range(unroll):
                n = i * unroll + u
                prod = jnp.dot(src[2 * n + 1][:, :KW], src[2 * n], preferred_element_type=f32)
                top = jnp.max(jnp.max(prod, axis=0, keepdims=True), axis=1, keepdims=True)
                dst[n] = (prod * (1.0 / top)).astype(bf16)
                logs[pl.ds(base + n, 1), :] = jnp.broadcast_to(top, (1, LANES))
            return 0

        lax.fori_loop(0, count // unroll, level, 0)
        src, dst, count, base = dst, src, count // 2, base + count
    final = jnp.sum(jnp.sum(src[0].astype(f32), axis=0, keepdims=True), axis=1, keepdims=True)
    scale = jnp.sum(jnp.log(logs[...]), axis=0, keepdims=True)
    out_ref[...] = jnp.broadcast_to(jnp.log(final) + shift + scale, (8, LANES))


def chain(slots, panels, ez):
    length = slots.shape[0]
    vmem = pl.BlockSpec(memory_space=pltpu.VMEM)
    return pl.pallas_call(
        chain_kernel,
        out_shape=jax.ShapeDtypeStruct((8, LANES), f32),
        in_specs=[pl.BlockSpec(memory_space=pltpu.SMEM), vmem, vmem],
        out_specs=vmem,
        scratch_shapes=[
            pltpu.VMEM((4096, LANES), f32),
            pltpu.VMEM((4096, LANES), f32),
            pltpu.VMEM((length, LANES), f32),
            pltpu.VMEM((length, LANES), f32),
            pltpu.VMEM((length, KW, LANES), bf16),
            pltpu.VMEM((length // 2, KW, LANES), bf16),
            pltpu.VMEM((length, LANES), f32),
        ],
        compiler_params=pltpu.CompilerParams(vmem_limit_bytes=40 * 1024 * 1024),
        name="chain",
    )(slots, panels, ez)


def local(
    emit_states, trans_out, trans_in, word_emb, word_cluster, cluster_block, kept_parts, tokens
):
    states = lax.axis_size("state")
    me = lax.axis_index("state")
    share = lax.axis_index("seq")
    odd = me % 2
    blocks = cluster_block.shape[0]
    all_clusters = word_cluster.reshape(states, -1)
    vocab_local = all_clusters.shape[1]
    my_parts = lax.dynamic_slice_in_dim(kept_parts, me * 2, 2, 0).reshape(-1)
    scal = jnp.concatenate([my_parts, share[None].astype(jnp.int32), jnp.zeros((3,), jnp.int32)])
    own_clusters = lax.dynamic_slice_in_dim(word_cluster, me * vocab_local, vocab_local, 0)
    msg, out_kept, emit_kept = prep(
        scal, emit_states, trans_out, trans_in, word_emb,
        own_clusters.reshape(-1, LANES), cluster_block[:, None],
    )
    arrived = lax.all_to_all(msg, "state", split_axis=0, concat_axis=0, tiled=True)
    swap = [(i, i ^ 1) for i in range(states)]
    out_other = lax.ppermute(out_kept, "state", swap)
    mat = jnp.concatenate(
        [
            jnp.where(odd == 0, out_kept, out_other),
            jnp.where(odd == 0, out_other, out_kept),
            emit_kept,
        ],
        axis=0,
    )

    flat = tokens.reshape(-1)
    length = flat.shape[0]
    shard = flat // vocab_local
    cluster = jnp.take(word_cluster, flat)
    shard_rows = jnp.take(all_clusters, shard, axis=0)
    within = flat - shard * vocab_local
    earlier = (shard_rows == cluster[:, None]) & (
        jnp.arange(vocab_local, dtype=jnp.int32)[None, :] < within[:, None]
    )
    rank = jnp.sum(earlier.astype(jnp.int32), axis=1)
    hit = cluster[:, None] == jnp.arange(blocks, dtype=jnp.int32)[None, :]
    block = jnp.sum(jnp.where(hit, cluster_block[None, :], 0), axis=1)
    times = jnp.arange(length, dtype=jnp.int32)
    same = (block[:, None] == block[None, :]) & (times[None, :] < times[:, None])
    slots = block * 2 + jnp.sum(same.astype(jnp.int32), axis=1)
    following = jnp.concatenate([block[1:], block[-1:]])
    key = (rank // RANKS) * 256 + shard * 4 + rank % RANKS
    code = following * 2048 + key
    at = slots[:, None] == jnp.arange(2 * blocks, dtype=jnp.int32)[None, :]
    request = jnp.sum(jnp.where(at, code[:, None], 0), axis=0)
    group = lax.all_gather(request, "seq", axis=0, tiled=False)
    by_pair = group.reshape(8, states // 2, 8).transpose(1, 0, 2).reshape(states // 2, 1, 64)
    asked = lax.all_to_all(
        jnp.repeat(by_pair, 2, axis=0), "state", split_axis=0, concat_axis=0, tiled=True
    )[:, 0, :]

    panels, z_part, ws = pick(arrived, mat, (asked >> 11).astype(f32))
    got = lax.all_to_all(
        panels.reshape(512, 8, 256), ("state", "seq"), split_axis=0, concat_axis=0, tiled=True
    ).reshape(4096, 256)

    z_half = lax.psum(z_part[0], "seq")
    z_all = z_half + lax.ppermute(z_half, "state", swap)
    trans_norm = jnp.log(lax.dynamic_slice_in_dim(z_all, odd * 128, 128, 0))
    my_blocks = me * 2 + jnp.arange(2, dtype=jnp.int32)
    mine = (cluster_block[None, :] == my_blocks[:, None]).astype(jnp.int32)
    my_clusters = jnp.sum(mine * jnp.arange(blocks, dtype=jnp.int32)[None, :], axis=1)
    present = jnp.sum(
        (all_clusters[None, :, :] == my_clusters[:, None, None]).astype(jnp.int32), axis=2
    )
    x = jnp.arange(4, dtype=jnp.int32)
    valid = (x[None, None, :] < RANKS) & (x[None, None, :] + RANKS * share < present[:, :, None])
    valid = jnp.broadcast_to(
        valid.reshape(2, 256).T[:, :, None], (256, 2, KW)
    ).reshape(256, LANES)
    ws = jnp.where(valid, ws, -1e30)
    ws_all = lax.all_gather(ws, "seq", axis=0, tiled=True)
    emit_norm = jnp.log(jnp.sum(jnp.exp(ws_all), axis=0))
    mine_asked = lax.dynamic_slice_in_dim(asked, share * 8 + odd * 4, 4, 1) & 2047
    rows = jnp.take(ws_all, mine_asked.reshape(-1), axis=0) - emit_norm[None, :]
    rows = rows.reshape(states, 2, 2, 2, KW)
    log_emit = jnp.stack([rows[:, 0, :, 0, :], rows[:, 1, :, 1, :]], axis=1)
    norms = jnp.broadcast_to(trans_norm.reshape(1, 2, 1, KW), log_emit.shape)
    ez = lax.all_to_all(
        jnp.concatenate([log_emit, norms], axis=3).reshape(states, 4, LANES),
        "state", split_axis=0, concat_axis=0, tiled=True,
    ).reshape(4 * states, LANES)

    total = chain(slots, got, ez)[0, :1]
    token_loglik = (total - jnp.log(jnp.asarray(KW * blocks, f32))) / length
    return (token_loglik, trans_norm, emit_norm)


def solution(mesh):
    placed = (
        P("state", None),
        P("state", None),
        P("state", None),
        P("state", None),
        P(),
        P(),
        P(),
        P(("state", "seq"), None),
    )
    return jax.shard_map(
        local,
        mesh=mesh,
        in_specs=placed,
        out_specs=(P(("state", "seq")), P("state"), P("state")),
        check_vma=False,
    )
```

profile of v0, /device:TPU:1, one launch (start us, length us, event | category | flops | bytes accessed | tf_op | source)
XLA Modules:
  0.0 240.4 jit_solution(7561742257516384502)
XLA Ops:
  7.2 0.7 fusion.6
  7.9 0.7 compare_and_fusion.1
  8.5 1.9 reshape.323
  10.4 2.1 gather_fusion
  12.6 0.7 bitcast_subtract_fusion
  13.2 0.8 select_reduce_fusion.1
  14.1 0.6 slice.19
  14.7 0.2 convert_reduce_fusion.2
  14.9 3.6 %gather_fusion.1 = s32[128,2048]{1,0:T(8,128)} fusion(s32[64,2048]{1,0:T(8,128)} %reshape.323, s32[1024]{0:T(1024)S(1)} %get-tuple-element.27), kind=kCustom, calls=%fused_computation.1 | custom fusion | bytes 2097664 | tf_op jit(solution)/shard_map/jit(_take)/gather | solution.py:278
  18.5 1.6 convert_reduce_fusion.1
  20.1 0.7 fusion.4
  21.0 14.5 %all-gather.1 = s32[8,1,256]{2,1,0:T(1,128)S(1)} all-gather(s32[1,1,256]{2,1,0:T(1,128)S(1)} %bitcast.64), channel_id=2, replica_groups=mesh['state'=64,'seq'=8] {'seq'}, dimensions={0}, use_global_device_ids=true | all-gather | bytes 9216 | tf_op jit(solution)/shard_map/all_gather | solution.py:294
  35.8 0.7 broadcast_in_dim.108
  36.4 13.6 %all-to-all-start.1 = ((s32[64,1,64]{2,1,0:T(1,128)}), s32[64,1,64]{2,1,0:T(1,128)S(1)}, u32[]{:S(2)}, u32[]{:S(2)}) async-start(s32[64,1,64]{2,1,0:T(1,128)} %bitcast.10), calls=%async_computation.1 | async-start | bytes 65536 | tf_op jit(solution)/shard_map/all_to_all | solution.py:296
  50.3 0.7 dynamic-slice_bitcast_fusion.cluster_ref
  51.3 1.0 copy-done.4
  52.3 3.3 %prep.1 = (bf16[64,16,512]{2,1,0:T(8,128)(2,1)}, bf16[128,512]{1,0:T(8,128)(2,1)S(1)}, bf16[128,512]{1,0:T(8,128)(2,1)S(1)}) custom-call(s32[8]{0:T(128)S(1)} %pad_add_fusion.scal_ref, bf16[512,512]{1,0:T(8,128)(2,1)S(1)} %copy-done.2, bf16[512,512]{1,0:T(8,128)(2,1)S(1)} %copy-done.3, bf16[512,512]{1,0:T(8,128)(2,1)S(1)} %copy-done.4, ...), custom_call_target="tpu_custom_call" | custom-call | tf_op jit(solution)/shard_map/prep/pallas_call | solution.py:75
  55.6 0.7 copy-done.6
  56.3 4.6 %all-to-all-done.1 = s32[64,1,64]{2,1,0:T(1,128)S(1)} async-done(((s32[64,1,64]{2,1,0:T(1,128)}), s32[64,1,64]{2,1,0:T(1,128)S(1)}, u32[]{:S(2)}, u32[]{:S(2)}) %all-to-all-start.1) | async-done | bytes 16416 | tf_op jit(solution)/shard_map/all_to_all | solution.py:296
  60.9 7.6 %all-to-all-start = ((bf16[64,16,512]{2,1,0:T(8,128)(2,1)}), bf16[64,16,512]{2,1,0:T(8,128)(2,1)S(1)}, u32[]{:S(2)}, u32[]{:S(2)}) async-start(bf16[64,16,512]{2,1,0:T(8,128)(2,1)} %get-tuple-element.9), calls=%async_computation | async-start | bytes 2097152 | tf_op jit(solution)/shard_map/all_to_all | solution.py:262
  68.6 2.9 %collective-permute-start = (bf16[128,512]{1,0:T(8,128)(2,1)S(1)}, bf16[128,512]{1,0:T(8,128)(2,1)S(1)}, u32[]{:S(2)}, u32[]{:S(2)}) collective-permute-start(bf16[128,512]{1,0:T(8,128)(2,1)S(1)} %get-tuple-element.10), channel_id=1, source_target_pairs={{0,8},{8,0},{16,24},{24,16},{32,40},{40,32},{48,56},{56,48},{64,72... | collective-permute-start | bytes 393224 | tf_op jit(solution)/shard_map/ppermute | solution.py:264
  71.6 0.2 fusion.2
  71.8 0.3 convert_reduce_fusion
  72.1 0.1 lt.169
  72.5 0.7 copy.50
  73.3 0.6 convert_bitcast_fusion.next_ref
  73.9 20.6 %collective-permute-done = bf16[128,512]{1,0:T(8,128)(2,1)S(1)} collective-permute-done((bf16[128,512]{1,0:T(8,128)(2,1)S(1)}, bf16[128,512]{1,0:T(8,128)(2,1)S(1)}, u32[]{:S(2)}, u32[]{:S(2)}) %collective-permute-start) | collective-permute-done | bytes 131104 | tf_op jit(solution)/shard_map/ppermute | solution.py:264
  94.6 1.4 all-to-all-done.msg_ref
  96.0 0.8 copy-done.5
  96.7 4.3 %pick.1 = (bf16[4096,256]{1,0:T(8,128)(2,1)S(1)}, f32[8,256]{1,0:T(8,128)S(1)}, f32[256,128]{1,0:T(8,128)S(1)}) custom-call(bf16[64,16,512]{2,1,0:T(8,128)(2,1)S(1)} %all-to-all-done.msg_ref, bf16[384,512]{1,0:T(8,128)(2,1)S(1)} %pad_maximum_fusion.mat_ref, f32[64,64]{1,0:T(8,128)S(1)} %copy-done.5), custom_call_target="tpu_custom_call" | custom-call | tf_op jit(solution)/shard_map/pick/pallas_call | solution.py:139
  101.0 1.4 broadcast_select_fusion.2
  102.5 0.5 broadcast.335
  103.0 1.6 fusion.7
  104.8 15.1 %psum.7 = f32[256]{0:T(256)S(1)} all-reduce(f32[256]{0:T(256)S(1)} %bitcast.65), channel_id=1, replica_groups=mesh['state'=64,'seq'=8] {'seq'}, use_global_device_ids=true, to_apply=%region_7.8 | all-reduce | flops 256 | bytes 2048 | tf_op jit(solution)/shard_map/psum | solution.py:305
  119.9 4.0 %collective-permute-start.1 = (f32[256]{0:T(256)S(1)}, f32[256]{0:T(256)S(1)}, u32[]{:S(2)}, u32[]{:S(2)}) collective-permute-start(f32[256]{0:T(256)S(1)} %psum.7), channel_id=1, source_target_pairs={{0,8},{8,0},{16,24},{24,16},{32,40},{40,32},{48,56},{56,48},{64,72... | collective-permute-start | bytes 3080 | tf_op jit(solution)/shard_map/ppermute | solution.py:306
  123.8 0.8 copy.49
  124.6 0.6 collective-permute-done.1
  125.3 4.0 %all-gather.4.cloned.1.call-done = f32[2048,128]{1,0:T(8,128)} async-done(((f32[256,128]{1,0:T(8,128)}), f32[2048,128]{1,0:T(8,128)}) %all-gather.4.cloned.1.call-update) | async-done | bytes 1048592 | tf_op jit(solution)/shard_map/all_gather | solution.py:320
  129.3 2.0 gather_fusion.2
  131.3 0.2 gather.17
  131.6 0.3 exponential_reduce_fusion
  131.9 1.1 select_subtract_fusion
  133.0 0.1 fusion.8
  133.2 0.2 pad_maximum_fusion.1
  133.5 24.1 %all_to_all.20 = f32[64,4,128]{2,1,0:T(4,128)S(1)} all-to-all(f32[64,4,128]{2,1,0:T(4,128)S(1)} %bitcast.56), channel_id=1, replica_groups=mesh['state'=64,'seq'=8] {'state'}, dimensions={0} | all-to-all | bytes 262144 | tf_op jit(solution)/shard_map/all_to_all | solution.py:327
  157.6 64.8 %all_to_all.21 = bf16[512,8,256]{2,1,0:T(8,128)(2,1)S(1)} all-to-all(bf16[512,8,256]{2,1,0:T(8,128)(2,1)S(1)} %bitcast.53), channel_id=1, replica_groups=mesh['state'=64,'seq'=8] {'state','seq'}, dimensions={0} | all-to-all | bytes 4194304 | tf_op jit(solution)/shard_map/all_to_all | solution.py:301
  222.5 8.8 %chain.1 = f32[8,128]{1,0:T(8,128)S(1)} custom-call(s32[128]{0:T(128)S(1)} %multiply_add_fusion.slot_ref, bf16[4096,256]{1,0:T(8,128)(2,1)S(1)} %bitcast.52, f32[256,128]{1,0:T(8,128)S(1)} %bitcast.54), custom_call_target="tpu_custom_call" | custom-call | tf_op jit(solution)/shard_map/chain/pallas_call | solution.py:226
  231.2 0.5 slice.23
  (66 shorter events, 2.0 us)
Async XLA Ops:
  7.2 42.9 %copy-start = (s32[128,2]{0,1:T(2,128)S(1)}, s32[128,2]{0,1:T(2,128)}, u32[]{:S(2)}) copy-start(s32[128,2]{0,1:T(2,128)} %param.14) | copy-start | bytes 3076
  14.9 36.2 %copy-start.11 = (s32[128]{0:T(128)S(1)}, s32[128]{0:T(128)}, u32[]{:S(2)}) copy-start(s32[128]{0:T(128)} %param.13) | copy-start | bytes 1540
  14.9 36.3 %copy-start.1 = (bf16[2048,512]{1,0:T(8,128)(2,1)S(1)}, bf16[2048,512]{1,0:T(8,128)(2,1)}, u32[]{:S(2)}) copy-start(bf16[2048,512]{1,0:T(8,128)(2,1)} %word_ref.1) | copy-start | bytes 6291460
  14.9 36.3 %copy-start.2 = (bf16[512,512]{1,0:T(8,128)(2,1)S(1)}, bf16[512,512]{1,0:T(8,128)(2,1)}, u32[]{:S(2)}) copy-start(bf16[512,512]{1,0:T(8,128)(2,1)} %emit_ref.1) | copy-start | bytes 1572868
  14.9 36.3 %copy-start.3 = (bf16[512,512]{1,0:T(8,128)(2,1)S(1)}, bf16[512,512]{1,0:T(8,128)(2,1)}, u32[]{:S(2)}) copy-start(bf16[512,512]{1,0:T(8,128)(2,1)} %out_ref.1) | copy-start | bytes 1572868
  36.4 24.5 %all-to-all-start.1 = ((s32[64,1,64]{2,1,0:T(1,128)}), s32[64,1,64]{2,1,0:T(1,128)S(1)}, u32[]{:S(2)}, u32[]{:S(2)}) async-start(s32[64,1,64]{2,1,0:T(1,128)} %bitcast.10), calls=%async_computation.1 | async-start | bytes 65536 | tf_op jit(solution)/shard_map/all_to_all | solution.py:296
  51.3 1.0 copy-start.4
  55.6 0.7 copy-start.6
  56.3 15.5 %copy-start.8 = (s32[64,2048]{1,0:T(8,128)S(1)}, s32[64,2048]{1,0:T(8,128)}, u32[]{:S(2)}) copy-start(s32[64,2048]{1,0:T(8,128)} %reshape.323) | copy-start | bytes 1572868
  60.9 33.6 %copy-start.10 = (s32[64,1,64]{2,1,0:T(1,128)}, s32[64,1,64]{2,1,0:T(1,128)S(1)}, u32[]{:S(2)}) copy-start(s32[64,1,64]{2,1,0:T(1,128)S(1)} %all-to-all-done.1) | copy-start | bytes 49156
  60.9 33.7 %copy-start.7 = (bf16[128,512]{1,0:T(8,128)(2,1)S(1)}, bf16[128,512]{1,0:T(8,128)(2,1)}, u32[]{:S(2)}) copy-start(bf16[128,512]{1,0:T(8,128)(2,1)} %copy-done.6) | copy-start | bytes 393220
  60.9 35.1 %all-to-all-start = ((bf16[64,16,512]{2,1,0:T(8,128)(2,1)}), bf16[64,16,512]{2,1,0:T(8,128)(2,1)S(1)}, u32[]{:S(2)}, u32[]{:S(2)}) async-start(bf16[64,16,512]{2,1,0:T(8,128)(2,1)} %get-tuple-element.9), calls=%async_computation | async-start | bytes 2097152 | tf_op jit(solution)/shard_map/all_to_all | solution.py:262
  68.6 60.7 %all-gather.4.cloned.1.call-start = ((), (), s32[]{:S(2)}) async-start(), calls=%async_computation.4 | async-start | bytes 1179648 | tf_op jit(solution)/shard_map/all_gather | solution.py:320
  68.6 25.9 %collective-permute-start = (bf16[128,512]{1,0:T(8,128)(2,1)S(1)}, bf16[128,512]{1,0:T(8,128)(2,1)S(1)}, u32[]{:S(2)}, u32[]{:S(2)}) collective-permute-start(bf16[128,512]{1,0:T(8,128)(2,1)S(1)} %get-tuple-element.10), channel_id=1, source_target_pairs={{0,8},{8,0},{16,24},{24,16},{32,40},{40,32},{48,56},{56,48},{64,72... | collective-permute-start | bytes 393224 | tf_op jit(solution)/shard_map/ppermute | solution.py:264
  96.0 0.8 copy-start.5
  119.9 5.3 %collective-permute-start.1 = (f32[256]{0:T(256)S(1)}, f32[256]{0:T(256)S(1)}, u32[]{:S(2)}, u32[]{:S(2)}) collective-permute-start(f32[256]{0:T(256)S(1)} %psum.7), channel_id=1, source_target_pairs={{0,8},{8,0},{16,24},{24,16},{32,40},{40,32},{48,56},{56,48},{64,72... | collective-permute-start | bytes 3080 | tf_op jit(solution)/shard_map/ppermute | solution.py:306
  125.3 8.2 %copy-start.12 = (f32[128]{0:T(128)}, f32[128]{0:T(128)S(1)}, u32[]{:S(2)}) copy-start(f32[128]{0:T(128)S(1)} %dynamic-slice_log_fusion) | copy-start | bytes 1540
  129.3 2.2 copy-start.9
  131.9 90.6 %copy-start.13 = (f32[128]{0:T(128)}, f32[128]{0:T(128)S(1)}, u32[]{:S(2)}) copy-start(f32[128]{0:T(128)S(1)} %log.13) | copy-start | bytes 1540
Sparse Core Ops, SparseCore 0:
  102.6 26.6 all-gather.3
where the time goes:
time: 241 us; the launch traced here: 240 us
  blocking collectives  119 us (49%)
  waiting for transfers between devices  31.2 us (13%)
  starting transfers between devices  28.2 us (12%)
  local copies, waits for them, and re-layouts  18.5 us (8%)
  Pallas kernels  16.3 us (7%)
  between operations  16.2 us (7%)
  other arithmetic  11.3 us (5%)
    all_to_all x1, blocking collectives, local(): lax.all_to_all(panels.reshape(512, 8, 256), ('state', 'seq'), split_axis=...  64.8 us
    all_to_all x1, blocking collectives, local(): lax.all_to_all(jnp.concatenate([log_emit, norms], axis=3).reshape(states,...  24.1 us
    ppermute x1, waiting for transfers between devices, local(): out_other = lax.ppermute(out_kept, 'state', swap)  20.6 us
    psum x1, blocking collectives, local(): z_half = lax.psum(z_part[0], 'seq')  15.1 us
    all_gather x1, blocking collectives, local(): group = lax.all_gather(request, 'seq', axis=0, tiled=False)  14.5 us
    all_to_all x1, starting transfers between devices, local(): lax.all_to_all(jnp.repeat(by_pair, 2, axis=0), 'state', split_axis=0, con...  13.6 us
    pallas_call x1, Pallas kernels, chain(): pl.pallas_call(chain_kernel, out_shape=jax.ShapeDtypeStruct((8, LANES), f...  8.76 us
    all_to_all x1, starting transfers between devices, local(): lax.all_to_all(msg, 'state', split_axis=0, concat_axis=0, tiled=True)  7.65 us
  transfers between devices with their start and end apart: 5, of which 5 were waited for; matrix products, arithmetic and copies ran while one was open for 3% of the time, Pallas kernels for 1%

commit v1 on v0

v1 whole, which is shorter than its diff:
```python
import jax
import jax.numpy as jnp
from jax import lax
from jax.experimental import pallas as pl
from jax.experimental.pallas import tpu as pltpu
from jax.sharding import PartitionSpec as P

BS = 256
PART = 32
KW = 64
LANES = 128
RANKS = 3
SHARDS = 64
ROWS = 24
XROWS = 208
f32 = jnp.float32
bf16 = jnp.bfloat16
i32 = jnp.int32


def iota(shape, axis):
    return lax.broadcasted_iota(i32, shape, axis)


def one_hot(mask):
    return jnp.where(mask, 1.0, 0.0).astype(bf16)


def ints(mask, value):
    return jnp.where(mask, value, 0)


def prep_kernel(
    parts_ref, token_ref, tokens_ref, cluster_ref, table_ref, emit_ref, out_ref, in_ref, word_ref,
    msg_ref, mat_ref, slot_ref, in_kept, slot_of, near, wide, counts_of,
):
    me = lax.axis_index("state")
    share = lax.axis_index("seq")
    sub = iota((LANES, LANES), 0)
    lane = iota((LANES, LANES), 1)
    eye = sub == lane

    def column(row):
        return jnp.sum(ints(eye, row), axis=1, keepdims=True)

    def line(col):
        return jnp.sum(ints(eye, col), axis=0, keepdims=True)

    for blk in range(2):
        for part in range(2):
            start = blk * BS + parts_ref[me * 2 + blk, part] * PART
            src = pl.ds(pl.multiple_of(start, PART), PART)
            at = (blk * 2 + part) * PART
            mat_ref[at : at + PART, :] = out_ref[src, :]
            mat_ref[2 * KW + at : 2 * KW + at + PART, :] = emit_ref[src, :]
            in_kept[at : at + PART, :] = in_ref[src, :]
    row = iota((16, LANES), 0)
    want = (row >> 3) * KW + (row & 3) * 16 + share * 2 + ((row >> 2) & 1)
    targets = jnp.dot(
        one_hot(iota((16, LANES), 1) == want), in_kept[...], preferred_element_type=f32
    ).astype(bf16)

    sums = jnp.concatenate([one_hot(sub < lane), jnp.ones((LANES, LANES), bf16)], axis=1)
    block_row = table_ref[...]
    block_col = column(block_row)
    block_col_f = block_col.astype(f32)
    carry = jnp.zeros((LANES, LANES), f32)
    chunks = 2048 // LANES
    own = pl.multiple_of(me * chunks, chunks)
    own_rows = cluster_ref[pl.ds(own, chunks), :]
    for c in range(chunks):
        hit = sub == own_rows[c : c + 1, :]
        found = jnp.dot(one_hot(hit), sums, preferred_element_type=f32)
        before = found[:, :LANES] + carry
        carry = carry + found[:, LANES:]
        rank = jnp.sum(jnp.where(hit, before, 0.0), axis=0, keepdims=True).astype(i32)
        block = jnp.sum(jnp.where(hit, block_col_f, 0.0), axis=0, keepdims=True).astype(i32)
        x = rank - RANKS * share
        slot = (block >> 1) * 8 + x * 2 + (block & 1)
        slot_of[c : c + 1, :] = jnp.where((x >= 0) & (x < RANKS), slot, -1)
    counts_of[...] = carry

    length = token_ref.shape[1]

    def pull(i, _):
        for u in range(8):
            t = i * 8 + u
            near[pl.ds(t, 1), :] = cluster_ref[pl.ds(token_ref[0, t] >> 7, 1), :]
        return 0

    lax.fori_loop(0, length // 8, pull, 0)
    token_col = column(tokens_ref[...])
    cluster_col = jnp.sum(ints(lane == (token_col & 127), near[...]), axis=1, keepdims=True)
    near[...] = jnp.broadcast_to(cluster_col, (LANES, LANES))
    place = iota((chunks, LANES), 0) * LANES + iota((chunks, LANES), 1)

    def tally(i, _):
        for u in range(8):
            t = i * 8 + u
            token = token_ref[0, t]
            shard_rows = cluster_ref[pl.ds(pl.multiple_of((token >> 11) * chunks, chunks), chunks), :]
            earlier = (shard_rows == near[pl.ds(t, 1), :]) & (place < (token & 2047))
            wide[pl.ds(t, 1), :] = jnp.sum(ints(earlier, 1), axis=0, keepdims=True)
        return 0

    lax.fori_loop(0, length // 8, tally, 0)
    rank_col = jnp.sum(wide[...], axis=1, keepdims=True)
    own_block_col = jnp.sum(ints(lane == cluster_col, block_row), axis=1, keepdims=True)
    own_block_row = line(own_block_col)
    same = own_block_col == own_block_row
    times_col = jnp.sum(ints(same & (lane < sub), 1), axis=1, keepdims=True)
    times_row = jnp.sum(ints(same & (sub < lane), 1), axis=0, keepdims=True)
    slot_ref[...] = (own_block_row >> 1) * 64 + (own_block_row & 1) * 2 + times_row
    following = jnp.sum(ints(lane == sub + 1, own_block_row), axis=1, keepdims=True)
    following = jnp.where(iota((LANES, 1), 0) == length - 1, LANES, following)
    slots_col = own_block_col * 2 + times_col
    asked = jnp.zeros((SHARDS, LANES), f32)
    slot_line = iota((LANES, 2 * LANES), 1)
    at_slot = slot_line == slots_col
    owner = (iota((SHARDS, 2 * LANES), 1) >> 2) == iota((SHARDS, 2 * LANES), 0)
    slot_sub = iota((2 * LANES, LANES), 0) & 3
    slot_lane = iota((2 * LANES, LANES), 1)
    for field, values in enumerate((following, token_col >> 11, rank_col)):
        value_row = jnp.sum(ints(at_slot, values), axis=0, keepdims=True)
        spread = jnp.where(owner, value_row.astype(f32), 0.0).astype(bf16)
        asked += jnp.dot(
            spread, one_hot(slot_lane == field * 4 + slot_sub), preferred_element_type=f32
        )
    count_lane = jnp.where(lane == 12 + (block_col & 1), counts_of[...], 0.0).astype(bf16)
    count_owner = one_hot((block_row >> 1) == iota((SHARDS, LANES), 0))
    asked += jnp.dot(count_owner, count_lane, preferred_element_type=f32)

    request_row = iota((8, LANES), 0) == 6
    for tile in range(4):
        rows = sub + tile * LANES
        chosen = jnp.concatenate(
            [one_hot(rows == slot_of[c : c + 1, :]) for c in range(chunks)], axis=1
        )
        words = jnp.dot(chosen, word_ref[...], preferred_element_type=f32)
        for d in range(16):
            to = tile * 16 + d
            mine = words[d * 8 : d * 8 + 8, :]
            head = jnp.where(request_row, asked[to : to + 1, :], mine[:, :LANES])
            msg_ref[to, 0:16, :] = targets
            msg_ref[to, 16:24, :] = jnp.concatenate([head, mine[:, LANES:]], axis=1).astype(bf16)


def prep(kept_parts, tokens, word_cluster, cluster_block, emit_states, trans_out, trans_in, word_emb):
    width = emit_states.shape[1]
    vmem = pl.BlockSpec(memory_space=pltpu.VMEM)
    smem = pl.BlockSpec(memory_space=pltpu.SMEM)
    return pl.pallas_call(
        prep_kernel,
        out_shape=(
            jax.ShapeDtypeStruct((SHARDS, ROWS, width), bf16),
            jax.ShapeDtypeStruct((4 * KW, width), bf16),
            jax.ShapeDtypeStruct((1, LANES), i32),
        ),
        in_specs=[smem, smem] + [vmem] * 7,
        out_specs=(vmem, vmem, vmem),
        scratch_shapes=[
            pltpu.VMEM((2 * KW, width), bf16),
            pltpu.VMEM((16, LANES), i32),
            pltpu.VMEM((LANES, LANES), i32),
            pltpu.VMEM((LANES, LANES), i32),
            pltpu.VMEM((LANES, LANES), f32),
        ],
        compiler_params=pltpu.CompilerParams(vmem_limit_bytes=40 * 1024 * 1024),
        name="prep",
    )(
        kept_parts, tokens, tokens, word_cluster.reshape(-1, LANES), cluster_block[None, :],
        emit_states, trans_out, trans_in, word_emb,
    )


def score_kernel(msg_ref, mat_ref, exps_ref, out_ref, words, raw):
    share = lax.axis_index("seq")
    total = jnp.zeros((1, LANES), f32)
    for tile in range(8):
        got = msg_ref[tile * 8 : tile * 8 + 8].reshape(8 * ROWS, msg_ref.shape[2])
        res = lax.dot_general(
            got, mat_ref[...], (((1,), (1,)), ((), ())), preferred_element_type=f32
        ).reshape(8, ROWS, 2 * LANES)
        exps = jnp.exp(res[:, :16, :LANES]).reshape(LANES, LANES)
        exps_ref[tile * LANES : (tile + 1) * LANES, :] = exps
        total = total + jnp.sum(exps, axis=0, keepdims=True)
        words[tile * 64 : (tile + 1) * 64, :] = res[:, 16:, LANES:].reshape(64, LANES)
        raw[tile * 64 : (tile + 1) * 64, :] = (
            msg_ref[tile * 8 : tile * 8 + 8, 16:24, :LANES].astype(f32).reshape(64, LANES)
        )
    asked = raw[pl.ds(6, SHARDS, stride=8), :]
    spread = one_hot(iota((LANES, LANES), 0) == 12 + (iota((LANES, LANES), 1) >> 6))
    counts = jnp.dot(asked.astype(bf16), spread, preferred_element_type=f32)
    low = iota((SHARDS, LANES), 1) < KW
    for x in range(RANKS):
        scores = jnp.where(
            low,
            words[pl.ds(2 * x, SHARDS, stride=8), :],
            words[pl.ds(2 * x + 1, SHARDS, stride=8), :],
        )
        valid = (RANKS * share + x).astype(f32) < counts
        out_ref[x * SHARDS : (x + 1) * SHARDS, :] = jnp.where(valid, scores, -1e30)
    lane16 = iota((8, LANES), 1) >> 4
    packed = jnp.zeros((8, LANES), f32)
    for m in range(8):
        some = raw[pl.ds(m * 8 + 6, 8, stride=64), :]
        some = pltpu.roll(some, m * 16, 1) if m else some
        packed = jnp.where(lane16 == m, some, packed)
    out_ref[192:200, :] = packed
    out_ref[200:208, :] = jnp.broadcast_to(total, (8, LANES))


def score(msg, mat):
    vmem = pl.BlockSpec(memory_space=pltpu.VMEM)
    return pl.pallas_call(
        score_kernel,
        out_shape=(
            jax.ShapeDtypeStruct((1024, LANES), f32),
            jax.ShapeDtypeStruct((XROWS, LANES), f32),
        ),
        in_specs=[vmem] * 2,
        out_specs=(vmem, vmem),
        scratch_shapes=[pltpu.VMEM((512, LANES), f32), pltpu.VMEM((512, LANES), f32)],
        compiler_params=pltpu.CompilerParams(vmem_limit_bytes=40 * 1024 * 1024),
        name="score",
    )(msg, mat)


def pick_kernel(exps_ref, all_ref, panel_ref, trans_ref, emit_ref, table, emits):
    share = lax.axis_index("seq")
    total = jnp.zeros((1, LANES), f32)
    heap = jnp.zeros((SHARDS, LANES), f32)
    for g in range(8):
        total = total + all_ref[g, 200:201, :]
        for x in range(RANKS):
            heap = heap + jnp.exp(all_ref[g, x * SHARDS : (x + 1) * SHARDS, :])
    trans_ref[...] = jnp.broadcast_to(jnp.log(total), (8, LANES))
    emit_norm = jnp.log(jnp.sum(heap, axis=0, keepdims=True))
    emit_ref[...] = jnp.broadcast_to(emit_norm, (8, LANES))
    for g in range(8):
        rows = slice(g * 192, (g + 1) * 192)
        emits[rows, :] = jnp.exp(all_ref[g, 0:192, :] - emit_norm).astype(bf16)
    low = iota((LANES, LANES), 1) < KW
    for half in range(2):
        cols = [exps_ref[pl.ds(half * 4 + j, LANES, stride=8), :] / total for j in range(4)]
        for pair in range(2):
            first, second = cols[2 * pair], cols[2 * pair + 1]
            lanes = slice(pair * LANES, (pair + 1) * LANES)
            at = 2 * half * LANES
            table[at : at + LANES, lanes] = jnp.where(
                low, first, pltpu.roll(second, KW, 1)
            ).astype(bf16)
            table[at + LANES : at + 2 * LANES, lanes] = jnp.where(
                low, pltpu.roll(first, KW, 1), second
            ).astype(bf16)
    row8, lane8 = iota((512, LANES), 0), iota((512, LANES), 1)
    row4, lane4 = iota((256, LANES), 0), iota((256, LANES), 1)
    from8 = one_hot(((iota((512, 8), 0) >> 3) & 7) == iota((512, 8), 1))
    from4 = one_hot(((iota((256, 8), 0) >> 2) & 7) == iota((256, 8), 1))
    next_at = lane8 == (row8 >> 6) * 16 + (row8 & 3)
    key_at = ((lane4 >> 4) == (row4 >> 5)) & ((lane4 & 3) == (row4 & 3))
    key_at = key_at & ((lane4 & 15) >= 4) & ((lane4 & 15) < 12)
    ones = jnp.ones((LANES, LANES), bf16)
    weights = jnp.where((iota((LANES, LANES), 0) & 15) >= 8, 64.0, 1.0).astype(bf16)
    code = (row8 & 7) >> 1
    lane_f = lane8.astype(f32)
    key_lane = lane4.astype(f32)
    wide = iota((512, 2 * LANES), 1)
    half_of = (iota((512, 2 * LANES), 0) >> 2) & 1
    diagonal = (wide & (KW - 1)) == (wide >> 6) * 16 + share * 2 + half_of
    keep = (lane4 < KW) == ((row4 & 2) == 0)
    upper = (iota((32, 8, LANES), 1)) < 4

    def step(tile, _):
        asked = jnp.concatenate(
            [all_ref[g, pl.ds(192 + tile, 1), :] for g in range(8)], axis=0
        ).astype(bf16)
        spread = jnp.dot(from8, asked, preferred_element_type=f32)
        wanted = jnp.dot(
            jnp.where(next_at, spread, 0.0).astype(bf16), ones, preferred_element_type=f32
        )
        hit = wanted == lane_f
        chosen = jnp.concatenate([one_hot(hit & (code == b)) for b in range(4)], axis=1)
        panels = jnp.dot(chosen, table[...], preferred_element_type=f32)
        last = wanted == float(LANES)
        last = jnp.concatenate([last, last], axis=1)
        panels = jnp.where(last & diagonal, 1.0, panels)
        spread = jnp.dot(from4, asked, preferred_element_type=f32)
        keys = jnp.dot(
            jnp.where(key_at, spread, 0.0).astype(bf16), weights, preferred_element_type=f32
        )
        chosen = jnp.concatenate(
            [one_hot(keys == key_lane + float(n * LANES)) for n in range(12)], axis=1
        )
        got = jnp.dot(chosen, emits[...], preferred_element_type=f32)
        got = jnp.where(keep, got, pltpu.roll(got, KW, 1)).reshape(32, 8, LANES)
        other = pltpu.roll(got, 4, 1)
        even = jnp.where(upper, got, other)
        odd = jnp.where(upper, other, got)
        both = jnp.stack([even, odd], axis=1).reshape(512, LANES)
        panels = panels * jnp.concatenate([both, both], axis=1)
        panel_ref[pl.ds(pl.multiple_of(tile * 512, 512), 512), :] = panels.astype(bf16)
        return 0

    lax.fori_loop(0, 8, step, 0)


def pick(exps, everything):
    vmem = pl.BlockSpec(memory_space=pltpu.VMEM)
    return pl.pallas_call(
        pick_kernel,
        out_shape=(
            jax.ShapeDtypeStruct((4096, 2 * LANES), bf16),
            jax.ShapeDtypeStruct((8, LANES), f32),
            jax.ShapeDtypeStruct((8, LANES), f32),
        ),
        in_specs=[vmem] * 2,
        out_specs=(vmem, vmem, vmem),
        scratch_shapes=[pltpu.VMEM((512, 2 * LANES), bf16), pltpu.VMEM((1536, LANES), bf16)],
        compiler_params=pltpu.CompilerParams(vmem_limit_bytes=40 * 1024 * 1024),
        name="pick",
    )(exps, everything)


def chain_kernel(slot_ref, panel_ref, out_ref, ya, yb, ping, pong, logs):
    length = slot_ref.shape[1]

    def widen(i, _):
        rows = pl.ds(pl.multiple_of(i * 256, 256), 256)
        got = panel_ref[rows, :].astype(f32)
        ya[rows, :] = got[:, :LANES]
        yb[rows, :] = got[:, LANES:]
        return 0

    lax.fori_loop(0, panel_ref.shape[0] // 256, widen, 0)
    low = iota((KW, LANES), 1) < KW
    logs[...] = jnp.ones_like(logs)

    def scaled(value, at):
        top = jnp.max(jnp.max(value, axis=0, keepdims=True), axis=1, keepdims=True)
        logs[pl.ds(at, 1), :] = jnp.broadcast_to(top, (1, LANES))
        return (value * (1.0 / top)).astype(bf16)

    def build(i, _):
        for u in range(8):
            t = i * 8 + u
            rows = pl.ds(slot_ref[0, t], 16, stride=4)
            a, b = ya[rows, :], yb[rows, :]
            move = jnp.concatenate([a, pltpu.roll(a, KW, 1), b, pltpu.roll(b, KW, 1)], axis=0)
            ping[t] = scaled(jnp.where(low, move, 0.0), t)
        return 0

    lax.fori_loop(0, length // 8, build, 0)
    src, dst, count, base = ping, pong, length // 2, length
    while count >= 1:
        unroll = min(count, 8)

        def level(i, _, src=src, dst=dst, unroll=unroll, base=base):
            for u in range(unroll):
                n = i * unroll + u
                prod = jnp.dot(src[2 * n + 1][:, :KW], src[2 * n], preferred_element_type=f32)
                dst[n] = scaled(prod, base + n)
            return 0

        lax.fori_loop(0, count // unroll, level, 0)
        src, dst, count, base = dst, src, count // 2, base + count
    final = jnp.sum(jnp.sum(src[0].astype(f32), axis=0, keepdims=True), axis=1, keepdims=True)
    scale = jnp.sum(jnp.log(logs[...]), axis=0, keepdims=True)
    total = jnp.log(final) + scale - jnp.log(jnp.full((1, LANES), 8192.0, f32))
    out_ref[...] = jnp.broadcast_to(total / length, (8, LANES))


def chain(slots, panels):
    length = slots.shape[1]
    vmem = pl.BlockSpec(memory_space=pltpu.VMEM)
    return pl.pallas_call(
        chain_kernel,
        out_shape=jax.ShapeDtypeStruct((8, LANES), f32),
        in_specs=[pl.BlockSpec(memory_space=pltpu.SMEM), vmem],
        out_specs=vmem,
        scratch_shapes=[
            pltpu.VMEM((4096, LANES), f32),
            pltpu.VMEM((4096, LANES), f32),
            pltpu.VMEM((length, KW, LANES), bf16),
            pltpu.VMEM((length // 2, KW, LANES), bf16),
            pltpu.VMEM((2 * length, LANES), f32),
        ],
        compiler_params=pltpu.CompilerParams(vmem_limit_bytes=40 * 1024 * 1024),
        name="chain",
    )(slots, panels)


def local(
    emit_states, trans_out, trans_in, word_emb, word_cluster, cluster_block, kept_parts, tokens
):
    msg, mat, slots = prep(
        kept_parts, tokens, word_cluster, cluster_block, emit_states, trans_out, trans_in, word_emb
    )
    arrived = lax.all_to_all(msg, "state", split_axis=0, concat_axis=0, tiled=True)
    exps, mine = score(arrived, mat)
    everything = lax.all_gather(mine, "seq", axis=0, tiled=False)
    panels, trans_norm, emit_norm = pick(exps, everything)
    got = lax.all_to_all(
        panels.reshape(512, 8, 2 * LANES),
        ("state", "seq"),
        split_axis=0,
        concat_axis=0,
        tiled=True,
    ).reshape(4096, 2 * LANES)
    token_loglik = chain(slots, got)
    return (token_loglik[0, :1], trans_norm[0], emit_norm[0])


def solution(mesh):
    placed = (
        P("state", None),
        P("state", None),
        P("state", None),
        P("state", None),
        P(),
        P(),
        P(),
        P(("state", "seq"), None),
    )
    return jax.shard_map(
        local,
        mesh=mesh,
        in_specs=placed,
        out_specs=(P(("state", "seq")), P("state"), P("state")),
        check_vma=False,
    )
```

time: 241 us -> 173 us (0.72)
  blocking collectives: 119 us -> 72.9 us
  waiting for transfers between devices: 31.2 us -> 53.5 us
  starting transfers between devices: 28.2 us -> 11.2 us
  between operations: 16.2 us -> 0.68 us
  other arithmetic: 11.3 us -> 0 us
  local copies, waits for them, and re-layouts: 18.5 us -> 10.2 us
  Pallas kernels: 16.3 us -> 23.6 us
    all_to_all x2 -> x1, waiting for transfers between devices: 6.01 us -> 53.5 us  [local(): lax.all_to_all(panels.reshape(512, 8, 2 * LANES), ('state', 'seq'), split...]
    all_to_all x2 -> x1, blocking collectives: 89 us -> 55.9 us  [local(): lax.all_to_all(msg, 'state', split_axis=0, concat_axis=0, tiled=True)]
    ppermute x2 -> x0, waiting for transfers between devices: 21.2 us -> none  [the longest x1 20.6 us: local(): out_other = lax.ppermute(out_kept, 'state', swap)]
    psum x1 -> x0, blocking collectives: 15.1 us -> none  [local(): z_half = lax.psum(z_part[0], 'seq')]
    all_to_all x2 -> x1, starting transfers between devices: 21.3 us -> 11.2 us  [local(): lax.all_to_all(panels.reshape(512, 8, 2 * LANES), ('state', 'seq'), split...]
    gather x4 -> x0, local copies, waits for them, and re-layouts: 7.89 us -> none  [the longest x1 3.57 us: local(): shard_rows = jnp.take(all_clusters, shard, axis=0)]
    pallas_call x2 -> x3, Pallas kernels: 7.56 us -> 14.8 us  [the longest x1 9.2 us: pick(): pl.pallas_call(pick_kernel, out_shape=(jax.ShapeDtypeStruct((4096, 2 * LA...]
    ppermute x2 -> x0, starting transfers between devices: 6.88 us -> none  [the longest x1 3.96 us: local(): z_all = z_half + lax.ppermute(z_half, 'state', swap)]
  transfers between devices with their start and end apart: 5 -> 1, of which waited for: 5 -> 1; matrix products, arithmetic and copies ran while one was open for 3% -> 0% of each run, Pallas kernels for 1% -> 0%
where the time goes in v1:
time: 173 us; the launch traced here: 172 us
  blocking collectives  72.9 us (42%)
  waiting for transfers between devices  53.5 us (31%)
  Pallas kernels  23.6 us (14%)
  starting transfers between devices  11.2 us (6%)
  local copies, waits for them, and re-layouts  10.2 us (6%)
    all_to_all x1, blocking collectives, local(): lax.all_to_all(msg, 'state', split_axis=0, concat_axis=0, tiled=True)  55.9 us
    all_to_all x1, waiting for transfers between devices, local(): lax.all_to_all(panels.reshape(512, 8, 2 * LANES), ('state', 'seq'), split...  53.5 us
    all_gather x1, blocking collectives, local(): everything = lax.all_gather(mine, 'seq', axis=0, tiled=False)  17 us
    all_to_all x1, starting transfers between devices, local(): lax.all_to_all(panels.reshape(512, 8, 2 * LANES), ('state', 'seq'), split...  11.2 us
    pallas_call x1, Pallas kernels, pick(): pl.pallas_call(pick_kernel, out_shape=(jax.ShapeDtypeStruct((4096, 2 * LA...  9.2 us
    unnamed x17, local copies, waits for them, and re-layouts  9.16 us
    pallas_call x1, Pallas kernels, chain(): pl.pallas_call(chain_kernel, out_shape=jax.ShapeDtypeStruct((8, LANES), f...  8.84 us
    pallas_call x1, Pallas kernels, prep(): pl.pallas_call(prep_kernel, out_shape=(jax.ShapeDtypeStruct((SHARDS, ROWS...  4.73 us
  transfers between devices with their start and end apart: 1, of which 1 were waited for; matrix products, arithmetic and copies ran while one was open for 0% of the time, Pallas kernels for 0%

profile of v1, /device:TPU:1, one launch (start us, length us, event | category | flops | bytes accessed | tf_op | source)
XLA Modules:
  0.0 172.1 jit_solution(2037751864012945581)
XLA Ops:
  0.6 0.8 copy.11.parts_ref
  1.4 0.0 copy-start
  1.4 1.6 copy-done
  3.0 0.0 copy-start.2
  3.0 1.0 copy-done.2
  4.0 0.0 copy-start.3
  4.1 1.0 copy-done.3
  5.1 0.0 copy-start.4
  5.1 1.0 copy-done.4
  6.1 0.0 copy-start.5
  6.1 1.0 copy-done.5
  7.2 0.0 copy-start.6
  7.2 0.7 copy-done.6
  7.8 0.0 copy-start.7
  7.8 0.7 copy-done.7
  8.5 4.7 %prep.1 = (bf16[64,24,512]{2,1,0:T(8,128)(2,1)S(1)}, bf16[256,512]{1,0:T(8,128)(2,1)S(1)}, s32[1,128]{1,0:T(1,128)S(1)}) custom-call(s32[128,2]{1,0:T(8,128)S(1)} %copy.11.parts_ref, s32[1,128]{1,0:T(1,128)S(1)} %copy-done.6, s32[1,128]{1,0:T(1,128)S(1)} %copy-done.6, s32[1024,128]{1,0:T(8,128)S(1)} %bitcast.13, s32[1,128]{1,0:T(1,128)S(1)} %bitcast.14, ...), custom_call_target="tpu_custom_call" | custom-call | tf_op jit(solution)/shard_map/prep/pallas_call | solution.py:152
  13.2 55.9 %all_to_all.10.msg_ref = bf16[64,24,512]{2,1,0:T(8,128)(2,1)S(1)} all-to-all(bf16[64,24,512]{2,1,0:T(8,128)(2,1)S(1)} %get-tuple-element.12), channel_id=1, replica_groups=mesh['state'=64,'seq'=8] {'state'}, dimensions={0} | all-to-all | bytes 3145728 | tf_op jit(solution)/shard_map/all_to_all | solution.py:399
  69.1 0.9 score.1
  70.0 17.0 %all-gather = f32[1664,128]{1,0:T(8,128)S(1)} all-gather(f32[208,128]{1,0:T(8,128)S(1)} %get-tuple-element.15), channel_id=2, replica_groups=mesh['state'=64,'seq'=8] {'seq'}, dimensions={0}, use_global_device_ids=true | all-gather | bytes 958464 | tf_op jit(solution)/shard_map/all_gather | solution.py:401
  87.0 9.2 %pick.1 = (bf16[4096,256]{1,0:T(8,128)(2,1)S(1)}, f32[8,128]{1,0:T(8,128)S(1)}, f32[8,128]{1,0:T(8,128)S(1)}) custom-call(f32[1024,128]{1,0:T(8,128)S(1)} %get-tuple-element.14.exps_ref, f32[8,208,128]{2,1,0:T(8,128)S(1)} %bitcast.11), custom_call_target="tpu_custom_call" | custom-call | tf_op jit(solution)/shard_map/pick/pallas_call | solution.py:310
  96.2 0.0 copy-start.1
  96.2 1.3 copy-done.1
  97.6 11.2 %all-to-all-start.1 = ((bf16[512,8,256]{2,1,0:T(8,128)(2,1)}), bf16[512,8,256]{2,1,0:T(8,128)(2,1)S(1)}, u32[]{:S(2)}, u32[]{:S(2)}) async-start(bf16[512,8,256]{2,1,0:T(8,128)(2,1)} %bitcast.12), calls=%async_computation.1 | async-start | bytes 4194304 | tf_op jit(solution)/shard_map/all_to_all | solution.py:403
  108.8 0.5 slice_bitcast_fusion
  109.3 53.5 %all-to-all-done.1 = bf16[512,8,256]{2,1,0:T(8,128)(2,1)S(1)} async-done(((bf16[512,8,256]{2,1,0:T(8,128)(2,1)}), bf16[512,8,256]{2,1,0:T(8,128)(2,1)S(1)}, u32[]{:S(2)}, u32[]{:S(2)}) %all-to-all-start.1) | async-done | bytes 2097184 | tf_op jit(solution)/shard_map/all_to_all | solution.py:403
  162.8 8.8 %chain.1 = f32[8,128]{1,0:T(8,128)S(1)} custom-call(s32[1,128]{1,0:T(1,128)S(1)} %get-tuple-element.11.slot_ref, bf16[4096,256]{1,0:T(8,128)(2,1)S(1)} %bitcast.10), custom_call_target="tpu_custom_call" | custom-call | tf_op jit(solution)/shard_map/chain/pallas_call | solution.py:376
  171.6 0.5 slice.9
Async XLA Ops:
  1.4 1.6 copy-start
  3.0 1.0 copy-start.2
  4.0 1.0 copy-start.3
  5.1 1.0 copy-start.4
  6.1 1.0 copy-start.5
  7.2 0.7 copy-start.6
  7.8 0.7 copy-start.7
  96.2 1.3 copy-start.1
  97.6 65.2 %all-to-all-start.1 = ((bf16[512,8,256]{2,1,0:T(8,128)(2,1)}), bf16[512,8,256]{2,1,0:T(8,128)(2,1)S(1)}, u32[]{:S(2)}, u32[]{:S(2)}) async-start(bf16[512,8,256]{2,1,0:T(8,128)(2,1)} %bitcast.12), calls=%async_computation.1 | async-start | bytes 4194304 | tf_op jit(solution)/shard_map/all_to_all | solution.py:403

commit v2 on v1

--- a/solution.py
+++ b/solution.py
@@ -31,11 +31,34 @@
 
 
 def prep_kernel(
-    parts_ref, token_ref, tokens_ref, cluster_ref, table_ref, emit_ref, out_ref, in_ref, word_ref,
-    msg_ref, mat_ref, slot_ref, in_kept, slot_of, near, wide, counts_of,
+    parts_ref, token_ref, tokens_hbm, cluster_hbm, table_hbm, emit_hbm, out_hbm, in_hbm, word_hbm,
+    msg_ref, mat_ref, slot_ref,
+    in_kept, slot_of, near, wide, counts_of, tokens_ref, cluster_ref, table_ref, word_ref, chosen, sems,
 ):
     me = lax.axis_index("state")
     share = lax.axis_index("seq")
+    head = []
+    for n, (src, dst) in enumerate(
+        ((cluster_hbm, cluster_ref), (table_hbm, table_ref), (tokens_hbm, tokens_ref))
+    ):
+        head.append(pltpu.make_async_copy(src, dst, sems.at[n]))
+        head[-1].start()
+    word_copy = pltpu.make_async_copy(word_hbm, word_ref, sems.at[3])
+    word_copy.start()
+    kept = []
+    for blk in range(2):
+        for part in range(2):
+            start = blk * BS + parts_ref[part, me * 2 + blk] * PART
+            src = pl.ds(pl.multiple_of(start, PART), PART)
+            at = (blk * 2 + part) * PART
+            for which, (hbm, ref, to) in enumerate(
+                ((in_hbm, in_kept, at), (out_hbm, mat_ref, at), (emit_hbm, mat_ref, 2 * KW + at))
+            ):
+                sem = sems.at[4 + (blk * 2 + part) * 3 + which]
+                kept.append(pltpu.make_async_copy(hbm.at[src, :], ref.at[pl.ds(to, PART), :], sem))
+                kept[-1].start()
+    for copy in head:
+        copy.wait()
     sub = iota((LANES, LANES), 0)
     lane = iota((LANES, LANES), 1)
     eye = sub == lane
@@ -45,20 +68,6 @@
 
     def line(col):
         return jnp.sum(ints(eye, col), axis=0, keepdims=True)
-
-    for blk in range(2):
-        for part in range(2):
-            start = blk * BS + parts_ref[me * 2 + blk, part] * PART
-            src = pl.ds(pl.multiple_of(start, PART), PART)
-            at = (blk * 2 + part) * PART
-            mat_ref[at : at + PART, :] = out_ref[src, :]
-            mat_ref[2 * KW + at : 2 * KW + at + PART, :] = emit_ref[src, :]
-            in_kept[at : at + PART, :] = in_ref[src, :]
-    row = iota((16, LANES), 0)
-    want = (row >> 3) * KW + (row & 3) * 16 + share * 2 + ((row >> 2) & 1)
-    targets = jnp.dot(
-        one_hot(iota((16, LANES), 1) == want), in_kept[...], preferred_element_type=f32
-    ).astype(bf16)
 
     sums = jnp.concatenate([one_hot(sub < lane), jnp.ones((LANES, LANES), bf16)], axis=1)
     block_row = table_ref[...]
@@ -130,25 +139,34 @@
     count_owner = one_hot((block_row >> 1) == iota((SHARDS, LANES), 0))
     asked += jnp.dot(count_owner, count_lane, preferred_element_type=f32)
 
+    for copy in kept:
+        copy.wait()
+    row = iota((16, LANES), 0)
+    want = (row >> 3) * KW + (row & 3) * 16 + share * 2 + ((row >> 2) & 1)
+    targets = jnp.dot(
+        one_hot(iota((16, LANES), 1) == want), in_kept[...], preferred_element_type=f32
+    ).astype(bf16)
+    for to in range(SHARDS):
+        msg_ref[to, 0:16, :] = targets
+    for tile in range(4):
+        for c in range(chunks):
+            chosen[tile * LANES : (tile + 1) * LANES, c * LANES : (c + 1) * LANES] = one_hot(
+                sub + tile * LANES == slot_of[c : c + 1, :]
+            )
+    word_copy.wait()
     request_row = iota((8, LANES), 0) == 6
-    for tile in range(4):
-        rows = sub + tile * LANES
-        chosen = jnp.concatenate(
-            [one_hot(rows == slot_of[c : c + 1, :]) for c in range(chunks)], axis=1
-        )
-        words = jnp.dot(chosen, word_ref[...], preferred_element_type=f32)
-        for d in range(16):
-            to = tile * 16 + d
-            mine = words[d * 8 : d * 8 + 8, :]
-            head = jnp.where(request_row, asked[to : to + 1, :], mine[:, :LANES])
-            msg_ref[to, 0:16, :] = targets
-            msg_ref[to, 16:24, :] = jnp.concatenate([head, mine[:, LANES:]], axis=1).astype(bf16)
+    words = jnp.dot(chosen[...], word_ref[...], preferred_element_type=f32)
+    for to in range(SHARDS):
+        mine = words[to * 8 : to * 8 + 8, :]
+        first = jnp.where(request_row, asked[to : to + 1, :], mine[:, :LANES])
+        msg_ref[to, 16:24, :] = jnp.concatenate([first, mine[:, LANES:]], axis=1).astype(bf16)
 
 
 def prep(kept_parts, tokens, word_cluster, cluster_block, emit_states, trans_out, trans_in, word_emb):
     width = emit_states.shape[1]
     vmem = pl.BlockSpec(memory_space=pltpu.VMEM)
     smem = pl.BlockSpec(memory_space=pltpu.SMEM)
+    clusters = word_cluster.reshape(-1, LANES)
     return pl.pallas_call(
         prep_kernel,
         out_shape=(
@@ -156,7 +174,7 @@
             jax.ShapeDtypeStruct((4 * KW, width), bf16),
             jax.ShapeDtypeStruct((1, LANES), i32),
         ),
-        in_specs=[smem, smem] + [vmem] * 7,
+        in_specs=[smem, smem] + [pl.BlockSpec(memory_space=pltpu.HBM)] * 7,
         out_specs=(vmem, vmem, vmem),
         scratch_shapes=[
             pltpu.VMEM((2 * KW, width), bf16),
@@ -164,11 +182,17 @@
             pltpu.VMEM((LANES, LANES), i32),
             pltpu.VMEM((LANES, LANES), i32),
             pltpu.VMEM((LANES, LANES), f32),
+            pltpu.VMEM((1, LANES), i32),
+            pltpu.VMEM(clusters.shape, i32),
+            pltpu.VMEM((1, LANES), i32),
+            pltpu.VMEM(word_emb.shape, bf16),
+            pltpu.VMEM((8 * SHARDS, word_emb.shape[0]), bf16),
+            pltpu.SemaphoreType.DMA((16,)),
         ],
-        compiler_params=pltpu.CompilerParams(vmem_limit_bytes=40 * 1024 * 1024),
+        compiler_params=pltpu.CompilerParams(vmem_limit_bytes=60 * 1024 * 1024),
         name="prep",
     )(
-        kept_parts, tokens, tokens, word_cluster.reshape(-1, LANES), cluster_block[None, :],
+        kept_parts.T, tokens, tokens, clusters, cluster_block[None, :],
         emit_states, trans_out, trans_in, word_emb,
     )
 
@@ -226,33 +250,41 @@
     )(msg, mat)
 
 
-def pick_kernel(exps_ref, all_ref, panel_ref, trans_ref, emit_ref, table, emits):
+def pick_kernel(
+    exps_ref, all_ref, panel_ref, trans_ref, emit_ref, table, emits, next_rows, word_rows
+):
     share = lax.axis_index("seq")
-    total = jnp.zeros((1, LANES), f32)
-    heap = jnp.zeros((SHARDS, LANES), f32)
-    for g in range(8):
-        total = total + all_ref[g, 200:201, :]
-        for x in range(RANKS):
-            heap = heap + jnp.exp(all_ref[g, x * SHARDS : (x + 1) * SHARDS, :])
-    trans_ref[...] = jnp.broadcast_to(jnp.log(total), (8, LANES))
-    emit_norm = jnp.log(jnp.sum(heap, axis=0, keepdims=True))
-    emit_ref[...] = jnp.broadcast_to(emit_norm, (8, LANES))
-    for g in range(8):
-        rows = slice(g * 192, (g + 1) * 192)
-        emits[rows, :] = jnp.exp(all_ref[g, 0:192, :] - emit_norm).astype(bf16)
-    low = iota((LANES, LANES), 1) < KW
-    for half in range(2):
-        cols = [exps_ref[pl.ds(half * 4 + j, LANES, stride=8), :] / total for j in range(4)]
-        for pair in range(2):
-            first, second = cols[2 * pair], cols[2 * pair + 1]
-            lanes = slice(pair * LANES, (pair + 1) * LANES)
-            at = 2 * half * LANES
-            table[at : at + LANES, lanes] = jnp.where(
-                low, first, pltpu.roll(second, KW, 1)
-            ).astype(bf16)
-            table[at + LANES : at + 2 * LANES, lanes] = jnp.where(
-                low, pltpu.roll(first, KW, 1), second
-            ).astype(bf16)
+    step = pl.program_id(0)
+
+    @pl.when(step == 0)
+    def _():
+        total = jnp.zeros((1, LANES), f32)
+        heap = jnp.zeros((SHARDS, LANES), f32)
+        for g in range(8):
+            total = total + all_ref[g, 200:201, :]
+            for x in range(RANKS):
+                heap = heap + jnp.exp(all_ref[g, x * SHARDS : (x + 1) * SHARDS, :])
+        trans_ref[...] = jnp.broadcast_to(jnp.log(total), (8, LANES))
+        emit_norm = jnp.log(jnp.sum(heap, axis=0, keepdims=True))
+        emit_ref[...] = jnp.broadcast_to(emit_norm, (8, LANES))
+        for g in range(8):
+            rows = slice((g & 3) * 192, (g & 3) * 192 + 192)
+            lanes = slice((g >> 2) * LANES, (g >> 2) * LANES + LANES)
+            emits[rows, lanes] = jnp.exp(all_ref[g, 0:192, :] - emit_norm).astype(bf16)
+        low = iota((LANES, LANES), 1) < KW
+        for half in range(2):
+            cols = [exps_ref[pl.ds(half * 4 + j, LANES, stride=8), :] / total for j in range(4)]
+            for pair in range(2):
+                first, second = cols[2 * pair], cols[2 * pair + 1]
+                lanes = slice(pair * LANES, (pair + 1) * LANES)
+                at = 2 * half * LANES
+                table[at : at + LANES, lanes] = jnp.where(
+                    low, first, pltpu.roll(second, KW, 1)
+                ).astype(bf16)
+                table[at + LANES : at + 2 * LANES, lanes] = jnp.where(
+                    low, pltpu.roll(first, KW, 1), second
+                ).astype(bf16)
+
     row8, lane8 = iota((512, LANES), 0), iota((512, LANES), 1)
     row4, lane4 = iota((256, LANES), 0), iota((256, LANES), 1)
     from8 = one_hot(((iota((512, 8), 0) >> 3) & 7) == iota((512, 8), 1))
@@ -265,64 +297,77 @@
     code = (row8 & 7) >> 1
     lane_f = lane8.astype(f32)
     key_lane = lane4.astype(f32)
+    wanted, late = [], []
+    for part in range(2):
+        asked = jnp.concatenate(
+            [all_ref[g, pl.ds(192 + step * 2 + part, 1), :] for g in range(8)], axis=0
+        ).astype(bf16)
+        spread = jnp.dot(from8, asked, preferred_element_type=f32)
+        block = jnp.dot(
+            jnp.where(next_at, spread, 0.0).astype(bf16), ones, preferred_element_type=f32
+        )
+        hit = block == lane_f
+        for b in range(4):
+            next_rows[part * 512 : part * 512 + 512, b * LANES : (b + 1) * LANES] = one_hot(
+                hit & (code == b)
+            )
+        wanted.append(block == float(LANES))
+        spread = jnp.dot(from4, asked, preferred_element_type=f32)
+        keys = jnp.dot(
+            jnp.where(key_at, spread, 0.0).astype(bf16), weights, preferred_element_type=f32
+        )
+        late.append(keys >= 768.0)
+        keys = jnp.where(late[-1], keys - 768.0, keys)
+        for n in range(6):
+            word_rows[part * 256 : part * 256 + 256, n * LANES : (n + 1) * LANES] = one_hot(
+                keys == key_lane + float(n * LANES)
+            )
+    panels = jnp.dot(next_rows[...], table[...], preferred_element_type=f32)
+    got = jnp.dot(word_rows[...], emits[...], preferred_element_type=f32)
     wide = iota((512, 2 * LANES), 1)
     half_of = (iota((512, 2 * LANES), 0) >> 2) & 1
     diagonal = (wide & (KW - 1)) == (wide >> 6) * 16 + share * 2 + half_of
     keep = (lane4 < KW) == ((row4 & 2) == 0)
     upper = (iota((32, 8, LANES), 1)) < 4
-
-    def step(tile, _):
-        asked = jnp.concatenate(
-            [all_ref[g, pl.ds(192 + tile, 1), :] for g in range(8)], axis=0
-        ).astype(bf16)
-        spread = jnp.dot(from8, asked, preferred_element_type=f32)
-        wanted = jnp.dot(
-            jnp.where(next_at, spread, 0.0).astype(bf16), ones, preferred_element_type=f32
-        )
-        hit = wanted == lane_f
-        chosen = jnp.concatenate([one_hot(hit & (code == b)) for b in range(4)], axis=1)
-        panels = jnp.dot(chosen, table[...], preferred_element_type=f32)
-        last = wanted == float(LANES)
-        last = jnp.concatenate([last, last], axis=1)
-        panels = jnp.where(last & diagonal, 1.0, panels)
-        spread = jnp.dot(from4, asked, preferred_element_type=f32)
-        keys = jnp.dot(
-            jnp.where(key_at, spread, 0.0).astype(bf16), weights, preferred_element_type=f32
-        )
-        chosen = jnp.concatenate(
-            [one_hot(keys == key_lane + float(n * LANES)) for n in range(12)], axis=1
-        )
-        got = jnp.dot(chosen, emits[...], preferred_element_type=f32)
-        got = jnp.where(keep, got, pltpu.roll(got, KW, 1)).reshape(32, 8, LANES)
-        other = pltpu.roll(got, 4, 1)
-        even = jnp.where(upper, got, other)
-        odd = jnp.where(upper, other, got)
+    for part in range(2):
+        rows = slice(part * 256, part * 256 + 256)
+        mine = jnp.where(late[part], got[rows, LANES:], got[rows, :LANES])
+        mine = jnp.where(keep, mine, pltpu.roll(mine, KW, 1)).reshape(32, 8, LANES)
+        other = pltpu.roll(mine, 4, 1)
+        even = jnp.where(upper, mine, other)
+        odd = jnp.where(upper, other, mine)
         both = jnp.stack([even, odd], axis=1).reshape(512, LANES)
-        panels = panels * jnp.concatenate([both, both], axis=1)
-        panel_ref[pl.ds(pl.multiple_of(tile * 512, 512), 512), :] = panels.astype(bf16)
-        return 0
-
-    lax.fori_loop(0, 8, step, 0)
+        rows = slice(part * 512, part * 512 + 512)
+        last = jnp.concatenate([wanted[part], wanted[part]], axis=1)
+        panel = jnp.where(last & diagonal, 1.0, panels[rows, :])
+        panel_ref[rows, :] = (panel * jnp.concatenate([both, both], axis=1)).astype(bf16)
 
 
 def pick(exps, everything):
     vmem = pl.BlockSpec(memory_space=pltpu.VMEM)
+    small = pl.BlockSpec((8, LANES), lambda i: (0, 0))
     return pl.pallas_call(
         pick_kernel,
+        grid=(4,),
         out_shape=(
             jax.ShapeDtypeStruct((4096, 2 * LANES), bf16),
             jax.ShapeDtypeStruct((8, LANES), f32),
             jax.ShapeDtypeStruct((8, LANES), f32),
         ),
         in_specs=[vmem] * 2,
-        out_specs=(vmem, vmem, vmem),
-        scratch_shapes=[pltpu.VMEM((512, 2 * LANES), bf16), pltpu.VMEM((1536, LANES), bf16)],
-        compiler_params=pltpu.CompilerParams(vmem_limit_bytes=40 * 1024 * 1024),
+        out_specs=(pl.BlockSpec((1024, 2 * LANES), lambda i: (i, 0)), small, small),
+        scratch_shapes=[
+            pltpu.VMEM((512, 2 * LANES), bf16),
+            pltpu.VMEM((768, 2 * LANES), bf16),
+            pltpu.VMEM((1024, 512), bf16),
+            pltpu.VMEM((512, 768), bf16),
+        ],
+        compiler_params=pltpu.CompilerParams(vmem_limit_bytes=60 * 1024 * 1024),
         name="pick",
     )(exps, everything)
 
 
-def chain_kernel(slot_ref, panel_ref, out_ref, ya, yb, ping, pong, logs):
+def chain_kernel(slot_ref, panel_ref, out_ref, ya, yb, ping, pong, logs, tops):
     length = slot_ref.shape[1]
 
     def widen(i, _):
@@ -333,38 +378,45 @@
         return 0
 
     lax.fori_loop(0, panel_ref.shape[0] // 256, widen, 0)
-    low = iota((KW, LANES), 1) < KW
-    logs[...] = jnp.ones_like(logs)
-
-    def scaled(value, at):
-        top = jnp.max(jnp.max(value, axis=0, keepdims=True), axis=1, keepdims=True)
-        logs[pl.ds(at, 1), :] = jnp.broadcast_to(top, (1, LANES))
-        return (value * (1.0 / top)).astype(bf16)
+    low = iota((16, LANES), 1) < KW
 
     def build(i, _):
         for u in range(8):
             t = i * 8 + u
             rows = pl.ds(slot_ref[0, t], 16, stride=4)
             a, b = ya[rows, :], yb[rows, :]
-            move = jnp.concatenate([a, pltpu.roll(a, KW, 1), b, pltpu.roll(b, KW, 1)], axis=0)
-            ping[t] = scaled(jnp.where(low, move, 0.0), t)
+            logs[pl.ds(t, 1), :] = jnp.max(jnp.maximum(a, b), axis=0, keepdims=True)
+            move = [a, pltpu.roll(a, KW, 1), b, pltpu.roll(b, KW, 1)]
+            move = [jnp.where(low, part, 0.0) for part in move]
+            ping[t] = jnp.concatenate(move, axis=0).astype(bf16)
         return 0
 
     lax.fori_loop(0, length // 8, build, 0)
+    peak = jnp.max(logs[0:length, :], axis=1, keepdims=True)
+    tops[...] = jnp.broadcast_to((1.0 / peak).astype(bf16).astype(f32), (length, LANES))
+    logs[0:length, :] = 1.0 / tops[...]
+    logs[length:, :] = jnp.ones((length, LANES), f32)
     src, dst, count, base = ping, pong, length // 2, length
-    while count >= 1:
-        unroll = min(count, 8)
-
-        def level(i, _, src=src, dst=dst, unroll=unroll, base=base):
+    while count > 1:
+        unroll = min(count, 16)
+
+        def level(i, _, src=src, dst=dst, unroll=unroll, base=base, first=src is ping and base == length):
             for u in range(unroll):
                 n = i * unroll + u
-                prod = jnp.dot(src[2 * n + 1][:, :KW], src[2 * n], preferred_element_type=f32)
-                dst[n] = scaled(prod, base + n)
+                left, right = src[2 * n + 1][:, :KW], src[2 * n]
+                if first:
+                    left = left * tops[pl.ds(2 * n + 1, 1), :KW].astype(bf16)
+                    right = right * tops[pl.ds(2 * n, 1), :].astype(bf16)
+                prod = jnp.dot(left, right, preferred_element_type=f32)
+                top = jnp.max(jnp.max(prod, axis=0, keepdims=True), axis=1, keepdims=True)
+                logs[pl.ds(base + n, 1), :] = jnp.broadcast_to(top, (1, LANES))
+                dst[n] = (prod * (1.0 / top)).astype(bf16)
             return 0
 
         lax.fori_loop(0, count // unroll, level, 0)
         src, dst, count, base = dst, src, count // 2, base + count
-    final = jnp.sum(jnp.sum(src[0].astype(f32), axis=0, keepdims=True), axis=1, keepdims=True)
+    prod = jnp.dot(src[1][:, :KW], src[0], preferred_element_type=f32)
+    final = jnp.sum(jnp.sum(prod, axis=0, keepdims=True), axis=1, keepdims=True)
     scale = jnp.sum(jnp.log(logs[...]), axis=0, keepdims=True)
     total = jnp.log(final) + scale - jnp.log(jnp.full((1, LANES), 8192.0, f32))
     out_ref[...] = jnp.broadcast_to(total / length, (8, LANES))
@@ -384,6 +436,7 @@
             pltpu.VMEM((length, KW, LANES), bf16),
             pltpu.VMEM((length // 2, KW, LANES), bf16),
             pltpu.VMEM((2 * length, LANES), f32),
+            pltpu.VMEM((length, LANES), f32),
         ],
         compiler_params=pltpu.CompilerParams(vmem_limit_bytes=40 * 1024 * 1024),
         name="chain",

time: 173 us -> 163 us (0.942)
  local copies, waits for them, and re-layouts: 10.2 us -> 2.53 us
  Pallas kernels: 23.6 us -> 20.9 us
    unnamed x17 -> x6, local copies, waits for them, and re-layouts: 9.16 us -> 0.81 us
    pallas_call x1, Pallas kernels: 8.84 us -> 5.47 us  [chain(): pl.pallas_call(chain_kernel, out_shape=jax.ShapeDtypeStruct((8, LANES), f...]
    pallas_call x1, Pallas kernels: 4.73 us -> 6.87 us  [prep(): pl.pallas_call(prep_kernel, out_shape=(jax.ShapeDtypeStruct((SHARDS, ROWS...]
  transfers between devices with their start and end apart: 1 -> 1, of which waited for: 1 -> 1; matrix products, arithmetic and copies ran while one was open for 0% -> 1% of each run, Pallas kernels for 0% -> 0%
where the time goes in v2:
time: 163 us; the launch traced here: 162 us
  blocking collectives  74.2 us (46%)
  waiting for transfers between devices  52.8 us (32%)
  Pallas kernels  20.9 us (13%)
  starting transfers between devices  11.2 us (7%)
  local copies, waits for them, and re-layouts  2.53 us (2%)
    all_to_all x1, blocking collectives, local(): lax.all_to_all(msg, 'state', split_axis=0, concat_axis=0, tiled=True)  56.3 us
    all_to_all x1, waiting for transfers between devices, local(): lax.all_to_all(panels.reshape(512, 8, 2 * LANES), ('state', 'seq'), split...  52.8 us
    all_gather x1, blocking collectives, local(): everything = lax.all_gather(mine, 'seq', axis=0, tiled=False)  17.9 us
    all_to_all x1, starting transfers between devices, local(): lax.all_to_all(panels.reshape(512, 8, 2 * LANES), ('state', 'seq'), split...  11.2 us
    pallas_call x1, Pallas kernels, pick(): pl.pallas_call(pick_kernel, grid=(4,), out_shape=(jax.ShapeDtypeStruct((4...  7.67 us
    pallas_call x1, Pallas kernels, prep(): pl.pallas_call(prep_kernel, out_shape=(jax.ShapeDtypeStruct((SHARDS, ROWS...  6.87 us
    pallas_call x1, Pallas kernels, chain(): pl.pallas_call(chain_kernel, out_shape=jax.ShapeDtypeStruct((8, LANES), f...  5.47 us
  transfers between devices with their start and end apart: 1, of which 1 were waited for; matrix products, arithmetic and copies ran while one was open for 1% of the time, Pallas kernels for 0%

profile of v2, /device:TPU:1, one launch (start us, length us, event | category | flops | bytes accessed | tf_op | source)
XLA Modules:
  0.0 162.3 jit_solution(12654310106311339868)
XLA Ops:
  0.6 6.9 %prep.1 = (bf16[64,24,512]{2,1,0:T(8,128)(2,1)}, bf16[256,512]{1,0:T(8,128)(2,1)}, s32[1,128]{1,0:T(1,128)}) custom-call(s32[2,128]{1,0:T(2,128)} %bitcast.15, s32[1,128]{1,0:T(1,128)} %tokens_hbm.1, s32[1,128]{1,0:T(1,128)} %tokens_hbm.1, s32[1024,128]{1,0:T(8,128)} %bitcast.14, s32[1,128]{1,0:T(1,128)} %bitcast.16, bf16[512,512]{1,0:T(8,128)(2,1)} %emit_hbm.1, ...), custom_call_target="tpu_custom_call" | custom-call | tf_op jit(solution)/shard_map/prep/pallas_call | solution.py:170
  7.5 0.0 copy-start.1
  7.5 56.3 %all_to_all.10.msg_ref = bf16[64,24,512]{2,1,0:T(8,128)(2,1)S(1)} all-to-all(bf16[64,24,512]{2,1,0:T(8,128)(2,1)} %get-tuple-element.12), channel_id=1, replica_groups=mesh['state'=64,'seq'=8] {'state'}, dimensions={0} | all-to-all | bytes 3145728 | tf_op jit(solution)/shard_map/all_to_all | solution.py:452
  63.8 0.0 copy-done.1
  63.8 0.9 score.1
  64.7 0.0 copy-start
  64.7 0.8 copy-done
  65.5 17.9 %all-gather = f32[1664,128]{1,0:T(8,128)} all-gather(f32[208,128]{1,0:T(8,128)S(1)} %get-tuple-element.15), channel_id=2, replica_groups=mesh['state'=64,'seq'=8] {'seq'}, dimensions={0}, use_global_device_ids=true | all-gather | bytes 958464 | tf_op jit(solution)/shard_map/all_gather | solution.py:454
  83.4 7.7 %pick.1 = (bf16[4096,256]{1,0:T(8,128)(2,1)}, f32[8,128]{1,0:T(8,128)}, f32[8,128]{1,0:T(8,128)}) custom-call(f32[1024,128]{1,0:T(8,128)} %copy-done, f32[8,208,128]{2,1,0:T(8,128)} %bitcast.12), custom_call_target="tpu_custom_call" | custom-call | tf_op jit(solution)/shard_map/pick/pallas_call | solution.py:349
  91.1 0.0 copy-start.2
  91.1 11.2 %all-to-all-start.1 = ((bf16[512,8,256]{2,1,0:T(8,128)(2,1)}), bf16[512,8,256]{2,1,0:T(8,128)(2,1)S(1)}, u32[]{:S(2)}, u32[]{:S(2)}) async-start(bf16[512,8,256]{2,1,0:T(8,128)(2,1)} %bitcast.13), calls=%async_computation.1 | async-start | bytes 4194304 | tf_op jit(solution)/shard_map/all_to_all | solution.py:456
  102.3 1.2 slice_bitcast_fusion
  103.5 52.8 %all-to-all-done.1 = bf16[512,8,256]{2,1,0:T(8,128)(2,1)S(1)} async-done(((bf16[512,8,256]{2,1,0:T(8,128)(2,1)}), bf16[512,8,256]{2,1,0:T(8,128)(2,1)S(1)}, u32[]{:S(2)}, u32[]{:S(2)}) %all-to-all-start.1) | async-done | bytes 2097184 | tf_op jit(solution)/shard_map/all_to_all | solution.py:456
  156.3 0.0 copy-done.2
  156.3 5.5 %chain.1 = f32[8,128]{1,0:T(8,128)S(1)} custom-call(s32[1,128]{1,0:T(1,128)S(1)} %copy-done.2, bf16[4096,256]{1,0:T(8,128)(2,1)S(1)} %bitcast.11), custom_call_target="tpu_custom_call" | custom-call | tf_op jit(solution)/shard_map/chain/pallas_call | solution.py:428
  161.8 0.5 slice.9
Async XLA Ops:
  7.5 56.3 %copy-start.1 = (bf16[256,512]{1,0:T(8,128)(2,1)S(1)}, bf16[256,512]{1,0:T(8,128)(2,1)}, u32[]{:S(2)}) copy-start(bf16[256,512]{1,0:T(8,128)(2,1)} %get-tuple-element.13.mat_ref) | copy-start | bytes 786436
  64.7 0.8 copy-start
  91.1 65.2 %copy-start.2 = (s32[1,128]{1,0:T(1,128)S(1)}, s32[1,128]{1,0:T(1,128)}, u32[]{:S(2)}) copy-start(s32[1,128]{1,0:T(1,128)} %get-tuple-element.11.slot_ref) | copy-start | bytes 1540
  91.1 65.2 %all-to-all-start.1 = ((bf16[512,8,256]{2,1,0:T(8,128)(2,1)}), bf16[512,8,256]{2,1,0:T(8,128)(2,1)S(1)}, u32[]{:S(2)}, u32[]{:S(2)}) async-start(bf16[512,8,256]{2,1,0:T(8,128)(2,1)} %bitcast.13), calls=%async_computation.1 | async-start | bytes 4194304 | tf_op jit(solution)/shard_map/all_to_all | solution.py:456

commit v3 on v2

--- a/solution.py
+++ b/solution.py
@@ -11,6 +11,8 @@
 LANES = 128
 RANKS = 3
 SHARDS = 64
+SLOTS = 4
+SENT = 3
 ROWS = 24
 XROWS = 208
 f32 = jnp.float32
@@ -116,20 +118,20 @@
     rank_col = jnp.sum(wide[...], axis=1, keepdims=True)
     own_block_col = jnp.sum(ints(lane == cluster_col, block_row), axis=1, keepdims=True)
     own_block_row = line(own_block_col)
-    same = own_block_col == own_block_row
+    same = (own_block_col >> 1) == (own_block_row >> 1)
     times_col = jnp.sum(ints(same & (lane < sub), 1), axis=1, keepdims=True)
     times_row = jnp.sum(ints(same & (sub < lane), 1), axis=0, keepdims=True)
-    slot_ref[...] = (own_block_row >> 1) * 64 + (own_block_row & 1) * 2 + times_row
+    slot_ref[...] = times_row * 4096 + (own_block_row >> 1) * 64
     following = jnp.sum(ints(lane == sub + 1, own_block_row), axis=1, keepdims=True)
     following = jnp.where(iota((LANES, 1), 0) == length - 1, LANES, following)
-    slots_col = own_block_col * 2 + times_col
+    slots_col = (own_block_col >> 1) * SLOTS + times_col
     asked = jnp.zeros((SHARDS, LANES), f32)
     slot_line = iota((LANES, 2 * LANES), 1)
     at_slot = slot_line == slots_col
     owner = (iota((SHARDS, 2 * LANES), 1) >> 2) == iota((SHARDS, 2 * LANES), 0)
     slot_sub = iota((2 * LANES, LANES), 0) & 3
     slot_lane = iota((2 * LANES, LANES), 1)
-    for field, values in enumerate((following, token_col >> 11, rank_col)):
+    for field, values in enumerate((following, token_col >> 11, rank_col + 32 * (own_block_col & 1))):
         value_row = jnp.sum(ints(at_slot, values), axis=0, keepdims=True)
         spread = jnp.where(owner, value_row.astype(f32), 0.0).astype(bf16)
         asked += jnp.dot(
@@ -138,11 +140,13 @@
     count_lane = jnp.where(lane == 12 + (block_col & 1), counts_of[...], 0.0).astype(bf16)
     count_owner = one_hot((block_row >> 1) == iota((SHARDS, LANES), 0))
     asked += jnp.dot(count_owner, count_lane, preferred_element_type=f32)
+    full = jnp.max(times_row, axis=1, keepdims=True) >= SENT
+    asked += jnp.where(full & (iota((SHARDS, LANES), 1) == 14), 1.0, 0.0)
 
     for copy in kept:
         copy.wait()
     row = iota((16, LANES), 0)
-    want = (row >> 3) * KW + (row & 3) * 16 + share * 2 + ((row >> 2) & 1)
+    want = (row >> 3) * KW + (row & 7) * 8 + share
     targets = jnp.dot(
         one_hot(iota((16, LANES), 1) == want), in_kept[...], preferred_element_type=f32
     ).astype(bf16)
@@ -251,7 +255,8 @@
 
 
 def pick_kernel(
-    exps_ref, all_ref, panel_ref, trans_ref, emit_ref, table, emits, next_rows, word_rows
+    exps_ref, all_ref, panel_ref, spare_ref, trans_ref, emit_ref, full_ref,
+    table, emits, next_rows, word_rows, blocks, keys, stage,
 ):
     share = lax.axis_index("seq")
     step = pl.program_id(0)
@@ -260,10 +265,15 @@
     def _():
         total = jnp.zeros((1, LANES), f32)
         heap = jnp.zeros((SHARDS, LANES), f32)
+        full = jnp.zeros((8, LANES), f32)
         for g in range(8):
             total = total + all_ref[g, 200:201, :]
+            full = jnp.maximum(full, all_ref[g, 192:200, :])
             for x in range(RANKS):
                 heap = heap + jnp.exp(all_ref[g, x * SHARDS : (x + 1) * SHARDS, :])
+        full = jnp.where((iota((8, LANES), 1) & 15) == 14, full, 0.0)
+        full = jnp.max(jnp.max(full, axis=0, keepdims=True), axis=1, keepdims=True)
+        full_ref[...] = jnp.broadcast_to(full, (8, LANES))
         trans_ref[...] = jnp.broadcast_to(jnp.log(total), (8, LANES))
         emit_norm = jnp.log(jnp.sum(heap, axis=0, keepdims=True))
         emit_ref[...] = jnp.broadcast_to(emit_norm, (8, LANES))
@@ -272,75 +282,64 @@
             lanes = slice((g >> 2) * LANES, (g >> 2) * LANES + LANES)
             emits[rows, lanes] = jnp.exp(all_ref[g, 0:192, :] - emit_norm).astype(bf16)
         low = iota((LANES, LANES), 1) < KW
-        for half in range(2):
-            cols = [exps_ref[pl.ds(half * 4 + j, LANES, stride=8), :] / total for j in range(4)]
-            for pair in range(2):
-                first, second = cols[2 * pair], cols[2 * pair + 1]
-                lanes = slice(pair * LANES, (pair + 1) * LANES)
-                at = 2 * half * LANES
-                table[at : at + LANES, lanes] = jnp.where(
-                    low, first, pltpu.roll(second, KW, 1)
-                ).astype(bf16)
-                table[at + LANES : at + 2 * LANES, lanes] = jnp.where(
-                    low, pltpu.roll(first, KW, 1), second
-                ).astype(bf16)
-
-    row8, lane8 = iota((512, LANES), 0), iota((512, LANES), 1)
-    row4, lane4 = iota((256, LANES), 0), iota((256, LANES), 1)
-    from8 = one_hot(((iota((512, 8), 0) >> 3) & 7) == iota((512, 8), 1))
-    from4 = one_hot(((iota((256, 8), 0) >> 2) & 7) == iota((256, 8), 1))
-    next_at = lane8 == (row8 >> 6) * 16 + (row8 & 3)
-    key_at = ((lane4 >> 4) == (row4 >> 5)) & ((lane4 & 3) == (row4 & 3))
-    key_at = key_at & ((lane4 & 15) >= 4) & ((lane4 & 15) < 12)
+        for pair in range(4):
+            first = exps_ref[pl.ds(2 * pair, LANES, stride=8), :] / total
+            second = exps_ref[pl.ds(2 * pair + 1, LANES, stride=8), :] / total
+            lanes = slice(pair * LANES, (pair + 1) * LANES)
+            table[0:LANES, lanes] = jnp.where(low, first, pltpu.roll(second, KW, 1)).astype(bf16)
+            table[LANES:, lanes] = jnp.where(low, pltpu.roll(first, KW, 1), second).astype(bf16)
+
+    row, lane = iota((256, LANES), 0), iota((256, LANES), 1)
+    chain_of = one_hot((iota((256, 8), 0) & 7) == iota((256, 8), 1))
+    mine = ((lane >> 4) == ((row >> 3) & 7)) & ((lane & 3) == (row >> 6))
+    next_at = mine & ((lane & 15) < 4)
+    key_at = mine & ((lane & 15) >= 4) & ((lane & 15) < 12)
     ones = jnp.ones((LANES, LANES), bf16)
     weights = jnp.where((iota((LANES, LANES), 0) & 15) >= 8, 64.0, 1.0).astype(bf16)
-    code = (row8 & 7) >> 1
-    lane_f = lane8.astype(f32)
-    key_lane = lane4.astype(f32)
-    wanted, late = [], []
     for part in range(2):
         asked = jnp.concatenate(
             [all_ref[g, pl.ds(192 + step * 2 + part, 1), :] for g in range(8)], axis=0
         ).astype(bf16)
-        spread = jnp.dot(from8, asked, preferred_element_type=f32)
+        spread = jnp.dot(chain_of, asked, preferred_element_type=f32)
         block = jnp.dot(
             jnp.where(next_at, spread, 0.0).astype(bf16), ones, preferred_element_type=f32
         )
-        hit = block == lane_f
-        for b in range(4):
-            next_rows[part * 512 : part * 512 + 512, b * LANES : (b + 1) * LANES] = one_hot(
-                hit & (code == b)
-            )
-        wanted.append(block == float(LANES))
-        spread = jnp.dot(from4, asked, preferred_element_type=f32)
-        keys = jnp.dot(
+        key = jnp.dot(
             jnp.where(key_at, spread, 0.0).astype(bf16), weights, preferred_element_type=f32
         )
-        late.append(keys >= 768.0)
-        keys = jnp.where(late[-1], keys - 768.0, keys)
-        for n in range(6):
-            word_rows[part * 256 : part * 256 + 256, n * LANES : (n + 1) * LANES] = one_hot(
-                keys == key_lane + float(n * LANES)
-            )
+        for n in range(SLOTS):
+            rows = slice(n * LANES + part * 64, n * LANES + part * 64 + 64)
+            blocks[rows, :] = block[n * 64 : n * 64 + 64, :]
+            keys[rows, :] = key[n * 64 : n * 64 + 64, :]
+    lane_f = iota((512, LANES), 1).astype(f32)
+    block, key = blocks[...], keys[...]
+    second = key >= 2048.0
+    key = jnp.where(second, key - 2048.0, key)
+    late = key >= 768.0
+    key = jnp.where(late, key - 768.0, key)
+    hit = block == lane_f
+    next_rows[:, :LANES] = one_hot(hit & ~second)
+    next_rows[:, LANES:] = one_hot(hit & second)
+    for n in range(6):
+        word_rows[:, n * LANES : (n + 1) * LANES] = one_hot(key == lane_f + float(n * LANES))
+    got = jnp.dot(word_rows[...], emits[...], preferred_element_type=f32)
+    emit = jnp.where(late, got[:, LANES:], got[:, :LANES])
+    emit = jnp.where((lane_f < float(KW)) ^ second, emit, pltpu.roll(emit, KW, 1))
     panels = jnp.dot(next_rows[...], table[...], preferred_element_type=f32)
-    got = jnp.dot(word_rows[...], emits[...], preferred_element_type=f32)
-    wide = iota((512, 2 * LANES), 1)
-    half_of = (iota((512, 2 * LANES), 0) >> 2) & 1
-    diagonal = (wide & (KW - 1)) == (wide >> 6) * 16 + share * 2 + half_of
-    keep = (lane4 < KW) == ((row4 & 2) == 0)
-    upper = (iota((32, 8, LANES), 1)) < 4
-    for part in range(2):
-        rows = slice(part * 256, part * 256 + 256)
-        mine = jnp.where(late[part], got[rows, LANES:], got[rows, :LANES])
-        mine = jnp.where(keep, mine, pltpu.roll(mine, KW, 1)).reshape(32, 8, LANES)
-        other = pltpu.roll(mine, 4, 1)
-        even = jnp.where(upper, mine, other)
-        odd = jnp.where(upper, other, mine)
-        both = jnp.stack([even, odd], axis=1).reshape(512, LANES)
-        rows = slice(part * 512, part * 512 + 512)
-        last = jnp.concatenate([wanted[part], wanted[part]], axis=1)
-        panel = jnp.where(last & diagonal, 1.0, panels[rows, :])
-        panel_ref[rows, :] = (panel * jnp.concatenate([both, both], axis=1)).astype(bf16)
+    last = block == float(LANES)
+    row_of = iota((512, LANES), 1) & (KW - 1)
+    for pair in range(4):
+        column = (pair * 2 + (iota((512, LANES), 1) >> 6)) * 8 + share
+        panel = panels[:, pair * LANES : (pair + 1) * LANES]
+        panel = jnp.where(last & (row_of == column), 1.0, panel) * emit
+        for n in range(SLOTS):
+            stage[pl.ds(n * 512 + pair, LANES, stride=4), :] = panel[n * LANES : (n + 1) * LANES, :]
+    for n in range(SLOTS):
+        block = stage[n * 512 : (n + 1) * 512, :].reshape(LANES, 4, LANES).astype(bf16)
+        if n < SENT:
+            panel_ref[:, :, n * LANES : (n + 1) * LANES] = block
+        else:
+            spare_ref[...] = block
 
 
 def pick(exps, everything):
@@ -350,44 +349,61 @@
         pick_kernel,
         grid=(4,),
         out_shape=(
-            jax.ShapeDtypeStruct((4096, 2 * LANES), bf16),
+            jax.ShapeDtypeStruct((512, 4, SENT * LANES), bf16),
+            jax.ShapeDtypeStruct((512, 4, LANES), bf16),
+            jax.ShapeDtypeStruct((8, LANES), f32),
             jax.ShapeDtypeStruct((8, LANES), f32),
             jax.ShapeDtypeStruct((8, LANES), f32),
         ),
         in_specs=[vmem] * 2,
-        out_specs=(pl.BlockSpec((1024, 2 * LANES), lambda i: (i, 0)), small, small),
+        out_specs=(
+            pl.BlockSpec((LANES, 4, SENT * LANES), lambda i: (i, 0, 0)),
+            pl.BlockSpec((LANES, 4, LANES), lambda i: (i, 0, 0)),
+            small,
+            small,
+            small,
+        ),
         scratch_shapes=[
-            pltpu.VMEM((512, 2 * LANES), bf16),
-            pltpu.VMEM((768, 2 * LANES), bf16),
-            pltpu.VMEM((1024, 512), bf16),
+            pltpu.VMEM((256, 512), bf16),
+            pltpu.VMEM((768, 256), bf16),
+            pltpu.VMEM((512, 256), bf16),
             pltpu.VMEM((512, 768), bf16),
+            pltpu.VMEM((512, LANES), f32),
+            pltpu.VMEM((512, LANES), f32),
+            pltpu.VMEM((2048, LANES), f32),
         ],
         compiler_params=pltpu.CompilerParams(vmem_limit_bytes=60 * 1024 * 1024),
         name="pick",
     )(exps, everything)
 
 
-def chain_kernel(slot_ref, panel_ref, out_ref, ya, yb, ping, pong, logs, tops):
+def chain_kernel(slot_ref, panel_ref, spare_ref, out_ref, wide, ping, pong, logs, tops):
     length = slot_ref.shape[1]
 
     def widen(i, _):
-        rows = pl.ds(pl.multiple_of(i * 256, 256), 256)
-        got = panel_ref[rows, :].astype(f32)
-        ya[rows, :] = got[:, :LANES]
-        yb[rows, :] = got[:, LANES:]
+        some = pl.ds(pl.multiple_of(i * 32, 32), 32)
+        for n in range(SLOTS):
+            if n < SENT:
+                got = panel_ref[some, :, n * LANES : (n + 1) * LANES].astype(f32)
+            else:
+                got = spare_ref[some, :, :].astype(f32)
+            rows = pl.ds(pl.multiple_of(n * 4096 + i * 256, 256), 256)
+            wide[rows, :] = jnp.concatenate([got, got], axis=1).reshape(256, LANES)
         return 0
 
-    lax.fori_loop(0, panel_ref.shape[0] // 256, widen, 0)
-    low = iota((16, LANES), 1) < KW
+    lax.fori_loop(0, panel_ref.shape[0] // 32, widen, 0)
+    low = iota((8, LANES), 1) < KW
 
     def build(i, _):
         for u in range(8):
             t = i * 8 + u
-            rows = pl.ds(slot_ref[0, t], 16, stride=4)
-            a, b = ya[rows, :], yb[rows, :]
-            logs[pl.ds(t, 1), :] = jnp.max(jnp.maximum(a, b), axis=0, keepdims=True)
-            move = [a, pltpu.roll(a, KW, 1), b, pltpu.roll(b, KW, 1)]
-            move = [jnp.where(low, part, 0.0) for part in move]
+            start = slot_ref[0, t]
+            parts = [wide[pl.ds(start + pair, 8, stride=8), :] for pair in range(4)]
+            top = jnp.maximum(jnp.maximum(parts[0], parts[1]), jnp.maximum(parts[2], parts[3]))
+            logs[pl.ds(t, 1), :] = jnp.max(top, axis=0, keepdims=True)
+            move = []
+            for part in parts:
+                move += [jnp.where(low, part, 0.0), jnp.where(low, pltpu.roll(part, KW, 1), 0.0)]
             ping[t] = jnp.concatenate(move, axis=0).astype(bf16)
         return 0
 
@@ -422,17 +438,16 @@
     out_ref[...] = jnp.broadcast_to(total / length, (8, LANES))
 
 
-def chain(slots, panels):
+def chain(slots, panels, spare):
     length = slots.shape[1]
     vmem = pl.BlockSpec(memory_space=pltpu.VMEM)
     return pl.pallas_call(
         chain_kernel,
         out_shape=jax.ShapeDtypeStruct((8, LANES), f32),
-        in_specs=[pl.BlockSpec(memory_space=pltpu.SMEM), vmem],
+        in_specs=[pl.BlockSpec(memory_space=pltpu.SMEM), vmem, vmem],
         out_specs=vmem,
         scratch_shapes=[
-            pltpu.VMEM((4096, LANES), f32),
-            pltpu.VMEM((4096, LANES), f32),
+            pltpu.VMEM((SLOTS * 4096, LANES), f32),
             pltpu.VMEM((length, KW, LANES), bf16),
             pltpu.VMEM((length // 2, KW, LANES), bf16),
             pltpu.VMEM((2 * length, LANES), f32),
@@ -440,7 +455,7 @@
         ],
         compiler_params=pltpu.CompilerParams(vmem_limit_bytes=40 * 1024 * 1024),
         name="chain",
-    )(slots, panels)
+    )(slots, panels, spare)
 
 
 def local(
@@ -452,15 +467,14 @@
     arrived = lax.all_to_all(msg, "state", split_axis=0, concat_axis=0, tiled=True)
     exps, mine = score(arrived, mat)
     everything = lax.all_gather(mine, "seq", axis=0, tiled=False)
-    panels, trans_norm, emit_norm = pick(exps, everything)
-    got = lax.all_to_all(
-        panels.reshape(512, 8, 2 * LANES),
-        ("state", "seq"),
-        split_axis=0,
-        concat_axis=0,
-        tiled=True,
-    ).reshape(4096, 2 * LANES)
-    token_loglik = chain(slots, got)
+    panels, spare, trans_norm, emit_norm, full = pick(exps, everything)
+
+    def exchange(value):
+        return lax.all_to_all(value, ("state", "seq"), split_axis=0, concat_axis=0, tiled=True)
+
+    got = exchange(panels)
+    spare = lax.cond(full[0, 0] > 0.5, exchange, lambda value: value, spare)
+    token_loglik = chain(slots, got, spare)
     return (token_loglik[0, :1], trans_norm[0], emit_norm[0])
 
 

time: 163 us -> 154 us (0.945)
  waiting for transfers between devices: 52.8 us -> 41.8 us
    all_to_all x1, waiting for transfers between devices: 52.8 us -> 41.8 us  [exchange(): lax.all_to_all(value, ('state', 'seq'), split_axis=0, concat_axis=0, tile...]
where the time goes in v3:
time: 154 us
  blocking collectives  74.2 us (48%)
  waiting for transfers between devices  41.8 us (27%)
  Pallas kernels  21.6 us (14%)
  starting transfers between devices  11.2 us (7%)
  local copies, waits for them, and re-layouts  3.73 us (2%)
    all_to_all x1, blocking collectives, local(): lax.all_to_all(msg, 'state', split_axis=0, concat_axis=0, tiled=True)  56.3 us
    all_to_all x1, waiting for transfers between devices, exchange(): lax.all_to_all(value, ('state', 'seq'), split_axis=0, concat_axis=0, tile...  41.8 us
    all_gather x1, blocking collectives, local(): everything = lax.all_gather(mine, 'seq', axis=0, tiled=False)  17.9 us
    all_to_all x1, starting transfers between devices, exchange(): lax.all_to_all(value, ('state', 'seq'), split_axis=0, concat_axis=0, tile...  11.2 us
    pallas_call x1, Pallas kernels, pick(): pl.pallas_call(pick_kernel, grid=(4,), out_shape=(jax.ShapeDtypeStruct((5...  7.75 us
    pallas_call x1, Pallas kernels, prep(): pl.pallas_call(prep_kernel, out_shape=(jax.ShapeDtypeStruct((SHARDS, ROWS...  6.87 us
    pallas_call x1, Pallas kernels, chain(): pl.pallas_call(chain_kernel, out_shape=jax.ShapeDtypeStruct((8, LANES), f...  6.13 us
  transfers between devices with their start and end apart: 1, of which 1 were waited for; matrix products, arithmetic and copies ran while one was open for 1% of the time, Pallas kernels for 0%

profile of v3, /device:TPU:1, one launch (start us, length us, event | category | flops | bytes accessed | tf_op | source)
XLA Modules:
  0.0 153.9 jit_solution(5814200156411359045)
XLA Ops:
  0.6 6.9 %prep.1 = (bf16[64,24,512]{2,1,0:T(8,128)(2,1)}, bf16[256,512]{1,0:T(8,128)(2,1)}, s32[1,128]{1,0:T(1,128)}) custom-call(s32[2,128]{1,0:T(2,128)} %bitcast.12, s32[1,128]{1,0:T(1,128)} %tokens_hbm.1, s32[1,128]{1,0:T(1,128)} %tokens_hbm.1, s32[1024,128]{1,0:T(8,128)} %bitcast.11, s32[1,128]{1,0:T(1,128)} %bitcast.13, bf16[512,512]{1,0:T(8,128)(2,1)} %emit_hbm.1, ...), custom_call_target="tpu_custom_call" | custom-call | tf_op jit(solution)/shard_map/prep/pallas_call | solution.py:174
  7.5 0.0 copy-start.1
  7.5 56.3 %all_to_all.15.msg_ref = bf16[64,24,512]{2,1,0:T(8,128)(2,1)S(1)} all-to-all(bf16[64,24,512]{2,1,0:T(8,128)(2,1)} %get-tuple-element.19), channel_id=1, replica_groups=mesh['state'=64,'seq'=8] {'state'}, dimensions={0} | all-to-all | bytes 3145728 | tf_op jit(solution)/shard_map/all_to_all | solution.py:467
  63.8 0.0 copy-done.1
  63.8 0.9 score.1
  64.7 0.0 copy-start
  64.7 0.8 copy-done
  65.5 17.9 %all-gather = f32[1664,128]{1,0:T(8,128)} all-gather(f32[208,128]{1,0:T(8,128)S(1)} %get-tuple-element.22), channel_id=2, replica_groups=mesh['state'=64,'seq'=8] {'seq'}, dimensions={0}, use_global_device_ids=true | all-gather | bytes 958464 | tf_op jit(solution)/shard_map/all_gather | solution.py:469
  83.4 7.8 %pick.1 = (bf16[512,4,384]{2,1,0:T(4,128)(2,1)}, bf16[512,4,128]{2,1,0:T(4,128)(2,1)S(1)}, f32[8,128]{1,0:T(8,128)}, f32[8,128]{1,0:T(8,128)}, f32[8,128]{1,0:T(8,128)}) custom-call(f32[1024,128]{1,0:T(8,128)} %copy-done, f32[8,208,128]{2,1,0:T(8,128)} %bitcast.10), custom_call_target="tpu_custom_call" | custom-call | tf_op jit(solution)/shard_map/pick/pallas_call | solution.py:348
  91.2 1.2 slice.12
  93.0 0.0 copy-start.2
  93.0 11.2 %all-to-all-start.2 = ((bf16[512,4,384]{2,1,0:T(4,128)(2,1)}), bf16[512,4,384]{2,1,0:T(4,128)(2,1)S(1)}, u32[]{:S(2)}, u32[]{:S(2)}) async-start(bf16[512,4,384]{2,1,0:T(4,128)(2,1)} %get-tuple-element.23), calls=%async_computation.2 | async-start | bytes 3145728 | tf_op jit(solution)/shard_map/all_to_all | solution.py:473
  104.3 1.2 slice_bitcast_fusion
  105.5 41.8 %all-to-all-done.2.panel_ref = bf16[512,4,384]{2,1,0:T(4,128)(2,1)S(1)} async-done(((bf16[512,4,384]{2,1,0:T(4,128)(2,1)}), bf16[512,4,384]{2,1,0:T(4,128)(2,1)S(1)}, u32[]{:S(2)}, u32[]{:S(2)}) %all-to-all-start.2) | async-done | bytes 1572896 | tf_op jit(solution)/shard_map/all_to_all | solution.py:473
  147.3 0.0 copy-done.2
  147.3 6.1 %chain.1 = f32[8,128]{1,0:T(8,128)S(1)} custom-call(s32[1,128]{1,0:T(1,128)S(1)} %copy-done.2, bf16[512,4,384]{2,1,0:T(4,128)(2,1)S(1)} %all-to-all-done.2.panel_ref, bf16[512,4,128]{2,1,0:T(4,128)(2,1)S(1)} %get-tuple-element.30.spare_ref), custom_call_target="tpu_custom_call" | custom-call | tf_op jit(solution)/shard_map/chain/pallas_call | solution.py:444
  153.4 0.5 slice.13
  (1 shorter events, 0.0 us)
Async XLA Ops:
  7.5 56.3 %copy-start.1 = (bf16[256,512]{1,0:T(8,128)(2,1)S(1)}, bf16[256,512]{1,0:T(8,128)(2,1)}, u32[]{:S(2)}) copy-start(bf16[256,512]{1,0:T(8,128)(2,1)} %get-tuple-element.20.mat_ref) | copy-start | bytes 786436
  64.7 0.8 copy-start
  93.0 54.3 %copy-start.2 = (s32[1,128]{1,0:T(1,128)S(1)}, s32[1,128]{1,0:T(1,128)}, u32[]{:S(2)}) copy-start(s32[1,128]{1,0:T(1,128)} %get-tuple-element.18.slot_ref) | copy-start | bytes 1540
  93.0 54.2 %all-to-all-start.2 = ((bf16[512,4,384]{2,1,0:T(4,128)(2,1)}), bf16[512,4,384]{2,1,0:T(4,128)(2,1)S(1)}, u32[]{:S(2)}, u32[]{:S(2)}) async-start(bf16[512,4,384]{2,1,0:T(4,128)(2,1)} %get-tuple-element.23), calls=%async_computation.2 | async-start | bytes 3145728 | tf_op jit(solution)/shard_map/all_to_all | solution.py:473

commit v4 on v3

--- a/solution.py
+++ b/solution.py
@@ -11,6 +11,7 @@
 LANES = 128
 RANKS = 3
 SHARDS = 64
+PICK_VMEM = 60 * 1024 * 1024 + 512 * 1024
 SLOTS = 4
 SENT = 3
 ROWS = 24
@@ -201,6 +202,12 @@
     )
 
 
+def thirds(value):
+    high = value.astype(bf16).astype(f32)
+    mid = (value - high).astype(bf16).astype(f32)
+    return [high, mid, value - high - mid]
+
+
 def score_kernel(msg_ref, mat_ref, exps_ref, out_ref, words, raw):
     share = lax.axis_index("seq")
     total = jnp.zeros((1, LANES), f32)
@@ -220,22 +227,29 @@
     spread = one_hot(iota((LANES, LANES), 0) == 12 + (iota((LANES, LANES), 1) >> 6))
     counts = jnp.dot(asked.astype(bf16), spread, preferred_element_type=f32)
     low = iota((SHARDS, LANES), 1) < KW
+    scores, valid = [], []
     for x in range(RANKS):
-        scores = jnp.where(
+        some = jnp.where(
             low,
             words[pl.ds(2 * x, SHARDS, stride=8), :],
             words[pl.ds(2 * x + 1, SHARDS, stride=8), :],
         )
-        valid = (RANKS * share + x).astype(f32) < counts
-        out_ref[x * SHARDS : (x + 1) * SHARDS, :] = jnp.where(valid, scores, -1e30)
+        valid.append((RANKS * share + x).astype(f32) < counts)
+        scores.append(jnp.where(valid[-1], some, -1e30))
+    top = jnp.max(jnp.maximum(jnp.maximum(scores[0], scores[1]), scores[2]), axis=0, keepdims=True)
+    top = top.astype(bf16).astype(f32)
+    parts = [jnp.where(v, jnp.exp(s - top), 0.0) for s, v in zip(scores, valid)]
+    mass = jnp.sum(parts[0] + parts[1] + parts[2], axis=0, keepdims=True)
     lane16 = iota((8, LANES), 1) >> 4
     packed = jnp.zeros((8, LANES), f32)
     for m in range(8):
         some = raw[pl.ds(m * 8 + 6, 8, stride=64), :]
         some = pltpu.roll(some, m * 16, 1) if m else some
         packed = jnp.where(lane16 == m, some, packed)
-    out_ref[192:200, :] = packed
-    out_ref[200:208, :] = jnp.broadcast_to(total, (8, LANES))
+    sums = jnp.concatenate([top] + thirds(mass) + thirds(total) + [jnp.zeros_like(top)], axis=0)
+    message = jnp.concatenate(parts + [packed, sums], axis=0).astype(bf16)
+    for copy in range(4):
+        out_ref[copy] = message
 
 
 def score(msg, mat):
@@ -244,7 +258,7 @@
         score_kernel,
         out_shape=(
             jax.ShapeDtypeStruct((1024, LANES), f32),
-            jax.ShapeDtypeStruct((XROWS, LANES), f32),
+            jax.ShapeDtypeStruct((4, XROWS, LANES), bf16),
         ),
         in_specs=[vmem] * 2,
         out_specs=(vmem, vmem),
@@ -255,32 +269,35 @@
 
 
 def pick_kernel(
-    exps_ref, all_ref, panel_ref, spare_ref, trans_ref, emit_ref, full_ref,
-    table, emits, next_rows, word_rows, blocks, keys, stage,
+    exps_ref, all_ref, panel_hbm, spare_hbm, trans_ref, emit_ref, full_ref,
+    table, emits, next_rows, word_rows, blocks, keys, stage, panel_ref, spare_ref, sems,
 ):
     share = lax.axis_index("seq")
-    step = pl.program_id(0)
-
-    @pl.when(step == 0)
-    def _():
+    order = [(g & 1) * 4 + (g >> 1) for g in range(8)]
+    if True:
+        sums = [all_ref[n, 200:208, :].astype(f32) for n in order]
         total = jnp.zeros((1, LANES), f32)
-        heap = jnp.zeros((SHARDS, LANES), f32)
+        top = sums[0][0:1, :]
         full = jnp.zeros((8, LANES), f32)
         for g in range(8):
-            total = total + all_ref[g, 200:201, :]
-            full = jnp.maximum(full, all_ref[g, 192:200, :])
-            for x in range(RANKS):
-                heap = heap + jnp.exp(all_ref[g, x * SHARDS : (x + 1) * SHARDS, :])
+            total = total + (sums[g][4:5, :] + sums[g][5:6, :] + sums[g][6:7, :])
+            top = jnp.maximum(top, sums[g][0:1, :])
+            full = jnp.maximum(full, all_ref[order[g], 192:200, :].astype(f32))
+        mass = jnp.zeros((1, LANES), f32)
+        for g in range(8):
+            part = sums[g][1:2, :] + sums[g][2:3, :] + sums[g][3:4, :]
+            mass = mass + part * jnp.exp(sums[g][0:1, :] - top)
         full = jnp.where((iota((8, LANES), 1) & 15) == 14, full, 0.0)
         full = jnp.max(jnp.max(full, axis=0, keepdims=True), axis=1, keepdims=True)
         full_ref[...] = jnp.broadcast_to(full, (8, LANES))
         trans_ref[...] = jnp.broadcast_to(jnp.log(total), (8, LANES))
-        emit_norm = jnp.log(jnp.sum(heap, axis=0, keepdims=True))
+        emit_norm = top + jnp.log(mass)
         emit_ref[...] = jnp.broadcast_to(emit_norm, (8, LANES))
         for g in range(8):
             rows = slice((g & 3) * 192, (g & 3) * 192 + 192)
             lanes = slice((g >> 2) * LANES, (g >> 2) * LANES + LANES)
-            emits[rows, lanes] = jnp.exp(all_ref[g, 0:192, :] - emit_norm).astype(bf16)
+            scale = jnp.exp(sums[g][0:1, :] - emit_norm)
+            emits[rows, lanes] = (all_ref[order[g], 0:192, :].astype(f32) * scale).astype(bf16)
         low = iota((LANES, LANES), 1) < KW
         for pair in range(4):
             first = exps_ref[pl.ds(2 * pair, LANES, stride=8), :] / total
@@ -289,65 +306,77 @@
             table[0:LANES, lanes] = jnp.where(low, first, pltpu.roll(second, KW, 1)).astype(bf16)
             table[LANES:, lanes] = jnp.where(low, pltpu.roll(first, KW, 1), second).astype(bf16)
 
-    row, lane = iota((256, LANES), 0), iota((256, LANES), 1)
-    chain_of = one_hot((iota((256, 8), 0) & 7) == iota((256, 8), 1))
-    mine = ((lane >> 4) == ((row >> 3) & 7)) & ((lane & 3) == (row >> 6))
+    row, lane = iota((512, LANES), 0), iota((512, LANES), 1)
+    pick_row, pick_lane = iota((512, 64), 0), iota((512, 64), 1)
+    mine = ((lane >> 4) == ((row >> 3) & 7)) & ((lane & 3) == (row >> 7))
     next_at = mine & ((lane & 15) < 4)
     key_at = mine & ((lane & 15) >= 4) & ((lane & 15) < 12)
     ones = jnp.ones((LANES, LANES), bf16)
     weights = jnp.where((iota((LANES, LANES), 0) & 15) >= 8, 64.0, 1.0).astype(bf16)
-    for part in range(2):
-        asked = jnp.concatenate(
-            [all_ref[g, pl.ds(192 + step * 2 + part, 1), :] for g in range(8)], axis=0
-        ).astype(bf16)
-        spread = jnp.dot(chain_of, asked, preferred_element_type=f32)
+    asked = jnp.concatenate([all_ref[n, 192:200, :].astype(f32) for n in order], axis=0)
+    asked = asked.astype(bf16)
+    lane_f = lane.astype(f32)
+    row_of = lane & (KW - 1)
+    copies = []
+    for step in range(4):
+        source = (pick_row & 7) * 8 + step * 2 + ((pick_row >> 6) & 1)
+        spread = jnp.dot(one_hot(pick_lane == source), asked, preferred_element_type=f32)
         block = jnp.dot(
             jnp.where(next_at, spread, 0.0).astype(bf16), ones, preferred_element_type=f32
         )
         key = jnp.dot(
             jnp.where(key_at, spread, 0.0).astype(bf16), weights, preferred_element_type=f32
         )
+        blocks[step * 512 : (step + 1) * 512, :] = block
+        keys[step * 512 : (step + 1) * 512, :] = key
+    for step in range(4):
+        rows = slice(step * 512, (step + 1) * 512)
+        block, key = blocks[rows, :], keys[rows, :]
+        second = key >= 2048.0
+        key = jnp.where(second, key - 2048.0, key)
+        key = jnp.where(key >= 768.0, key - 768.0, key)
+        hit = block == lane_f
+        next_rows[rows, :LANES] = one_hot(hit & ~second)
+        next_rows[rows, LANES:] = one_hot(hit & second)
+        for n in range(6):
+            word_rows[rows, n * LANES : (n + 1) * LANES] = one_hot(key == lane_f + float(n * LANES))
+    for step in range(4):
+        rows = slice(step * 512, (step + 1) * 512)
+        got = jnp.dot(word_rows[rows, :], emits[...], preferred_element_type=f32)
+        panels = jnp.dot(next_rows[rows, :], table[...], preferred_element_type=f32)
+        block, key = blocks[rows, :], keys[rows, :]
+        second = key >= 2048.0
+        late = jnp.where(second, key - 2048.0, key) >= 768.0
+        emit = jnp.where(late, got[:, LANES:], got[:, :LANES])
+        emit = jnp.where((lane_f < float(KW)) ^ second, emit, pltpu.roll(emit, KW, 1))
+        last = block == float(LANES)
+        for pair in range(4):
+            column = (pair * 2 + (lane >> 6)) * 8 + share
+            panel = panels[:, pair * LANES : (pair + 1) * LANES]
+            panel = jnp.where(last & (row_of == column), 1.0, panel) * emit
+            for n in range(SLOTS):
+                stage[pl.ds(step * 2048 + n * 512 + pair, LANES, stride=4), :] = panel[
+                    n * LANES : (n + 1) * LANES, :
+                ]
         for n in range(SLOTS):
-            rows = slice(n * LANES + part * 64, n * LANES + part * 64 + 64)
-            blocks[rows, :] = block[n * 64 : n * 64 + 64, :]
-            keys[rows, :] = key[n * 64 : n * 64 + 64, :]
-    lane_f = iota((512, LANES), 1).astype(f32)
-    block, key = blocks[...], keys[...]
-    second = key >= 2048.0
-    key = jnp.where(second, key - 2048.0, key)
-    late = key >= 768.0
-    key = jnp.where(late, key - 768.0, key)
-    hit = block == lane_f
-    next_rows[:, :LANES] = one_hot(hit & ~second)
-    next_rows[:, LANES:] = one_hot(hit & second)
-    for n in range(6):
-        word_rows[:, n * LANES : (n + 1) * LANES] = one_hot(key == lane_f + float(n * LANES))
-    got = jnp.dot(word_rows[...], emits[...], preferred_element_type=f32)
-    emit = jnp.where(late, got[:, LANES:], got[:, :LANES])
-    emit = jnp.where((lane_f < float(KW)) ^ second, emit, pltpu.roll(emit, KW, 1))
-    panels = jnp.dot(next_rows[...], table[...], preferred_element_type=f32)
-    last = block == float(LANES)
-    row_of = iota((512, LANES), 1) & (KW - 1)
-    for pair in range(4):
-        column = (pair * 2 + (iota((512, LANES), 1) >> 6)) * 8 + share
-        panel = panels[:, pair * LANES : (pair + 1) * LANES]
-        panel = jnp.where(last & (row_of == column), 1.0, panel) * emit
-        for n in range(SLOTS):
-            stage[pl.ds(n * 512 + pair, LANES, stride=4), :] = panel[n * LANES : (n + 1) * LANES, :]
-    for n in range(SLOTS):
-        block = stage[n * 512 : (n + 1) * 512, :].reshape(LANES, 4, LANES).astype(bf16)
-        if n < SENT:
-            panel_ref[:, :, n * LANES : (n + 1) * LANES] = block
-        else:
-            spare_ref[...] = block
+            block = stage[step * 2048 + n * 512 : step * 2048 + (n + 1) * 512, :]
+            block = block.reshape(LANES, 4, LANES).astype(bf16)
+            if n < SENT:
+                panel_ref[step * LANES : (step + 1) * LANES, :, n * LANES : (n + 1) * LANES] = block
+            else:
+                spare_ref[step * LANES : (step + 1) * LANES, :, :] = block
+        some = pl.ds(step * LANES, LANES)
+        for n, (ref, hbm) in enumerate(((panel_ref, panel_hbm), (spare_ref, spare_hbm))):
+            copies.append(pltpu.make_async_copy(ref.at[some], hbm.at[some], sems.at[step * 2 + n]))
+            copies[-1].start()
+    for copy in copies:
+        copy.wait()
 
 
 def pick(exps, everything):
     vmem = pl.BlockSpec(memory_space=pltpu.VMEM)
-    small = pl.BlockSpec((8, LANES), lambda i: (0, 0))
     return pl.pallas_call(
         pick_kernel,
-        grid=(4,),
         out_shape=(
             jax.ShapeDtypeStruct((512, 4, SENT * LANES), bf16),
             jax.ShapeDtypeStruct((512, 4, LANES), bf16),
@@ -356,23 +385,20 @@
             jax.ShapeDtypeStruct((8, LANES), f32),
         ),
         in_specs=[vmem] * 2,
-        out_specs=(
-            pl.BlockSpec((LANES, 4, SENT * LANES), lambda i: (i, 0, 0)),
-            pl.BlockSpec((LANES, 4, LANES), lambda i: (i, 0, 0)),
-            small,
-            small,
-            small,
-        ),
+        out_specs=(pl.BlockSpec(memory_space=pl.ANY),) * 2 + (vmem,) * 3,
         scratch_shapes=[
             pltpu.VMEM((256, 512), bf16),
             pltpu.VMEM((768, 256), bf16),
-            pltpu.VMEM((512, 256), bf16),
-            pltpu.VMEM((512, 768), bf16),
-            pltpu.VMEM((512, LANES), f32),
-            pltpu.VMEM((512, LANES), f32),
+            pltpu.VMEM((2048, 256), bf16),
+            pltpu.VMEM((2048, 768), bf16),
             pltpu.VMEM((2048, LANES), f32),
+            pltpu.VMEM((2048, LANES), f32),
+            pltpu.VMEM((8192, LANES), f32),
+            pltpu.VMEM((512, 4, SENT * LANES), bf16),
+            pltpu.VMEM((512, 4, LANES), bf16),
+            pltpu.SemaphoreType.DMA((8,)),
         ],
-        compiler_params=pltpu.CompilerParams(vmem_limit_bytes=60 * 1024 * 1024),
+        compiler_params=pltpu.CompilerParams(vmem_limit_bytes=PICK_VMEM),
         name="pick",
     )(exps, everything)
 
@@ -466,7 +492,13 @@
     )
     arrived = lax.all_to_all(msg, "state", split_axis=0, concat_axis=0, tiled=True)
     exps, mine = score(arrived, mat)
-    everything = lax.all_gather(mine, "seq", axis=0, tiled=False)
+    along_x = lax.all_to_all(
+        mine, "seq", split_axis=0, concat_axis=0, tiled=True,
+        axis_index_groups=[[0, 2, 4, 6], [1, 3, 5, 7]],
+    )
+    everything = lax.all_gather(
+        along_x, "seq", axis=0, tiled=True, axis_index_groups=[[0, 1], [2, 3], [4, 5], [6, 7]]
+    )
     panels, spare, trans_norm, emit_norm, full = pick(exps, everything)
 
     def exchange(value):

time: 154 us -> 151 us (0.981)
  blocking collectives: 74.2 us -> 71.9 us
    all_gather x1, blocking collectives: 17.9 us -> 6.53 us  [local(): lax.all_gather(along_x, 'seq', axis=0, tiled=True, axis_index_groups=[[0,...]
    all_to_all x0 -> x1, blocking collectives: none -> 9.06 us  [local(): lax.all_to_all(mine, 'seq', split_axis=0, concat_axis=0, tiled=True, axis...]
where the time goes in v4:
time: 151 us
  blocking collectives  71.9 us (48%)
  waiting for transfers between devices  41.8 us (28%)
  Pallas kernels  22.1 us (15%)
  starting transfers between devices  10.2 us (7%)
  local copies, waits for them, and re-layouts  3.72 us (2%)
    all_to_all x1, blocking collectives, local(): lax.all_to_all(msg, 'state', split_axis=0, concat_axis=0, tiled=True)  56.3 us
    all_to_all x1, waiting for transfers between devices, exchange(): lax.all_to_all(value, ('state', 'seq'), split_axis=0, concat_axis=0, tile...  41.8 us
    all_to_all x1, starting transfers between devices, exchange(): lax.all_to_all(value, ('state', 'seq'), split_axis=0, concat_axis=0, tile...  10.2 us
    all_to_all x1, blocking collectives, local(): lax.all_to_all(mine, 'seq', split_axis=0, concat_axis=0, tiled=True, axis...  9.06 us
    pallas_call x1, Pallas kernels, pick(): pl.pallas_call(pick_kernel, out_shape=(jax.ShapeDtypeStruct((512, 4, SENT...  8.18 us
    pallas_call x1, Pallas kernels, prep(): pl.pallas_call(prep_kernel, out_shape=(jax.ShapeDtypeStruct((SHARDS, ROWS...  6.87 us
    all_gather x1, blocking collectives, local(): lax.all_gather(along_x, 'seq', axis=0, tiled=True, axis_index_groups=[[0,...  6.53 us
    pallas_call x1, Pallas kernels, chain(): pl.pallas_call(chain_kernel, out_shape=jax.ShapeDtypeStruct((8, LANES), f...  6.13 us
  transfers between devices with their start and end apart: 1, of which 1 were waited for; matrix products, arithmetic and copies ran while one was open for 1% of the time, Pallas kernels for 0%

profile of v4, /device:TPU:1, one launch (start us, length us, event | category | flops | bytes accessed | tf_op | source)
XLA Modules:
  0.0 151.1 jit_solution(18367999835609932740)
XLA Ops:
  0.6 6.9 %prep.1 = (bf16[64,24,512]{2,1,0:T(8,128)(2,1)}, bf16[256,512]{1,0:T(8,128)(2,1)}, s32[1,128]{1,0:T(1,128)}) custom-call(s32[2,128]{1,0:T(2,128)} %bitcast.10, s32[1,128]{1,0:T(1,128)} %tokens_hbm.1, s32[1,128]{1,0:T(1,128)} %tokens_hbm.1, s32[1024,128]{1,0:T(8,128)} %bitcast.9, s32[1,128]{1,0:T(1,128)} %bitcast.11, bf16[512,512]{1,0:T(8,128)(2,1)} %emit_hbm.1, ...), custom_call_target="tpu_custom_call" | custom-call | tf_op jit(solution)/shard_map/prep/pallas_call | solution.py:175
  7.5 0.0 copy-start.1
  7.5 56.3 %all_to_all.20.msg_ref = bf16[64,24,512]{2,1,0:T(8,128)(2,1)S(1)} all-to-all(bf16[64,24,512]{2,1,0:T(8,128)(2,1)} %get-tuple-element.19), channel_id=1, replica_groups=mesh['state'=64,'seq'=8] {'state'}, dimensions={0} | all-to-all | bytes 3145728 | tf_op jit(solution)/shard_map/all_to_all | solution.py:493
  63.8 0.0 copy-done.1
  63.8 0.9 score.1
  64.7 0.0 copy-start
  64.7 0.8 copy-done
  65.5 9.1 %all_to_all.21 = bf16[4,208,128]{2,1,0:T(8,128)(2,1)S(1)} all-to-all(bf16[4,208,128]{2,1,0:T(8,128)(2,1)S(1)} %get-tuple-element.22), channel_id=1, replica_groups={{0,2,4,6},{1,3,5,7},{8,10,12,14},{9,11,13,15},{16,18,20,22},{17,19,21,2..., dimensions={0} | all-to-all | bytes 425984 | tf_op jit(solution)/shard_map/all_to_all | solution.py:495
  74.5 6.5 %all_gather.3.all_ref = bf16[8,208,128]{2,1,0:T(8,128)(2,1)} all-gather(bf16[4,208,128]{2,1,0:T(8,128)(2,1)S(1)} %all_to_all.21), channel_id=1, replica_groups={{0,1},{2,3},{4,5},{6,7},{8,9},{10,11},{12,13},{14,15},{16,17},{18,19},{..., dimensions={0}, use_global_device_ids=true | all-gather | bytes 638976 | tf_op jit(solution)/shard_map/all_gather | solution.py:499
  81.1 8.2 %pick.1 = (bf16[512,4,384]{2,1,0:T(4,128)(2,1)}, bf16[512,4,128]{2,1,0:T(4,128)(2,1)S(1)}, f32[8,128]{1,0:T(8,128)}, f32[8,128]{1,0:T(8,128)}, f32[8,128]{1,0:T(8,128)}) custom-call(f32[1024,128]{1,0:T(8,128)} %copy-done, bf16[8,208,128]{2,1,0:T(8,128)(2,1)} %all_gather.3.all_ref), custom_call_target="tpu_custom_call" | custom-call | tf_op jit(solution)/shard_map/pick/pallas_call | solution.py:378
  89.3 1.2 slice.12
  91.1 0.0 copy-start.2
  91.1 10.2 %all-to-all-start.3 = ((bf16[512,4,384]{2,1,0:T(4,128)(2,1)}), bf16[512,4,384]{2,1,0:T(4,128)(2,1)S(1)}, u32[]{:S(2)}, u32[]{:S(2)}) async-start(bf16[512,4,384]{2,1,0:T(4,128)(2,1)} %get-tuple-element.23), calls=%async_computation.3 | async-start | bytes 3145728 | tf_op jit(solution)/shard_map/all_to_all | solution.py:505
  101.4 1.2 slice_bitcast_fusion
  102.6 41.8 %all-to-all-done.3.panel_ref = bf16[512,4,384]{2,1,0:T(4,128)(2,1)S(1)} async-done(((bf16[512,4,384]{2,1,0:T(4,128)(2,1)}), bf16[512,4,384]{2,1,0:T(4,128)(2,1)S(1)}, u32[]{:S(2)}, u32[]{:S(2)}) %all-to-all-start.3) | async-done | bytes 1572896 | tf_op jit(solution)/shard_map/all_to_all | solution.py:505
  144.4 0.0 copy-done.2
  144.4 6.1 %chain.1 = f32[8,128]{1,0:T(8,128)S(1)} custom-call(s32[1,128]{1,0:T(1,128)S(1)} %copy-done.2, bf16[512,4,384]{2,1,0:T(4,128)(2,1)S(1)} %all-to-all-done.3.panel_ref, bf16[512,4,128]{2,1,0:T(4,128)(2,1)S(1)} %get-tuple-element.30.spare_ref), custom_call_target="tpu_custom_call" | custom-call | tf_op jit(solution)/shard_map/chain/pallas_call | solution.py:470
  150.5 0.5 slice.13
  (1 shorter events, 0.0 us)
Async XLA Ops:
  7.5 56.3 %copy-start.1 = (bf16[256,512]{1,0:T(8,128)(2,1)S(1)}, bf16[256,512]{1,0:T(8,128)(2,1)}, u32[]{:S(2)}) copy-start(bf16[256,512]{1,0:T(8,128)(2,1)} %get-tuple-element.20.mat_ref) | copy-start | bytes 786436
  64.7 0.8 copy-start
  91.1 53.3 %copy-start.2 = (s32[1,128]{1,0:T(1,128)S(1)}, s32[1,128]{1,0:T(1,128)}, u32[]{:S(2)}) copy-start(s32[1,128]{1,0:T(1,128)} %get-tuple-element.18.slot_ref) | copy-start | bytes 1540
  91.1 53.2 %all-to-all-start.3 = ((bf16[512,4,384]{2,1,0:T(4,128)(2,1)}), bf16[512,4,384]{2,1,0:T(4,128)(2,1)S(1)}, u32[]{:S(2)}, u32[]{:S(2)}) async-start(bf16[512,4,384]{2,1,0:T(4,128)(2,1)} %get-tuple-element.23), calls=%async_computation.3 | async-start | bytes 3145728 | tf_op jit(solution)/shard_map/all_to_all | solution.py:505

commit v5 on v4

--- a/solution.py
+++ b/solution.py
@@ -11,7 +11,6 @@
 LANES = 128
 RANKS = 3
 SHARDS = 64
-PICK_VMEM = 60 * 1024 * 1024 + 512 * 1024
 SLOTS = 4
 SENT = 3
 ROWS = 24
@@ -94,28 +93,18 @@
 
     length = token_ref.shape[1]
 
-    def pull(i, _):
-        for u in range(8):
-            t = i * 8 + u
-            near[pl.ds(t, 1), :] = cluster_ref[pl.ds(token_ref[0, t] >> 7, 1), :]
-        return 0
-
-    lax.fori_loop(0, length // 8, pull, 0)
+    for t in range(length):
+        near[t : t + 1, :] = cluster_ref[pl.ds(token_ref[0, t] >> 7, 1), :]
     token_col = column(tokens_ref[...])
     cluster_col = jnp.sum(ints(lane == (token_col & 127), near[...]), axis=1, keepdims=True)
     near[...] = jnp.broadcast_to(cluster_col, (LANES, LANES))
     place = iota((chunks, LANES), 0) * LANES + iota((chunks, LANES), 1)
 
-    def tally(i, _):
-        for u in range(8):
-            t = i * 8 + u
-            token = token_ref[0, t]
-            shard_rows = cluster_ref[pl.ds(pl.multiple_of((token >> 11) * chunks, chunks), chunks), :]
-            earlier = (shard_rows == near[pl.ds(t, 1), :]) & (place < (token & 2047))
-            wide[pl.ds(t, 1), :] = jnp.sum(ints(earlier, 1), axis=0, keepdims=True)
-        return 0
-
-    lax.fori_loop(0, length // 8, tally, 0)
+    for t in range(length):
+        token = token_ref[0, t]
+        shard_rows = cluster_ref[pl.ds(pl.multiple_of((token >> 11) * chunks, chunks), chunks), :]
+        earlier = (shard_rows == near[t : t + 1, :]) & (place < (token & 2047))
+        wide[t : t + 1, :] = jnp.sum(ints(earlier, 1), axis=0, keepdims=True)
     rank_col = jnp.sum(wide[...], axis=1, keepdims=True)
     own_block_col = jnp.sum(ints(lane == cluster_col, block_row), axis=1, keepdims=True)
     own_block_row = line(own_block_col)
@@ -269,42 +258,41 @@
 
 
 def pick_kernel(
-    exps_ref, all_ref, panel_hbm, spare_hbm, trans_ref, emit_ref, full_ref,
-    table, emits, next_rows, word_rows, blocks, keys, stage, panel_ref, spare_ref, sems,
+    exps_ref, all_ref, panel_ref, spare_ref, trans_ref, emit_ref, full_ref,
+    table, emits, next_rows, word_rows, blocks, keys, stage,
 ):
     share = lax.axis_index("seq")
     order = [(g & 1) * 4 + (g >> 1) for g in range(8)]
-    if True:
-        sums = [all_ref[n, 200:208, :].astype(f32) for n in order]
-        total = jnp.zeros((1, LANES), f32)
-        top = sums[0][0:1, :]
-        full = jnp.zeros((8, LANES), f32)
-        for g in range(8):
-            total = total + (sums[g][4:5, :] + sums[g][5:6, :] + sums[g][6:7, :])
-            top = jnp.maximum(top, sums[g][0:1, :])
-            full = jnp.maximum(full, all_ref[order[g], 192:200, :].astype(f32))
-        mass = jnp.zeros((1, LANES), f32)
-        for g in range(8):
-            part = sums[g][1:2, :] + sums[g][2:3, :] + sums[g][3:4, :]
-            mass = mass + part * jnp.exp(sums[g][0:1, :] - top)
-        full = jnp.where((iota((8, LANES), 1) & 15) == 14, full, 0.0)
-        full = jnp.max(jnp.max(full, axis=0, keepdims=True), axis=1, keepdims=True)
-        full_ref[...] = jnp.broadcast_to(full, (8, LANES))
-        trans_ref[...] = jnp.broadcast_to(jnp.log(total), (8, LANES))
-        emit_norm = top + jnp.log(mass)
-        emit_ref[...] = jnp.broadcast_to(emit_norm, (8, LANES))
-        for g in range(8):
-            rows = slice((g & 3) * 192, (g & 3) * 192 + 192)
-            lanes = slice((g >> 2) * LANES, (g >> 2) * LANES + LANES)
-            scale = jnp.exp(sums[g][0:1, :] - emit_norm)
-            emits[rows, lanes] = (all_ref[order[g], 0:192, :].astype(f32) * scale).astype(bf16)
-        low = iota((LANES, LANES), 1) < KW
-        for pair in range(4):
-            first = exps_ref[pl.ds(2 * pair, LANES, stride=8), :] / total
-            second = exps_ref[pl.ds(2 * pair + 1, LANES, stride=8), :] / total
-            lanes = slice(pair * LANES, (pair + 1) * LANES)
-            table[0:LANES, lanes] = jnp.where(low, first, pltpu.roll(second, KW, 1)).astype(bf16)
-            table[LANES:, lanes] = jnp.where(low, pltpu.roll(first, KW, 1), second).astype(bf16)
+    sums = [all_ref[n, 200:208, :].astype(f32) for n in order]
+    total = jnp.zeros((1, LANES), f32)
+    top = sums[0][0:1, :]
+    full = jnp.zeros((8, LANES), f32)
+    for g in range(8):
+        total = total + (sums[g][4:5, :] + sums[g][5:6, :] + sums[g][6:7, :])
+        top = jnp.maximum(top, sums[g][0:1, :])
+        full = jnp.maximum(full, all_ref[order[g], 192:200, :].astype(f32))
+    mass = jnp.zeros((1, LANES), f32)
+    for g in range(8):
+        part = sums[g][1:2, :] + sums[g][2:3, :] + sums[g][3:4, :]
+        mass = mass + part * jnp.exp(sums[g][0:1, :] - top)
+    full = jnp.where((iota((8, LANES), 1) & 15) == 14, full, 0.0)
+    full = jnp.max(jnp.max(full, axis=0, keepdims=True), axis=1, keepdims=True)
+    full_ref[...] = full.astype(i32)
+    trans_ref[...] = jnp.log(total)
+    emit_norm = top + jnp.log(mass)
+    emit_ref[...] = emit_norm
+    for g in range(8):
+        rows = slice((g & 3) * 192, (g & 3) * 192 + 192)
+        lanes = slice((g >> 2) * LANES, (g >> 2) * LANES + LANES)
+        scale = jnp.exp(sums[g][0:1, :] - emit_norm)
+        emits[rows, lanes] = (all_ref[order[g], 0:192, :].astype(f32) * scale).astype(bf16)
+    low = iota((LANES, LANES), 1) < KW
+    for pair in range(4):
+        first = exps_ref[pl.ds(2 * pair, LANES, stride=8), :] / total
+        second = exps_ref[pl.ds(2 * pair + 1, LANES, stride=8), :] / total
+        lanes = slice(pair * LANES, (pair + 1) * LANES)
+        table[0:LANES, lanes] = jnp.where(low, first, pltpu.roll(second, KW, 1)).astype(bf16)
+        table[LANES:, lanes] = jnp.where(low, pltpu.roll(first, KW, 1), second).astype(bf16)
 
     row, lane = iota((512, LANES), 0), iota((512, LANES), 1)
     pick_row, pick_lane = iota((512, 64), 0), iota((512, 64), 1)
@@ -317,7 +305,6 @@
     asked = asked.astype(bf16)
     lane_f = lane.astype(f32)
     row_of = lane & (KW - 1)
-    copies = []
     for step in range(4):
         source = (pick_row & 7) * 8 + step * 2 + ((pick_row >> 6) & 1)
         spread = jnp.dot(one_hot(pick_lane == source), asked, preferred_element_type=f32)
@@ -365,12 +352,6 @@
                 panel_ref[step * LANES : (step + 1) * LANES, :, n * LANES : (n + 1) * LANES] = block
             else:
                 spare_ref[step * LANES : (step + 1) * LANES, :, :] = block
-        some = pl.ds(step * LANES, LANES)
-        for n, (ref, hbm) in enumerate(((panel_ref, panel_hbm), (spare_ref, spare_hbm))):
-            copies.append(pltpu.make_async_copy(ref.at[some], hbm.at[some], sems.at[step * 2 + n]))
-            copies[-1].start()
-    for copy in copies:
-        copy.wait()
 
 
 def pick(exps, everything):
@@ -380,12 +361,12 @@
         out_shape=(
             jax.ShapeDtypeStruct((512, 4, SENT * LANES), bf16),
             jax.ShapeDtypeStruct((512, 4, LANES), bf16),
-            jax.ShapeDtypeStruct((8, LANES), f32),
-            jax.ShapeDtypeStruct((8, LANES), f32),
-            jax.ShapeDtypeStruct((8, LANES), f32),
+            jax.ShapeDtypeStruct((1, LANES), f32),
+            jax.ShapeDtypeStruct((1, LANES), f32),
+            jax.ShapeDtypeStruct((1, 1), i32),
         ),
         in_specs=[vmem] * 2,
-        out_specs=(pl.BlockSpec(memory_space=pl.ANY),) * 2 + (vmem,) * 3,
+        out_specs=(vmem,) * 5,
         scratch_shapes=[
             pltpu.VMEM((256, 512), bf16),
             pltpu.VMEM((768, 256), bf16),
@@ -394,11 +375,8 @@
             pltpu.VMEM((2048, LANES), f32),
             pltpu.VMEM((2048, LANES), f32),
             pltpu.VMEM((8192, LANES), f32),
-            pltpu.VMEM((512, 4, SENT * LANES), bf16),
-            pltpu.VMEM((512, 4, LANES), bf16),
-            pltpu.SemaphoreType.DMA((8,)),
         ],
-        compiler_params=pltpu.CompilerParams(vmem_limit_bytes=PICK_VMEM),
+        compiler_params=pltpu.CompilerParams(vmem_limit_bytes=40 * 1024 * 1024),
         name="pick",
     )(exps, everything)
 
@@ -433,14 +411,14 @@
             ping[t] = jnp.concatenate(move, axis=0).astype(bf16)
         return 0
 
-    lax.fori_loop(0, length // 8, build, 0)
+    lax.fori_loop(0, length // 8, build, 0, unroll=2)
     peak = jnp.max(logs[0:length, :], axis=1, keepdims=True)
     tops[...] = jnp.broadcast_to((1.0 / peak).astype(bf16).astype(f32), (length, LANES))
     logs[0:length, :] = 1.0 / tops[...]
     logs[length:, :] = jnp.ones((length, LANES), f32)
     src, dst, count, base = ping, pong, length // 2, length
     while count > 1:
-        unroll = min(count, 16)
+        unroll = min(count, 32)
 
         def level(i, _, src=src, dst=dst, unroll=unroll, base=base, first=src is ping and base == length):
             for u in range(unroll):
@@ -461,7 +439,7 @@
     final = jnp.sum(jnp.sum(prod, axis=0, keepdims=True), axis=1, keepdims=True)
     scale = jnp.sum(jnp.log(logs[...]), axis=0, keepdims=True)
     total = jnp.log(final) + scale - jnp.log(jnp.full((1, LANES), 8192.0, f32))
-    out_ref[...] = jnp.broadcast_to(total / length, (8, LANES))
+    out_ref[...] = total[:, :1] / length
 
 
 def chain(slots, panels, spare):
@@ -469,7 +447,7 @@
     vmem = pl.BlockSpec(memory_space=pltpu.VMEM)
     return pl.pallas_call(
         chain_kernel,
-        out_shape=jax.ShapeDtypeStruct((8, LANES), f32),
+        out_shape=jax.ShapeDtypeStruct((1, 1), f32),
         in_specs=[pl.BlockSpec(memory_space=pltpu.SMEM), vmem, vmem],
         out_specs=vmem,
         scratch_shapes=[
@@ -505,9 +483,9 @@
         return lax.all_to_all(value, ("state", "seq"), split_axis=0, concat_axis=0, tiled=True)
 
     got = exchange(panels)
-    spare = lax.cond(full[0, 0] > 0.5, exchange, lambda value: value, spare)
+    spare = lax.cond(full.reshape(()) > 0, exchange, lambda value: value, spare)
     token_loglik = chain(slots, got, spare)
-    return (token_loglik[0, :1], trans_norm[0], emit_norm[0])
+    return (token_loglik.reshape(1), trans_norm.reshape(-1), emit_norm.reshape(-1))
 
 
 def solution(mesh):

time: 151 us -> 143 us (0.947)
  blocking collectives: 71.9 us -> 125 us
  waiting for transfers between devices: 41.8 us -> 0 us
  starting transfers between devices: 10.2 us -> 0 us
  Pallas kernels: 22.1 us -> 17.1 us
  local copies, waits for them, and re-layouts: 3.72 us -> 0.01 us
    all_to_all x0 -> x1, blocking collectives: none -> 53 us  [exchange(): lax.all_to_all(value, ('state', 'seq'), split_axis=0, concat_axis=0, tile...]
    all_to_all x1 -> x0, waiting for transfers between devices: 41.8 us -> none  [exchange(): lax.all_to_all(value, ('state', 'seq'), split_axis=0, concat_axis=0, tile...]
    all_to_all x1 -> x0, starting transfers between devices: 10.2 us -> none  [exchange(): lax.all_to_all(value, ('state', 'seq'), split_axis=0, concat_axis=0, tile...]
    pallas_call x1, Pallas kernels: 8.18 us -> 4.61 us  [pick(): pl.pallas_call(pick_kernel, out_shape=(jax.ShapeDtypeStruct((512, 4, SENT...]
    slice x2 -> x0, local copies, waits for them, and re-layouts: 1.72 us -> none  [the longest x1 1.2 us: local(): spare = lax.cond(full[0, 0] > 0.5, exchange, lambda value: value, spare)]
  transfers between devices with their start and end apart: 1 -> 0, of which waited for: 1 -> 0; matrix products, arithmetic and copies ran while one was open for 1% -> 0% of each run, Pallas kernels for 0% -> 0%
where the time goes in v5:
time: 143 us
  blocking collectives  125 us (87%)
  Pallas kernels  17.1 us (12%)
    all_to_all x1, blocking collectives, local(): lax.all_to_all(msg, 'state', split_axis=0, concat_axis=0, tiled=True)  56.3 us
    all_to_all x1, blocking collectives, exchange(): lax.all_to_all(value, ('state', 'seq'), split_axis=0, concat_axis=0, tile...  53 us
    all_to_all x1, blocking collectives, local(): lax.all_to_all(mine, 'seq', split_axis=0, concat_axis=0, tiled=True, axis...  9.08 us
    all_gather x1, blocking collectives, local(): lax.all_gather(along_x, 'seq', axis=0, tiled=True, axis_index_groups=[[0,...  6.4 us
    pallas_call x1, Pallas kernels, prep(): pl.pallas_call(prep_kernel, out_shape=(jax.ShapeDtypeStruct((SHARDS, ROWS...  6.25 us
    pallas_call x1, Pallas kernels, chain(): pl.pallas_call(chain_kernel, out_shape=jax.ShapeDtypeStruct((1, 1), f32),...  5.36 us
    pallas_call x1, Pallas kernels, pick(): pl.pallas_call(pick_kernel, out_shape=(jax.ShapeDtypeStruct((512, 4, SENT...  4.61 us

profile of v5, /device:TPU:1, one launch (start us, length us, event | category | flops | bytes accessed | tf_op | source)
XLA Modules:
  0.0 143.2 jit_solution(5062034398851131708)
XLA Ops:
  0.6 6.3 %prep.1 = (bf16[64,24,512]{2,1,0:T(8,128)(2,1)}, bf16[256,512]{1,0:T(8,128)(2,1)}, s32[1,128]{1,0:T(1,128)}) custom-call(s32[2,128]{1,0:T(2,128)} %bitcast.8, s32[1,128]{1,0:T(1,128)} %tokens_hbm.1, s32[1,128]{1,0:T(1,128)} %tokens_hbm.1, s32[1024,128]{1,0:T(8,128)} %bitcast.7, s32[1,128]{1,0:T(1,128)} %bitcast.9, bf16[512,512]{1,0:T(8,128)(2,1)} %emit_hbm.1, ...), custom_call_target="tpu_custom_call" | custom-call | tf_op jit(solution)/shard_map/prep/pallas_call | solution.py:164
  6.9 0.0 copy-start
  6.9 56.3 %all_to_all.20.msg_ref = bf16[64,24,512]{2,1,0:T(8,128)(2,1)S(1)} all-to-all(bf16[64,24,512]{2,1,0:T(8,128)(2,1)} %get-tuple-element.19), channel_id=1, replica_groups=mesh['state'=64,'seq'=8] {'state'}, dimensions={0} | all-to-all | bytes 3145728 | tf_op jit(solution)/shard_map/all_to_all | solution.py:471
  63.2 0.0 copy-done
  63.2 0.9 score.1
  64.1 9.1 %all_to_all.21 = bf16[4,208,128]{2,1,0:T(8,128)(2,1)S(1)} all-to-all(bf16[4,208,128]{2,1,0:T(8,128)(2,1)S(1)} %get-tuple-element.22), channel_id=1, replica_groups={{0,2,4,6},{1,3,5,7},{8,10,12,14},{9,11,13,15},{16,18,20,22},{17,19,21,2..., dimensions={0} | all-to-all | bytes 425984 | tf_op jit(solution)/shard_map/all_to_all | solution.py:473
  73.2 6.4 %all_gather.3.all_ref = bf16[8,208,128]{2,1,0:T(8,128)(2,1)S(1)} all-gather(bf16[4,208,128]{2,1,0:T(8,128)(2,1)S(1)} %all_to_all.21), channel_id=1, replica_groups={{0,1},{2,3},{4,5},{6,7},{8,9},{10,11},{12,13},{14,15},{16,17},{18,19},{..., dimensions={0}, use_global_device_ids=true | all-gather | bytes 638976 | tf_op jit(solution)/shard_map/all_gather | solution.py:477
  79.6 4.6 %pick.1 = (bf16[512,4,384]{2,1,0:T(4,128)(2,1)S(1)}, bf16[512,4,128]{2,1,0:T(4,128)(2,1)S(1)}, f32[1,128]{1,0:T(1,128)}, f32[1,128]{1,0:T(1,128)}, s32[1,1]{1,0:T(1,128)}) custom-call(f32[1024,128]{1,0:T(8,128)S(1)} %get-tuple-element.21.exps_ref, bf16[8,208,128]{2,1,0:T(8,128)(2,1)S(1)} %all_gather.3.all_ref), custom_call_target="tpu_custom_call" | custom-call | tf_op jit(solution)/shard_map/pick/pallas_call | solution.py:359
  84.8 0.0 copy-start.1
  84.8 53.0 %all_to_all.22.panel_ref = bf16[512,4,384]{2,1,0:T(4,128)(2,1)S(1)} all-to-all(bf16[512,4,384]{2,1,0:T(4,128)(2,1)S(1)} %get-tuple-element.23), channel_id=1, replica_groups=mesh['state'=64,'seq'=8] {'state','seq'}, dimensions={0} | all-to-all | bytes 3145728 | tf_op jit(solution)/shard_map/all_to_all | solution.py:483
  137.8 0.0 copy-done.1
  137.8 5.4 %chain.1 = f32[1,1]{1,0:T(1,128)} custom-call(s32[1,128]{1,0:T(1,128)S(1)} %copy-done.1, bf16[512,4,384]{2,1,0:T(4,128)(2,1)S(1)} %all_to_all.22.panel_ref, bf16[512,4,128]{2,1,0:T(4,128)(2,1)S(1)} %get-tuple-element.28.spare_ref), custom_call_target="tpu_custom_call" | custom-call | tf_op jit(solution)/shard_map/chain/pallas_call | solution.py:448
  (1 shorter events, 0.0 us)
Async XLA Ops:
  6.9 56.3 %copy-start = (bf16[256,512]{1,0:T(8,128)(2,1)S(1)}, bf16[256,512]{1,0:T(8,128)(2,1)}, u32[]{:S(2)}) copy-start(bf16[256,512]{1,0:T(8,128)(2,1)} %get-tuple-element.20.mat_ref) | copy-start | bytes 786436
  84.8 53.1 %copy-start.1 = (s32[1,128]{1,0:T(1,128)S(1)}, s32[1,128]{1,0:T(1,128)}, u32[]{:S(2)}) copy-start(s32[1,128]{1,0:T(1,128)} %get-tuple-element.18.slot_ref) | copy-start | bytes 1540

commit v6 on v5

--- a/solution.py
+++ b/solution.py
@@ -13,7 +13,8 @@
 SHARDS = 64
 SLOTS = 4
 SENT = 3
-ROWS = 24
+ROWS = 16
+SWAP = 528
 XROWS = 208
 f32 = jnp.float32
 bf16 = jnp.bfloat16
@@ -34,7 +35,7 @@
 
 def prep_kernel(
     parts_ref, token_ref, tokens_hbm, cluster_hbm, table_hbm, emit_hbm, out_hbm, in_hbm, word_hbm,
-    msg_ref, mat_ref, slot_ref,
+    msg_ref, out_kept, emit_kept, slot_ref,
     in_kept, slot_of, near, wide, counts_of, tokens_ref, cluster_ref, table_ref, word_ref, chosen, sems,
 ):
     me = lax.axis_index("state")
@@ -54,7 +55,7 @@
             src = pl.ds(pl.multiple_of(start, PART), PART)
             at = (blk * 2 + part) * PART
             for which, (hbm, ref, to) in enumerate(
-                ((in_hbm, in_kept, at), (out_hbm, mat_ref, at), (emit_hbm, mat_ref, 2 * KW + at))
+                ((in_hbm, in_kept, at), (out_hbm, out_kept, at), (emit_hbm, emit_kept, at))
             ):
                 sem = sems.at[4 + (blk * 2 + part) * 3 + which]
                 kept.append(pltpu.make_async_copy(hbm.at[src, :], ref.at[pl.ds(to, PART), :], sem))
@@ -136,12 +137,10 @@
     for copy in kept:
         copy.wait()
     row = iota((16, LANES), 0)
-    want = (row >> 3) * KW + (row & 7) * 8 + share
+    want = ((row >> 2) & 1) * KW + ((row >> 3) * 4 + (row & 3)) * 8 + share
     targets = jnp.dot(
         one_hot(iota((16, LANES), 1) == want), in_kept[...], preferred_element_type=f32
-    ).astype(bf16)
-    for to in range(SHARDS):
-        msg_ref[to, 0:16, :] = targets
+    )
     for tile in range(4):
         for c in range(chunks):
             chosen[tile * LANES : (tile + 1) * LANES, c * LANES : (c + 1) * LANES] = one_hot(
@@ -153,7 +152,9 @@
     for to in range(SHARDS):
         mine = words[to * 8 : to * 8 + 8, :]
         first = jnp.where(request_row, asked[to : to + 1, :], mine[:, :LANES])
-        msg_ref[to, 16:24, :] = jnp.concatenate([first, mine[:, LANES:]], axis=1).astype(bf16)
+        mine = jnp.concatenate([first, mine[:, LANES:]], axis=1)
+        head = targets[(to & 1) * 8 : (to & 1) * 8 + 8, :]
+        msg_ref[to] = jnp.concatenate([head, mine], axis=0).astype(bf16)
 
 
 def prep(kept_parts, tokens, word_cluster, cluster_block, emit_states, trans_out, trans_in, word_emb):
@@ -165,11 +166,12 @@
         prep_kernel,
         out_shape=(
             jax.ShapeDtypeStruct((SHARDS, ROWS, width), bf16),
-            jax.ShapeDtypeStruct((4 * KW, width), bf16),
+            jax.ShapeDtypeStruct((2 * KW, width), bf16),
+            jax.ShapeDtypeStruct((2 * KW, width), bf16),
             jax.ShapeDtypeStruct((1, LANES), i32),
         ),
         in_specs=[smem, smem] + [pl.BlockSpec(memory_space=pltpu.HBM)] * 7,
-        out_specs=(vmem, vmem, vmem),
+        out_specs=(vmem,) * 4,
         scratch_shapes=[
             pltpu.VMEM((2 * KW, width), bf16),
             pltpu.VMEM((16, LANES), i32),
@@ -197,21 +199,37 @@
     return [high, mid, value - high - mid]
 
 
-def score_kernel(msg_ref, mat_ref, exps_ref, out_ref, words, raw):
+def score_kernel(msg_ref, own_ref, other_ref, exps_ref, z_ref, swap_ref):
+    states = jnp.concatenate([own_ref[...], other_ref[...]], axis=0)
+    total = jnp.zeros((1, 2 * LANES), f32)
+    for tile in range(4):
+        got = msg_ref[tile * 16 : tile * 16 + 16].reshape(16 * ROWS, msg_ref.shape[2])
+        res = lax.dot_general(
+            got, states, (((1,), (1,)), ((), ())), preferred_element_type=f32
+        ).reshape(16, ROWS, 2 * LANES)
+        exps = jnp.exp(res[:, :8, :]).reshape(LANES, 2 * LANES)
+        total = total + jnp.sum(exps, axis=0, keepdims=True)
+        rows = slice(tile * LANES, (tile + 1) * LANES)
+        exps_ref[rows, :] = exps[:, :LANES]
+        swap_ref[rows, :] = jnp.minimum(exps[:, LANES:], 3.38e38).astype(bf16)
+    z_ref[...] = jnp.broadcast_to(total[:, :LANES], (8, LANES))
+    sums = thirds(total[:, LANES:]) + [jnp.zeros((13, LANES), f32)]
+    swap_ref[512:SWAP, :] = jnp.concatenate(sums, axis=0).astype(bf16)
+
+
+def words_kernel(msg_ref, emit_ref, z_ref, swap_ref, out_ref, words, raw):
     share = lax.axis_index("seq")
-    total = jnp.zeros((1, LANES), f32)
-    for tile in range(8):
-        got = msg_ref[tile * 8 : tile * 8 + 8].reshape(8 * ROWS, msg_ref.shape[2])
+    sums = swap_ref[512:SWAP, :].astype(f32)
+    total = z_ref[0:1, :] + (sums[0:1, :] + sums[1:2, :] + sums[2:3, :])
+    for tile in range(4):
+        got = msg_ref[tile * 16 : tile * 16 + 16].reshape(16 * ROWS, msg_ref.shape[2])
         res = lax.dot_general(
-            got, mat_ref[...], (((1,), (1,)), ((), ())), preferred_element_type=f32
-        ).reshape(8, ROWS, 2 * LANES)
-        exps = jnp.exp(res[:, :16, :LANES]).reshape(LANES, LANES)
-        exps_ref[tile * LANES : (tile + 1) * LANES, :] = exps
-        total = total + jnp.sum(exps, axis=0, keepdims=True)
-        words[tile * 64 : (tile + 1) * 64, :] = res[:, 16:, LANES:].reshape(64, LANES)
-        raw[tile * 64 : (tile + 1) * 64, :] = (
-            msg_ref[tile * 8 : tile * 8 + 8, 16:24, :LANES].astype(f32).reshape(64, LANES)
-        )
+            got, emit_ref[...], (((1,), (1,)), ((), ())), preferred_element_type=f32
+        ).reshape(16, ROWS, LANES)
+        rows = slice(tile * LANES, (tile + 1) * LANES)
+        words[rows, :] = res[:, 8:, :].reshape(LANES, LANES)
+        some = got[:, :LANES].astype(f32).reshape(16, ROWS, LANES)
+        raw[rows, :] = some[:, 8:, :].reshape(LANES, LANES)
     asked = raw[pl.ds(6, SHARDS, stride=8), :]
     spread = one_hot(iota((LANES, LANES), 0) == 12 + (iota((LANES, LANES), 1) >> 6))
     counts = jnp.dot(asked.astype(bf16), spread, preferred_element_type=f32)
@@ -241,25 +259,33 @@
         out_ref[copy] = message
 
 
-def score(msg, mat):
+def call(kernel, name, outs, scratch, *args):
     vmem = pl.BlockSpec(memory_space=pltpu.VMEM)
     return pl.pallas_call(
-        score_kernel,
-        out_shape=(
-            jax.ShapeDtypeStruct((1024, LANES), f32),
-            jax.ShapeDtypeStruct((4, XROWS, LANES), bf16),
-        ),
-        in_specs=[vmem] * 2,
-        out_specs=(vmem, vmem),
-        scratch_shapes=[pltpu.VMEM((512, LANES), f32), pltpu.VMEM((512, LANES), f32)],
+        kernel,
+        out_shape=tuple(jax.ShapeDtypeStruct(shape, kind) for shape, kind in outs),
+        in_specs=[vmem] * len(args),
+        out_specs=(vmem,) * len(outs),
+        scratch_shapes=[pltpu.VMEM(shape, kind) for shape, kind in scratch],
         compiler_params=pltpu.CompilerParams(vmem_limit_bytes=40 * 1024 * 1024),
-        name="score",
-    )(msg, mat)
+        name=name,
+    )(*args)
+
+
+def score(msg, own, other):
+    outs = [((512, LANES), f32), ((8, LANES), f32), ((SWAP, LANES), bf16)]
+    return call(score_kernel, "score", outs, [], msg, own, other)
+
+
+def words(msg, emit_kept, z_part, swapped):
+    outs = [((4, XROWS, LANES), bf16)]
+    scratch = [((512, LANES), f32)] * 2
+    return call(words_kernel, "words", outs, scratch, msg, emit_kept, z_part, swapped)[0]
 
 
 def pick_kernel(
-    exps_ref, all_ref, panel_ref, spare_ref, trans_ref, emit_ref, full_ref,
-    table, emits, next_rows, word_rows, blocks, keys, stage,
+    exps_ref, swap_ref, all_ref, panel_ref, spare_ref, trans_ref, emit_ref, full_ref,
+    halves, table, emits, next_rows, word_rows, blocks, keys, stage,
 ):
     share = lax.axis_index("seq")
     order = [(g & 1) * 4 + (g >> 1) for g in range(8)]
@@ -286,14 +312,17 @@
         lanes = slice((g >> 2) * LANES, (g >> 2) * LANES + LANES)
         scale = jnp.exp(sums[g][0:1, :] - emit_norm)
         emits[rows, lanes] = (all_ref[order[g], 0:192, :].astype(f32) * scale).astype(bf16)
+    odd = lax.axis_index("state") & 1
+    halves[pl.ds(pl.multiple_of(odd * 512, 512), 512), :] = exps_ref[...]
+    halves[pl.ds(pl.multiple_of((1 - odd) * 512, 512), 512), :] = swap_ref[0:512, :].astype(f32)
     low = iota((LANES, LANES), 1) < KW
     for pair in range(4):
-        first = exps_ref[pl.ds(2 * pair, LANES, stride=8), :] / total
-        second = exps_ref[pl.ds(2 * pair + 1, LANES, stride=8), :] / total
+        start = (pair >> 1) * 512 + (pair & 1) * 2
+        first = halves[pl.ds(start, LANES, stride=4), :] / total
+        second = halves[pl.ds(start + 1, LANES, stride=4), :] / total
         lanes = slice(pair * LANES, (pair + 1) * LANES)
         table[0:LANES, lanes] = jnp.where(low, first, pltpu.roll(second, KW, 1)).astype(bf16)
         table[LANES:, lanes] = jnp.where(low, pltpu.roll(first, KW, 1), second).astype(bf16)
-
     row, lane = iota((512, LANES), 0), iota((512, LANES), 1)
     pick_row, pick_lane = iota((512, 64), 0), iota((512, 64), 1)
     mine = ((lane >> 4) == ((row >> 3) & 7)) & ((lane & 3) == (row >> 7))
@@ -354,7 +383,7 @@
                 spare_ref[step * LANES : (step + 1) * LANES, :, :] = block
 
 
-def pick(exps, everything):
+def pick(exps, swapped, everything):
     vmem = pl.BlockSpec(memory_space=pltpu.VMEM)
     return pl.pallas_call(
         pick_kernel,
@@ -365,9 +394,10 @@
             jax.ShapeDtypeStruct((1, LANES), f32),
             jax.ShapeDtypeStruct((1, 1), i32),
         ),
-        in_specs=[vmem] * 2,
+        in_specs=[vmem] * 3,
         out_specs=(vmem,) * 5,
         scratch_shapes=[
+            pltpu.VMEM((1024, LANES), f32),
             pltpu.VMEM((256, 512), bf16),
             pltpu.VMEM((768, 256), bf16),
             pltpu.VMEM((2048, 256), bf16),
@@ -378,7 +408,7 @@
         ],
         compiler_params=pltpu.CompilerParams(vmem_limit_bytes=40 * 1024 * 1024),
         name="pick",
-    )(exps, everything)
+    )(exps, swapped, everything)
 
 
 def chain_kernel(slot_ref, panel_ref, spare_ref, out_ref, wide, ping, pong, logs, tops):
@@ -465,11 +495,15 @@
 def local(
     emit_states, trans_out, trans_in, word_emb, word_cluster, cluster_block, kept_parts, tokens
 ):
-    msg, mat, slots = prep(
+    msg, out_kept, emit_kept, slots = prep(
         kept_parts, tokens, word_cluster, cluster_block, emit_states, trans_out, trans_in, word_emb
     )
+    pairs = [(i, i ^ 1) for i in range(SHARDS)]
+    other = lax.ppermute(out_kept, "state", pairs)
     arrived = lax.all_to_all(msg, "state", split_axis=0, concat_axis=0, tiled=True)
-    exps, mine = score(arrived, mat)
+    exps, z_part, swap = score(arrived, out_kept, other)
+    swapped = lax.ppermute(swap, "state", pairs)
+    mine = words(arrived, emit_kept, z_part, swapped)
     along_x = lax.all_to_all(
         mine, "seq", split_axis=0, concat_axis=0, tiled=True,
         axis_index_groups=[[0, 2, 4, 6], [1, 3, 5, 7]],
@@ -477,7 +511,7 @@
     everything = lax.all_gather(
         along_x, "seq", axis=0, tiled=True, axis_index_groups=[[0, 1], [2, 3], [4, 5], [6, 7]]
     )
-    panels, spare, trans_norm, emit_norm, full = pick(exps, everything)
+    panels, spare, trans_norm, emit_norm, full = pick(exps, swapped, everything)
 
     def exchange(value):
         return lax.all_to_all(value, ("state", "seq"), split_axis=0, concat_axis=0, tiled=True)

time: 143 us -> 140 us (0.979)
  blocking collectives: 125 us -> 70.6 us
  waiting for transfers between devices: 0 us -> 26.9 us
  starting transfers between devices: 0 us -> 23.9 us
    all_to_all x1 -> x0, blocking collectives: 56.3 us -> none  [local(): lax.all_to_all(msg, 'state', split_axis=0, concat_axis=0, tiled=True)]
    ppermute x0 -> x2, waiting for transfers between devices: none -> 25.4 us  [the longest x1 23 us: local(): other = lax.ppermute(out_kept, 'state', pairs)]
    all_to_all x0 -> x1, starting transfers between devices: none -> 17.3 us  [local(): lax.all_to_all(msg, 'state', split_axis=0, concat_axis=0, tiled=True)]
    ppermute x0 -> x2, starting transfers between devices: none -> 6.61 us  [the longest x1 3.69 us: local(): swapped = lax.ppermute(swap, 'state', pairs)]
    all_to_all x0 -> x1, waiting for transfers between devices: none -> 1.43 us  [local(): lax.all_to_all(msg, 'state', split_axis=0, concat_axis=0, tiled=True)]
  transfers between devices with their start and end apart: 0 -> 3, of which waited for: 0 -> 3; matrix products, arithmetic and copies ran while one was open for 0% -> 0% of each run, Pallas kernels for 0% -> 0%
where the time goes in v6:
time: 140 us
  blocking collectives  70.6 us (50%)
  waiting for transfers between devices  26.9 us (19%)
  starting transfers between devices  23.9 us (17%)
  Pallas kernels  17 us (12%)
    all_to_all x1, blocking collectives, exchange(): lax.all_to_all(value, ('state', 'seq'), split_axis=0, concat_axis=0, tile...  53.9 us
    ppermute x1, waiting for transfers between devices, local(): other = lax.ppermute(out_kept, 'state', pairs)  23 us
    all_to_all x1, starting transfers between devices, local(): lax.all_to_all(msg, 'state', split_axis=0, concat_axis=0, tiled=True)  17.3 us
    all_to_all x1, blocking collectives, local(): lax.all_to_all(mine, 'seq', split_axis=0, concat_axis=0, tiled=True, axis...  9.1 us
    all_gather x1, blocking collectives, local(): lax.all_gather(along_x, 'seq', axis=0, tiled=True, axis_index_groups=[[0,...  7.58 us
    pallas_call x1, Pallas kernels, prep(): pl.pallas_call(prep_kernel, out_shape=(jax.ShapeDtypeStruct((SHARDS, ROWS...  6.01 us
    pallas_call x1, Pallas kernels, chain(): pl.pallas_call(chain_kernel, out_shape=jax.ShapeDtypeStruct((1, 1), f32),...  5.36 us
    pallas_call x1, Pallas kernels, pick(): pl.pallas_call(pick_kernel, out_shape=(jax.ShapeDtypeStruct((512, 4, SENT...  4.62 us
  transfers between devices with their start and end apart: 3, of which 3 were waited for; matrix products, arithmetic and copies ran while one was open for 0% of the time, Pallas kernels for 0%

profile of v6, /device:TPU:1, one launch (start us, length us, event | category | flops | bytes accessed | tf_op | source)
XLA Modules:
  0.0 139.7 jit_solution(4372137638465236202)
XLA Ops:
  0.6 6.0 %prep.1 = (bf16[64,16,512]{2,1,0:T(8,128)(2,1)}, bf16[128,512]{1,0:T(8,128)(2,1)}, bf16[128,512]{1,0:T(8,128)(2,1)}, s32[1,128]{1,0:T(1,128)}) custom-call(s32[2,128]{1,0:T(2,128)} %bitcast.8, s32[1,128]{1,0:T(1,128)} %tokens_hbm.1, s32[1,128]{1,0:T(1,128)} %tokens_hbm.1, s32[1024,128]{1,0:T(8,128)} %bitcast.7, s32[1,128]{1,0:T(1,128)} %bitcast.9, ...), custom_call_target="tpu_custom_call" | custom-call | tf_op jit(solution)/shard_map/prep/pallas_call | solution.py:165
  6.7 0.0 copy-start.1
  6.7 0.0 copy-start
  6.7 17.3 %all-to-all-start.1 = ((bf16[64,16,512]{2,1,0:T(8,128)(2,1)}), bf16[64,16,512]{2,1,0:T(8,128)(2,1)S(1)}, u32[]{:S(2)}, u32[]{:S(2)}) async-start(bf16[64,16,512]{2,1,0:T(8,128)(2,1)} %get-tuple-element.21), calls=%async_computation.1 | async-start | bytes 2097152 | tf_op jit(solution)/shard_map/all_to_all | solution.py:503
  24.0 0.0 copy-done.1
  24.0 2.9 %collective-permute-start = (bf16[128,512]{1,0:T(8,128)(2,1)S(1)}, bf16[128,512]{1,0:T(8,128)(2,1)S(1)}, u32[]{:S(2)}, u32[]{:S(2)}) collective-permute-start(bf16[128,512]{1,0:T(8,128)(2,1)S(1)} %copy-done.1), channel_id=1, source_target_pairs={{0,8},{8,0},{16,24},{24,16},{32,40},{40,32},{48,56},{56,48},{64,72... | collective-permute-start | bytes 393224 | tf_op jit(solution)/shard_map/ppermute | solution.py:502
  26.9 23.0 %collective-permute-done.other_ref = bf16[128,512]{1,0:T(8,128)(2,1)S(1)} collective-permute-done((bf16[128,512]{1,0:T(8,128)(2,1)S(1)}, bf16[128,512]{1,0:T(8,128)(2,1)S(1)}, u32[]{:S(2)}, u32[]{:S(2)}) %collective-permute-start) | collective-permute-done | bytes 131104 | tf_op jit(solution)/shard_map/ppermute | solution.py:502
  49.9 1.4 %all-to-all-done.1.msg_ref = bf16[64,16,512]{2,1,0:T(8,128)(2,1)S(1)} async-done(((bf16[64,16,512]{2,1,0:T(8,128)(2,1)}), bf16[64,16,512]{2,1,0:T(8,128)(2,1)S(1)}, u32[]{:S(2)}, u32[]{:S(2)}) %all-to-all-start.1) | async-done | bytes 1048608 | tf_op jit(solution)/shard_map/all_to_all | solution.py:503
  51.4 0.5 score.1
  51.9 3.7 %collective-permute-start.1 = (bf16[528,128]{1,0:T(8,128)(2,1)S(1)}, bf16[528,128]{1,0:T(8,128)(2,1)S(1)}, u32[]{:S(2)}, u32[]{:S(2)}) collective-permute-start(bf16[528,128]{1,0:T(8,128)(2,1)S(1)} %get-tuple-element.24), channel_id=1, source_target_pairs={{0,8},{8,0},{16,24},{24,16},{32,40},{40,32},{48,56},{56,48},{64,72... | collective-permute-start | bytes 405512 | tf_op jit(solution)/shard_map/ppermute | solution.py:505
  55.6 2.4 %collective-permute-done.1.swap_ref = bf16[528,128]{1,0:T(8,128)(2,1)S(1)} collective-permute-done((bf16[528,128]{1,0:T(8,128)(2,1)S(1)}, bf16[528,128]{1,0:T(8,128)(2,1)S(1)}, u32[]{:S(2)}, u32[]{:S(2)}) %collective-permute-start.1) | collective-permute-done | bytes 135200 | tf_op jit(solution)/shard_map/ppermute | solution.py:505
  57.9 0.0 copy-done
  58.0 0.5 words.1
  58.5 9.1 %all_to_all.20 = bf16[4,208,128]{2,1,0:T(8,128)(2,1)S(1)} all-to-all(bf16[4,208,128]{2,1,0:T(8,128)(2,1)S(1)} %words.1), channel_id=1, replica_groups={{0,2,4,6},{1,3,5,7},{8,10,12,14},{9,11,13,15},{16,18,20,22},{17,19,21,2..., dimensions={0} | all-to-all | bytes 425984 | tf_op jit(solution)/shard_map/all_to_all | solution.py:507
  67.6 7.6 %all_gather.3.all_ref = bf16[8,208,128]{2,1,0:T(8,128)(2,1)S(1)} all-gather(bf16[4,208,128]{2,1,0:T(8,128)(2,1)S(1)} %all_to_all.20), channel_id=1, replica_groups={{0,1},{2,3},{4,5},{6,7},{8,9},{10,11},{12,13},{14,15},{16,17},{18,19},{..., dimensions={0}, use_global_device_ids=true | all-gather | bytes 638976 | tf_op jit(solution)/shard_map/all_gather | solution.py:511
  75.1 4.6 %pick.1 = (bf16[512,4,384]{2,1,0:T(4,128)(2,1)S(1)}, bf16[512,4,128]{2,1,0:T(4,128)(2,1)S(1)}, f32[1,128]{1,0:T(1,128)}, f32[1,128]{1,0:T(1,128)}, s32[1,1]{1,0:T(1,128)}) custom-call(f32[512,128]{1,0:T(8,128)S(1)} %get-tuple-element.23.exps_ref, bf16[528,128]{1,0:T(8,128)(2,1)S(1)} %collective-permute-done.1.swap_ref, ...), custom_call_target="tpu_custom_call" | custom-call | tf_op jit(solution)/shard_map/pick/pallas_call | solution.py:388
  80.4 0.0 copy-start.2
  80.4 53.9 %all_to_all.21.panel_ref = bf16[512,4,384]{2,1,0:T(4,128)(2,1)S(1)} all-to-all(bf16[512,4,384]{2,1,0:T(4,128)(2,1)S(1)} %get-tuple-element.27), channel_id=1, replica_groups=mesh['state'=64,'seq'=8] {'state','seq'}, dimensions={0} | all-to-all | bytes 3145728 | tf_op jit(solution)/shard_map/all_to_all | solution.py:517
  134.3 0.0 copy-done.2
  134.3 5.4 %chain.1 = f32[1,1]{1,0:T(1,128)} custom-call(s32[1,128]{1,0:T(1,128)S(1)} %copy-done.2, bf16[512,4,384]{2,1,0:T(4,128)(2,1)S(1)} %all_to_all.21.panel_ref, bf16[512,4,128]{2,1,0:T(4,128)(2,1)S(1)} %get-tuple-element.32.spare_ref), custom_call_target="tpu_custom_call" | custom-call | tf_op jit(solution)/shard_map/chain/pallas_call | solution.py:478
  (1 shorter events, 0.0 us)
Async XLA Ops:
  6.7 17.3 %copy-start.1 = (bf16[128,512]{1,0:T(8,128)(2,1)S(1)}, bf16[128,512]{1,0:T(8,128)(2,1)}, u32[]{:S(2)}) copy-start(bf16[128,512]{1,0:T(8,128)(2,1)} %get-tuple-element.22.own_ref) | copy-start | bytes 393220
  6.7 51.3 %copy-start = (bf16[128,512]{1,0:T(8,128)(2,1)S(1)}, bf16[128,512]{1,0:T(8,128)(2,1)}, u32[]{:S(2)}) copy-start(bf16[128,512]{1,0:T(8,128)(2,1)} %get-tuple-element.25.emit_ref) | copy-start | bytes 393220
  6.7 44.7 %all-to-all-start.1 = ((bf16[64,16,512]{2,1,0:T(8,128)(2,1)}), bf16[64,16,512]{2,1,0:T(8,128)(2,1)S(1)}, u32[]{:S(2)}, u32[]{:S(2)}) async-start(bf16[64,16,512]{2,1,0:T(8,128)(2,1)} %get-tuple-element.21), calls=%async_computation.1 | async-start | bytes 2097152 | tf_op jit(solution)/shard_map/all_to_all | solution.py:503
  24.0 26.0 %collective-permute-start = (bf16[128,512]{1,0:T(8,128)(2,1)S(1)}, bf16[128,512]{1,0:T(8,128)(2,1)S(1)}, u32[]{:S(2)}, u32[]{:S(2)}) collective-permute-start(bf16[128,512]{1,0:T(8,128)(2,1)S(1)} %copy-done.1), channel_id=1, source_target_pairs={{0,8},{8,0},{16,24},{24,16},{32,40},{40,32},{48,56},{56,48},{64,72... | collective-permute-start | bytes 393224 | tf_op jit(solution)/shard_map/ppermute | solution.py:502
  51.9 6.1 %collective-permute-start.1 = (bf16[528,128]{1,0:T(8,128)(2,1)S(1)}, bf16[528,128]{1,0:T(8,128)(2,1)S(1)}, u32[]{:S(2)}, u32[]{:S(2)}) collective-permute-start(bf16[528,128]{1,0:T(8,128)(2,1)S(1)} %get-tuple-element.24), channel_id=1, source_target_pairs={{0,8},{8,0},{16,24},{24,16},{32,40},{40,32},{48,56},{56,48},{64,72... | collective-permute-start | bytes 405512 | tf_op jit(solution)/shard_map/ppermute | solution.py:505
  80.4 53.9 %copy-start.2 = (s32[1,128]{1,0:T(1,128)S(1)}, s32[1,128]{1,0:T(1,128)}, u32[]{:S(2)}) copy-start(s32[1,128]{1,0:T(1,128)} %get-tuple-element.20.slot_ref) | copy-start | bytes 1540

commit v7 on v6

--- a/solution.py
+++ b/solution.py
@@ -14,7 +14,6 @@
 SLOTS = 4
 SENT = 3
 ROWS = 16
-SWAP = 528
 XROWS = 208
 f32 = jnp.float32
 bf16 = jnp.bfloat16
@@ -199,7 +198,7 @@
     return [high, mid, value - high - mid]
 
 
-def score_kernel(msg_ref, own_ref, other_ref, exps_ref, z_ref, swap_ref):
+def score_kernel(msg_ref, own_ref, other_ref, exps_ref, z_ref, z_swap_ref, swap_ref):
     states = jnp.concatenate([own_ref[...], other_ref[...]], axis=0)
     total = jnp.zeros((1, 2 * LANES), f32)
     for tile in range(4):
@@ -213,14 +212,12 @@
         exps_ref[rows, :] = exps[:, :LANES]
         swap_ref[rows, :] = jnp.minimum(exps[:, LANES:], 3.38e38).astype(bf16)
     z_ref[...] = jnp.broadcast_to(total[:, :LANES], (8, LANES))
-    sums = thirds(total[:, LANES:]) + [jnp.zeros((13, LANES), f32)]
-    swap_ref[512:SWAP, :] = jnp.concatenate(sums, axis=0).astype(bf16)
-
-
-def words_kernel(msg_ref, emit_ref, z_ref, swap_ref, out_ref, words, raw):
+    z_swap_ref[...] = jnp.broadcast_to(total[:, LANES:], (8, LANES))
+
+
+def words_kernel(msg_ref, emit_ref, z_ref, z_other_ref, out_ref, words, raw):
     share = lax.axis_index("seq")
-    sums = swap_ref[512:SWAP, :].astype(f32)
-    total = z_ref[0:1, :] + (sums[0:1, :] + sums[1:2, :] + sums[2:3, :])
+    total = z_ref[0:1, :] + z_other_ref[0:1, :]
     for tile in range(4):
         got = msg_ref[tile * 16 : tile * 16 + 16].reshape(16 * ROWS, msg_ref.shape[2])
         res = lax.dot_general(
@@ -273,14 +270,14 @@
 
 
 def score(msg, own, other):
-    outs = [((512, LANES), f32), ((8, LANES), f32), ((SWAP, LANES), bf16)]
+    outs = [((512, LANES), f32)] + [((8, LANES), f32)] * 2 + [((512, LANES), bf16)]
     return call(score_kernel, "score", outs, [], msg, own, other)
 
 
-def words(msg, emit_kept, z_part, swapped):
+def words(msg, emit_kept, z_part, z_other):
     outs = [((4, XROWS, LANES), bf16)]
     scratch = [((512, LANES), f32)] * 2
-    return call(words_kernel, "words", outs, scratch, msg, emit_kept, z_part, swapped)[0]
+    return call(words_kernel, "words", outs, scratch, msg, emit_kept, z_part, z_other)[0]
 
 
 def pick_kernel(
@@ -314,7 +311,7 @@
         emits[rows, lanes] = (all_ref[order[g], 0:192, :].astype(f32) * scale).astype(bf16)
     odd = lax.axis_index("state") & 1
     halves[pl.ds(pl.multiple_of(odd * 512, 512), 512), :] = exps_ref[...]
-    halves[pl.ds(pl.multiple_of((1 - odd) * 512, 512), 512), :] = swap_ref[0:512, :].astype(f32)
+    halves[pl.ds(pl.multiple_of((1 - odd) * 512, 512), 512), :] = swap_ref[...].astype(f32)
     low = iota((LANES, LANES), 1) < KW
     for pair in range(4):
         start = (pair >> 1) * 512 + (pair & 1) * 2
@@ -411,21 +408,29 @@
     )(exps, swapped, everything)
 
 
-def chain_kernel(slot_ref, panel_ref, spare_ref, out_ref, wide, ping, pong, logs, tops):
+def chain_kernel(slot_ref, full_ref, panel_ref, spare_ref, out_ref, wide, ping, pong, logs, tops):
     length = slot_ref.shape[1]
 
-    def widen(i, _):
-        some = pl.ds(pl.multiple_of(i * 32, 32), 32)
-        for n in range(SLOTS):
-            if n < SENT:
-                got = panel_ref[some, :, n * LANES : (n + 1) * LANES].astype(f32)
-            else:
-                got = spare_ref[some, :, :].astype(f32)
-            rows = pl.ds(pl.multiple_of(n * 4096 + i * 256, 256), 256)
-            wide[rows, :] = jnp.concatenate([got, got], axis=1).reshape(256, LANES)
+    def widen(ref, lane, n, i):
+        got = ref[pl.ds(pl.multiple_of(i * 32, 32), 32), :, lane : lane + LANES].astype(f32)
+        rows = pl.ds(pl.multiple_of(n * 4096 + i * 256, 256), 256)
+        wide[rows, :] = jnp.concatenate([got, got], axis=1).reshape(256, LANES)
+
+    def widen_sent(i, _):
+        for n in range(SENT):
+            widen(panel_ref, n * LANES, n, i)
         return 0
 
-    lax.fori_loop(0, panel_ref.shape[0] // 32, widen, 0)
+    def widen_spare(i, _):
+        widen(spare_ref, 0, SENT, i)
+        return 0
+
+    lax.fori_loop(0, panel_ref.shape[0] // 32, widen_sent, 0)
+
+    @pl.when(full_ref[0, 0] > 0)
+    def _():
+        lax.fori_loop(0, panel_ref.shape[0] // 32, widen_spare, 0)
+
     low = iota((8, LANES), 1) < KW
 
     def build(i, _):
@@ -472,13 +477,14 @@
     out_ref[...] = total[:, :1] / length
 
 
-def chain(slots, panels, spare):
+def chain(slots, full, panels, spare):
     length = slots.shape[1]
     vmem = pl.BlockSpec(memory_space=pltpu.VMEM)
+    smem = pl.BlockSpec(memory_space=pltpu.SMEM)
     return pl.pallas_call(
         chain_kernel,
         out_shape=jax.ShapeDtypeStruct((1, 1), f32),
-        in_specs=[pl.BlockSpec(memory_space=pltpu.SMEM), vmem, vmem],
+        in_specs=[smem, smem, vmem, vmem],
         out_specs=vmem,
         scratch_shapes=[
             pltpu.VMEM((SLOTS * 4096, LANES), f32),
@@ -489,7 +495,7 @@
         ],
         compiler_params=pltpu.CompilerParams(vmem_limit_bytes=40 * 1024 * 1024),
         name="chain",
-    )(slots, panels, spare)
+    )(slots, full, panels, spare)
 
 
 def local(
@@ -501,9 +507,10 @@
     pairs = [(i, i ^ 1) for i in range(SHARDS)]
     other = lax.ppermute(out_kept, "state", pairs)
     arrived = lax.all_to_all(msg, "state", split_axis=0, concat_axis=0, tiled=True)
-    exps, z_part, swap = score(arrived, out_kept, other)
+    exps, z_part, z_swap, swap = score(arrived, out_kept, other)
+    z_other = lax.ppermute(z_swap, "state", pairs)
     swapped = lax.ppermute(swap, "state", pairs)
-    mine = words(arrived, emit_kept, z_part, swapped)
+    mine = words(arrived, emit_kept, z_part, z_other)
     along_x = lax.all_to_all(
         mine, "seq", split_axis=0, concat_axis=0, tiled=True,
         axis_index_groups=[[0, 2, 4, 6], [1, 3, 5, 7]],
@@ -518,7 +525,7 @@
 
     got = exchange(panels)
     spare = lax.cond(full.reshape(()) > 0, exchange, lambda value: value, spare)
-    token_loglik = chain(slots, got, spare)
+    token_loglik = chain(slots, full, got, spare)
     return (token_loglik.reshape(1), trans_norm.reshape(-1), emit_norm.reshape(-1))
 
 

time: 140 us -> 141 us (level)
  blocking collectives: 70.6 us -> 62.1 us
  starting transfers between devices: 23.9 us -> 31.3 us
    all_to_all x1 -> x0, blocking collectives: 9.1 us -> none  [local(): lax.all_to_all(mine, 'seq', split_axis=0, concat_axis=0, tiled=True, axis...]
    all_to_all x0 -> x1, starting transfers between devices: none -> 4.02 us  [local(): lax.all_to_all(mine, 'seq', split_axis=0, concat_axis=0, tiled=True, axis...]
    ppermute x0 -> x1, starting transfers between devices: none -> 3.71 us  [local(): z_other = lax.ppermute(z_swap, 'state', pairs)]
    ppermute x1, waiting for transfers between devices: 2.39 us -> 0.01 us  [local(): swapped = lax.ppermute(swap, 'state', pairs)]
    all_to_all x0 -> x1, waiting for transfers between devices: none -> 1.91 us  [local(): lax.all_to_all(mine, 'seq', split_axis=0, concat_axis=0, tiled=True, axis...]
  transfers between devices with their start and end apart: 3 -> 5, of which waited for: 3 -> 4; matrix products, arithmetic and copies ran while one was open for 0% -> 0% of each run, Pallas kernels for 0% -> 0%
where the time goes in v7:
time: 141 us; the launch traced here: 140 us
  blocking collectives  62.1 us (44%)
  starting transfers between devices  31.3 us (22%)
  waiting for transfers between devices  27.4 us (19%)
  Pallas kernels  18 us (13%)
    all_to_all x1, blocking collectives, exchange(): lax.all_to_all(value, ('state', 'seq'), split_axis=0, concat_axis=0, tile...  54.5 us
    ppermute x1, waiting for transfers between devices, local(): other = lax.ppermute(out_kept, 'state', pairs)  23 us
    all_to_all x1, starting transfers between devices, local(): lax.all_to_all(msg, 'state', split_axis=0, concat_axis=0, tiled=True)  17.3 us
    all_gather x1, blocking collectives, local(): lax.all_gather(along_x, 'seq', axis=0, tiled=True, axis_index_groups=[[0,...  7.6 us
    pallas_call x1, Pallas kernels, prep(): pl.pallas_call(prep_kernel, out_shape=(jax.ShapeDtypeStruct((SHARDS, ROWS...  6 us
    pallas_call x1, Pallas kernels, chain(): pl.pallas_call(chain_kernel, out_shape=jax.ShapeDtypeStruct((1, 1), f32),...  5.71 us
    pallas_call x1, Pallas kernels, pick(): pl.pallas_call(pick_kernel, out_shape=(jax.ShapeDtypeStruct((512, 4, SENT...  4.6 us
    all_to_all x1, starting transfers between devices, local(): lax.all_to_all(mine, 'seq', split_axis=0, concat_axis=0, tiled=True, axis...  4.02 us
  transfers between devices with their start and end apart: 5, of which 4 were waited for; matrix products, arithmetic and copies ran while one was open for 0% of the time, Pallas kernels for 0%

profile of v7, /device:TPU:1, one launch (start us, length us, event | category | flops | bytes accessed | tf_op | source)
XLA Modules:
  0.0 140.1 jit_solution(8517134027199066009)
XLA Ops:
  0.6 6.0 %prep.1 = (bf16[64,16,512]{2,1,0:T(8,128)(2,1)}, bf16[128,512]{1,0:T(8,128)(2,1)}, bf16[128,512]{1,0:T(8,128)(2,1)}, s32[1,128]{1,0:T(1,128)}) custom-call(s32[2,128]{1,0:T(2,128)} %bitcast.8, s32[1,128]{1,0:T(1,128)} %tokens_hbm.1, s32[1,128]{1,0:T(1,128)} %tokens_hbm.1, s32[1024,128]{1,0:T(8,128)} %bitcast.7, s32[1,128]{1,0:T(1,128)} %bitcast.9, ...), custom_call_target="tpu_custom_call" | custom-call | tf_op jit(solution)/shard_map/prep/pallas_call | solution.py:164
  6.6 0.0 copy-start
  6.7 0.0 copy-start.1
  6.7 17.3 %all-to-all-start.1 = ((bf16[64,16,512]{2,1,0:T(8,128)(2,1)}), bf16[64,16,512]{2,1,0:T(8,128)(2,1)S(1)}, u32[]{:S(2)}, u32[]{:S(2)}) async-start(bf16[64,16,512]{2,1,0:T(8,128)(2,1)} %get-tuple-element.22), calls=%async_computation.1 | async-start | bytes 2097152 | tf_op jit(solution)/shard_map/all_to_all | solution.py:509
  24.0 0.0 copy-done
  24.0 2.9 %collective-permute-start = (bf16[128,512]{1,0:T(8,128)(2,1)S(1)}, bf16[128,512]{1,0:T(8,128)(2,1)S(1)}, u32[]{:S(2)}, u32[]{:S(2)}) collective-permute-start(bf16[128,512]{1,0:T(8,128)(2,1)S(1)} %copy-done), channel_id=1, source_target_pairs={{0,8},{8,0},{16,24},{24,16},{32,40},{40,32},{48,56},{56,48},{64,72... | collective-permute-start | bytes 393224 | tf_op jit(solution)/shard_map/ppermute | solution.py:508
  26.9 23.0 %collective-permute-done.other_ref = bf16[128,512]{1,0:T(8,128)(2,1)S(1)} collective-permute-done((bf16[128,512]{1,0:T(8,128)(2,1)S(1)}, bf16[128,512]{1,0:T(8,128)(2,1)S(1)}, u32[]{:S(2)}, u32[]{:S(2)}) %collective-permute-start) | collective-permute-done | bytes 131104 | tf_op jit(solution)/shard_map/ppermute | solution.py:508
  49.9 1.4 %all-to-all-done.1.msg_ref = bf16[64,16,512]{2,1,0:T(8,128)(2,1)S(1)} async-done(((bf16[64,16,512]{2,1,0:T(8,128)(2,1)}), bf16[64,16,512]{2,1,0:T(8,128)(2,1)S(1)}, u32[]{:S(2)}, u32[]{:S(2)}) %all-to-all-start.1) | async-done | bytes 1048608 | tf_op jit(solution)/shard_map/all_to_all | solution.py:509
  51.4 0.5 score.1
  51.8 3.7 %collective-permute-start.2 = (f32[8,128]{1,0:T(8,128)S(1)}, f32[8,128]{1,0:T(8,128)S(1)}, u32[]{:S(2)}, u32[]{:S(2)}) collective-permute-start(f32[8,128]{1,0:T(8,128)S(1)} %get-tuple-element.28), channel_id=1, source_target_pairs={{0,8},{8,0},{16,24},{24,16},{32,40},{40,32},{48,56},{56,48},{64,72... | collective-permute-start | bytes 12296 | tf_op jit(solution)/shard_map/ppermute | solution.py:511
  55.6 1.0 collective-permute-done.2.z_other_ref
  56.5 0.0 copy-done.1
  56.5 1.2 words.1
  57.8 4.0 %all-to-all-start.2 = ((bf16[4,208,128]{2,1,0:T(8,128)(2,1)}), bf16[4,208,128]{2,1,0:T(8,128)(2,1)S(1)}, u32[]{:S(2)}, u32[]{:S(2)}) async-start(bf16[4,208,128]{2,1,0:T(8,128)(2,1)} %words.1), calls=%async_computation.2 | async-start | bytes 425984 | tf_op jit(solution)/shard_map/all_to_all | solution.py:514
  61.8 3.3 %collective-permute-start.1 = (bf16[512,128]{1,0:T(8,128)(2,1)S(1)}, bf16[512,128]{1,0:T(8,128)(2,1)S(1)}, u32[]{:S(2)}, u32[]{:S(2)}) collective-permute-start(bf16[512,128]{1,0:T(8,128)(2,1)S(1)} %get-tuple-element.25), channel_id=1, source_target_pairs={{0,8},{8,0},{16,24},{24,16},{32,40},{40,32},{48,56},{56,48},{64,72... | collective-permute-start | bytes 393224 | tf_op jit(solution)/shard_map/ppermute | solution.py:512
  65.1 1.9 %all-to-all-done.2 = bf16[4,208,128]{2,1,0:T(8,128)(2,1)S(1)} async-done(((bf16[4,208,128]{2,1,0:T(8,128)(2,1)}), bf16[4,208,128]{2,1,0:T(8,128)(2,1)S(1)}, u32[]{:S(2)}, u32[]{:S(2)}) %all-to-all-start.2) | async-done | bytes 213024 | tf_op jit(solution)/shard_map/all_to_all | solution.py:514
  67.0 7.6 %all_gather.3.all_ref = bf16[8,208,128]{2,1,0:T(8,128)(2,1)S(1)} all-gather(bf16[4,208,128]{2,1,0:T(8,128)(2,1)S(1)} %all-to-all-done.2), channel_id=1, replica_groups={{0,1},{2,3},{4,5},{6,7},{8,9},{10,11},{12,13},{14,15},{16,17},{18,19},{..., dimensions={0}, use_global_device_ids=true | all-gather | bytes 638976 | tf_op jit(solution)/shard_map/all_gather | solution.py:518
  74.6 0.0 collective-permute-done.1.swap_ref
  74.6 4.6 %pick.1 = (bf16[512,4,384]{2,1,0:T(4,128)(2,1)S(1)}, bf16[512,4,128]{2,1,0:T(4,128)(2,1)S(1)}, f32[1,128]{1,0:T(1,128)}, f32[1,128]{1,0:T(1,128)}, s32[1,1]{1,0:T(1,128)}) custom-call(f32[512,128]{1,0:T(8,128)S(1)} %get-tuple-element.24.exps_ref, bf16[512,128]{1,0:T(8,128)(2,1)S(1)} %collective-permute-done.1.swap_ref, ...), custom_call_target="tpu_custom_call" | custom-call | tf_op jit(solution)/shard_map/pick/pallas_call | solution.py:385
  79.8 0.0 copy-start.2
  79.8 54.5 %all_to_all.20.panel_ref = bf16[512,4,384]{2,1,0:T(4,128)(2,1)S(1)} all-to-all(bf16[512,4,384]{2,1,0:T(4,128)(2,1)S(1)} %get-tuple-element.30), channel_id=1, replica_groups=mesh['state'=64,'seq'=8] {'state','seq'}, dimensions={0} | all-to-all | bytes 3145728 | tf_op jit(solution)/shard_map/all_to_all | solution.py:524
  134.4 0.0 copy-done.2
  134.4 5.7 %chain.1 = f32[1,1]{1,0:T(1,128)} custom-call(s32[1,128]{1,0:T(1,128)S(1)} %copy-done.2, s32[1,1]{1,0:T(1,128)} %get-tuple-element.29.full_ref, bf16[512,4,384]{2,1,0:T(4,128)(2,1)S(1)} %all_to_all.20.panel_ref, bf16[512,4,128]{2,1,0:T(4,128)(2,1)S(1)} %get-tuple-element.34.spare_ref), custom_call_target="tpu_custom_call" | custom-call | tf_op jit(solution)/shard_map/chain/pallas_call | solution.py:484
  (1 shorter events, 0.0 us)
Async XLA Ops:
  6.6 17.3 %copy-start = (bf16[128,512]{1,0:T(8,128)(2,1)S(1)}, bf16[128,512]{1,0:T(8,128)(2,1)}, u32[]{:S(2)}) copy-start(bf16[128,512]{1,0:T(8,128)(2,1)} %get-tuple-element.23.own_ref) | copy-start | bytes 393220
  6.7 49.9 %copy-start.1 = (bf16[128,512]{1,0:T(8,128)(2,1)S(1)}, bf16[128,512]{1,0:T(8,128)(2,1)}, u32[]{:S(2)}) copy-start(bf16[128,512]{1,0:T(8,128)(2,1)} %get-tuple-element.26.emit_ref) | copy-start | bytes 393220
  6.7 44.7 %all-to-all-start.1 = ((bf16[64,16,512]{2,1,0:T(8,128)(2,1)}), bf16[64,16,512]{2,1,0:T(8,128)(2,1)S(1)}, u32[]{:S(2)}, u32[]{:S(2)}) async-start(bf16[64,16,512]{2,1,0:T(8,128)(2,1)} %get-tuple-element.22), calls=%async_computation.1 | async-start | bytes 2097152 | tf_op jit(solution)/shard_map/all_to_all | solution.py:509
  24.0 26.0 %collective-permute-start = (bf16[128,512]{1,0:T(8,128)(2,1)S(1)}, bf16[128,512]{1,0:T(8,128)(2,1)S(1)}, u32[]{:S(2)}, u32[]{:S(2)}) collective-permute-start(bf16[128,512]{1,0:T(8,128)(2,1)S(1)} %copy-done), channel_id=1, source_target_pairs={{0,8},{8,0},{16,24},{24,16},{32,40},{40,32},{48,56},{56,48},{64,72... | collective-permute-start | bytes 393224 | tf_op jit(solution)/shard_map/ppermute | solution.py:508
  51.8 4.7 %collective-permute-start.2 = (f32[8,128]{1,0:T(8,128)S(1)}, f32[8,128]{1,0:T(8,128)S(1)}, u32[]{:S(2)}, u32[]{:S(2)}) collective-permute-start(f32[8,128]{1,0:T(8,128)S(1)} %get-tuple-element.28), channel_id=1, source_target_pairs={{0,8},{8,0},{16,24},{24,16},{32,40},{40,32},{48,56},{56,48},{64,72... | collective-permute-start | bytes 12296 | tf_op jit(solution)/shard_map/ppermute | solution.py:511
  57.8 9.3 %all-to-all-start.2 = ((bf16[4,208,128]{2,1,0:T(8,128)(2,1)}), bf16[4,208,128]{2,1,0:T(8,128)(2,1)S(1)}, u32[]{:S(2)}, u32[]{:S(2)}) async-start(bf16[4,208,128]{2,1,0:T(8,128)(2,1)} %words.1), calls=%async_computation.2 | async-start | bytes 425984 | tf_op jit(solution)/shard_map/all_to_all | solution.py:514
  61.8 12.9 %collective-permute-start.1 = (bf16[512,128]{1,0:T(8,128)(2,1)S(1)}, bf16[512,128]{1,0:T(8,128)(2,1)S(1)}, u32[]{:S(2)}, u32[]{:S(2)}) collective-permute-start(bf16[512,128]{1,0:T(8,128)(2,1)S(1)} %get-tuple-element.25), channel_id=1, source_target_pairs={{0,8},{8,0},{16,24},{24,16},{32,40},{40,32},{48,56},{56,48},{64,72... | collective-permute-start | bytes 393224 | tf_op jit(solution)/shard_map/ppermute | solution.py:512
  79.8 54.6 %copy-start.2 = (s32[1,128]{1,0:T(1,128)S(1)}, s32[1,128]{1,0:T(1,128)}, u32[]{:S(2)}) copy-start(s32[1,128]{1,0:T(1,128)} %get-tuple-element.21.slot_ref) | copy-start | bytes 1540

commit v8 on v6

--- a/solution.py
+++ b/solution.py
@@ -283,9 +283,67 @@
     return call(words_kernel, "words", outs, scratch, msg, emit_kept, z_part, swapped)[0]
 
 
+def pick_slots(asked, share, first, count, outs, table, emits, next_rows, word_rows, stage):
+    size = count * LANES
+    row, lane = iota((size, LANES), 0), iota((size, LANES), 1)
+    pick_row, pick_lane = iota((size, 64), 0), iota((size, 64), 1)
+    mine = ((lane >> 4) == ((row >> 3) & 7)) & ((lane & 3) == (row >> 7) + first)
+    next_at = mine & ((lane & 15) < 4)
+    key_at = mine & ((lane & 15) >= 4) & ((lane & 15) < 12)
+    ones = jnp.ones((LANES, LANES), bf16)
+    weights = jnp.where((iota((LANES, LANES), 0) & 15) >= 8, 64.0, 1.0).astype(bf16)
+    lane_f = lane.astype(f32)
+    row_of = lane & (KW - 1)
+    found = []
+    for step in range(4):
+        source = (pick_row & 7) * 8 + step * 2 + ((pick_row >> 6) & 1)
+        spread = jnp.dot(one_hot(pick_lane == source), asked, preferred_element_type=f32)
+        block = jnp.dot(
+            jnp.where(next_at, spread, 0.0).astype(bf16), ones, preferred_element_type=f32
+        )
+        key = jnp.dot(
+            jnp.where(key_at, spread, 0.0).astype(bf16), weights, preferred_element_type=f32
+        )
+        found.append((block, key))
+    for step in range(4):
+        rows = slice(step * size, (step + 1) * size)
+        block, key = found[step]
+        second = key >= 2048.0
+        key = jnp.where(second, key - 2048.0, key)
+        key = jnp.where(key >= 768.0, key - 768.0, key)
+        hit = block == lane_f
+        next_rows[rows, :LANES] = one_hot(hit & ~second)
+        next_rows[rows, LANES:] = one_hot(hit & second)
+        for n in range(6):
+            word_rows[rows, n * LANES : (n + 1) * LANES] = one_hot(key == lane_f + float(n * LANES))
+    for step in range(4):
+        rows = slice(step * size, (step + 1) * size)
+        got = jnp.dot(word_rows[rows, :], emits[...], preferred_element_type=f32)
+        panels = jnp.dot(next_rows[rows, :], table[...], preferred_element_type=f32)
+        block, key = found[step]
+        second = key >= 2048.0
+        late = jnp.where(second, key - 2048.0, key) >= 768.0
+        emit = jnp.where(late, got[:, LANES:], got[:, :LANES])
+        emit = jnp.where((lane_f < float(KW)) ^ second, emit, pltpu.roll(emit, KW, 1))
+        last = block == float(LANES)
+        base = step * 4 * size
+        for pair in range(4):
+            column = (pair * 2 + (lane >> 6)) * 8 + share
+            panel = panels[:, pair * LANES : (pair + 1) * LANES]
+            panel = jnp.where(last & (row_of == column), 1.0, panel) * emit
+            for n in range(count):
+                stage[pl.ds(base + n * 512 + pair, LANES, stride=4), :] = panel[
+                    n * LANES : (n + 1) * LANES, :
+                ]
+        for n in range(count):
+            block = stage[base + n * 512 : base + (n + 1) * 512, :]
+            block = block.reshape(LANES, 4, LANES).astype(bf16)
+            outs[0][step * LANES : (step + 1) * LANES, :, n * LANES : (n + 1) * LANES] = block
+
+
 def pick_kernel(
     exps_ref, swap_ref, all_ref, panel_ref, spare_ref, trans_ref, emit_ref, full_ref,
-    halves, table, emits, next_rows, word_rows, blocks, keys, stage,
+    halves, table, emits, next_rows, word_rows, stage,
 ):
     share = lax.axis_index("seq")
     order = [(g & 1) * 4 + (g >> 1) for g in range(8)]
@@ -323,64 +381,15 @@
         lanes = slice(pair * LANES, (pair + 1) * LANES)
         table[0:LANES, lanes] = jnp.where(low, first, pltpu.roll(second, KW, 1)).astype(bf16)
         table[LANES:, lanes] = jnp.where(low, pltpu.roll(first, KW, 1), second).astype(bf16)
-    row, lane = iota((512, LANES), 0), iota((512, LANES), 1)
-    pick_row, pick_lane = iota((512, 64), 0), iota((512, 64), 1)
-    mine = ((lane >> 4) == ((row >> 3) & 7)) & ((lane & 3) == (row >> 7))
-    next_at = mine & ((lane & 15) < 4)
-    key_at = mine & ((lane & 15) >= 4) & ((lane & 15) < 12)
-    ones = jnp.ones((LANES, LANES), bf16)
-    weights = jnp.where((iota((LANES, LANES), 0) & 15) >= 8, 64.0, 1.0).astype(bf16)
     asked = jnp.concatenate([all_ref[n, 192:200, :].astype(f32) for n in order], axis=0)
     asked = asked.astype(bf16)
-    lane_f = lane.astype(f32)
-    row_of = lane & (KW - 1)
-    for step in range(4):
-        source = (pick_row & 7) * 8 + step * 2 + ((pick_row >> 6) & 1)
-        spread = jnp.dot(one_hot(pick_lane == source), asked, preferred_element_type=f32)
-        block = jnp.dot(
-            jnp.where(next_at, spread, 0.0).astype(bf16), ones, preferred_element_type=f32
+    pick_slots(asked, share, 0, SENT, (panel_ref,), table, emits, next_rows, word_rows, stage)
+
+    @pl.when(jnp.max(full) > 0.5)
+    def _():
+        pick_slots(
+            asked, share, SENT, SLOTS - SENT, (spare_ref,), table, emits, next_rows, word_rows, stage
         )
-        key = jnp.dot(
-            jnp.where(key_at, spread, 0.0).astype(bf16), weights, preferred_element_type=f32
-        )
-        blocks[step * 512 : (step + 1) * 512, :] = block
-        keys[step * 512 : (step + 1) * 512, :] = key
-    for step in range(4):
-        rows = slice(step * 512, (step + 1) * 512)
-        block, key = blocks[rows, :], keys[rows, :]
-        second = key >= 2048.0
-        key = jnp.where(second, key - 2048.0, key)
-        key = jnp.where(key >= 768.0, key - 768.0, key)
-        hit = block == lane_f
-        next_rows[rows, :LANES] = one_hot(hit & ~second)
-        next_rows[rows, LANES:] = one_hot(hit & second)
-        for n in range(6):
-            word_rows[rows, n * LANES : (n + 1) * LANES] = one_hot(key == lane_f + float(n * LANES))
-    for step in range(4):
-        rows = slice(step * 512, (step + 1) * 512)
-        got = jnp.dot(word_rows[rows, :], emits[...], preferred_element_type=f32)
-        panels = jnp.dot(next_rows[rows, :], table[...], preferred_element_type=f32)
-        block, key = blocks[rows, :], keys[rows, :]
-        second = key >= 2048.0
-        late = jnp.where(second, key - 2048.0, key) >= 768.0
-        emit = jnp.where(late, got[:, LANES:], got[:, :LANES])
-        emit = jnp.where((lane_f < float(KW)) ^ second, emit, pltpu.roll(emit, KW, 1))
-        last = block == float(LANES)
-        for pair in range(4):
-            column = (pair * 2 + (lane >> 6)) * 8 + share
-            panel = panels[:, pair * LANES : (pair + 1) * LANES]
-            panel = jnp.where(last & (row_of == column), 1.0, panel) * emit
-            for n in range(SLOTS):
-                stage[pl.ds(step * 2048 + n * 512 + pair, LANES, stride=4), :] = panel[
-                    n * LANES : (n + 1) * LANES, :
-                ]
-        for n in range(SLOTS):
-            block = stage[step * 2048 + n * 512 : step * 2048 + (n + 1) * 512, :]
-            block = block.reshape(LANES, 4, LANES).astype(bf16)
-            if n < SENT:
-                panel_ref[step * LANES : (step + 1) * LANES, :, n * LANES : (n + 1) * LANES] = block
-            else:
-                spare_ref[step * LANES : (step + 1) * LANES, :, :] = block
 
 
 def pick(exps, swapped, everything):
@@ -402,8 +411,6 @@
             pltpu.VMEM((768, 256), bf16),
             pltpu.VMEM((2048, 256), bf16),
             pltpu.VMEM((2048, 768), bf16),
-            pltpu.VMEM((2048, LANES), f32),
-            pltpu.VMEM((2048, LANES), f32),
             pltpu.VMEM((8192, LANES), f32),
         ],
         compiler_params=pltpu.CompilerParams(vmem_limit_bytes=40 * 1024 * 1024),
@@ -441,14 +448,14 @@
             ping[t] = jnp.concatenate(move, axis=0).astype(bf16)
         return 0
 
-    lax.fori_loop(0, length // 8, build, 0, unroll=2)
+    lax.fori_loop(0, length // 8, build, 0, unroll=4)
     peak = jnp.max(logs[0:length, :], axis=1, keepdims=True)
     tops[...] = jnp.broadcast_to((1.0 / peak).astype(bf16).astype(f32), (length, LANES))
     logs[0:length, :] = 1.0 / tops[...]
     logs[length:, :] = jnp.ones((length, LANES), f32)
     src, dst, count, base = ping, pong, length // 2, length
     while count > 1:
-        unroll = min(count, 32)
+        unroll = min(count, 64)
 
         def level(i, _, src=src, dst=dst, unroll=unroll, base=base, first=src is ping and base == length):
             for u in range(unroll):

time: 140 us -> 139 us (level)
  no operation moved by 1% of the time
where the time goes in v8:
time: 139 us; the launch traced here: 138 us
  blocking collectives  70.5 us (51%)
  waiting for transfers between devices  26.9 us (19%)
  starting transfers between devices  23.9 us (17%)
  Pallas kernels  15.7 us (11%)
    all_to_all x1, blocking collectives, exchange(): lax.all_to_all(value, ('state', 'seq'), split_axis=0, concat_axis=0, tile...  53.9 us
    ppermute x1, waiting for transfers between devices, local(): other = lax.ppermute(out_kept, 'state', pairs)  23 us
    all_to_all x1, starting transfers between devices, local(): lax.all_to_all(msg, 'state', split_axis=0, concat_axis=0, tiled=True)  17.3 us
    all_to_all x1, blocking collectives, local(): lax.all_to_all(mine, 'seq', split_axis=0, concat_axis=0, tiled=True, axis...  9.09 us
    all_gather x1, blocking collectives, local(): lax.all_gather(along_x, 'seq', axis=0, tiled=True, axis_index_groups=[[0,...  7.59 us
    pallas_call x1, Pallas kernels, prep(): pl.pallas_call(prep_kernel, out_shape=(jax.ShapeDtypeStruct((SHARDS, ROWS...  6.01 us
    pallas_call x1, Pallas kernels, chain(): pl.pallas_call(chain_kernel, out_shape=jax.ShapeDtypeStruct((1, 1), f32),...  4.84 us
    pallas_call x1, Pallas kernels, pick(): pl.pallas_call(pick_kernel, out_shape=(jax.ShapeDtypeStruct((512, 4, SENT...  3.87 us
  transfers between devices with their start and end apart: 3, of which 3 were waited for; matrix products, arithmetic and copies ran while one was open for 0% of the time, Pallas kernels for 0%

profile of v8, /device:TPU:1, one launch (start us, length us, event | category | flops | bytes accessed | tf_op | source)
XLA Modules:
  0.0 138.4 jit_solution(14433456411602784981)
XLA Ops:
  0.6 6.0 %prep.1 = (bf16[64,16,512]{2,1,0:T(8,128)(2,1)}, bf16[128,512]{1,0:T(8,128)(2,1)}, bf16[128,512]{1,0:T(8,128)(2,1)}, s32[1,128]{1,0:T(1,128)}) custom-call(s32[2,128]{1,0:T(2,128)} %bitcast.8, s32[1,128]{1,0:T(1,128)} %tokens_hbm.1, s32[1,128]{1,0:T(1,128)} %tokens_hbm.1, s32[1024,128]{1,0:T(8,128)} %bitcast.7, s32[1,128]{1,0:T(1,128)} %bitcast.9, ...), custom_call_target="tpu_custom_call" | custom-call | tf_op jit(solution)/shard_map/prep/pallas_call | solution.py:165
  6.7 0.0 copy-start.1
  6.7 0.0 copy-start
  6.7 17.3 %all-to-all-start.1 = ((bf16[64,16,512]{2,1,0:T(8,128)(2,1)}), bf16[64,16,512]{2,1,0:T(8,128)(2,1)S(1)}, u32[]{:S(2)}, u32[]{:S(2)}) async-start(bf16[64,16,512]{2,1,0:T(8,128)(2,1)} %get-tuple-element.21), calls=%async_computation.1 | async-start | bytes 2097152 | tf_op jit(solution)/shard_map/all_to_all | solution.py:510
  24.0 0.0 copy-done.1
  24.0 2.9 %collective-permute-start = (bf16[128,512]{1,0:T(8,128)(2,1)S(1)}, bf16[128,512]{1,0:T(8,128)(2,1)S(1)}, u32[]{:S(2)}, u32[]{:S(2)}) collective-permute-start(bf16[128,512]{1,0:T(8,128)(2,1)S(1)} %copy-done.1), channel_id=1, source_target_pairs={{0,8},{8,0},{16,24},{24,16},{32,40},{40,32},{48,56},{56,48},{64,72... | collective-permute-start | bytes 393224 | tf_op jit(solution)/shard_map/ppermute | solution.py:509
  26.9 23.0 %collective-permute-done.other_ref = bf16[128,512]{1,0:T(8,128)(2,1)S(1)} collective-permute-done((bf16[128,512]{1,0:T(8,128)(2,1)S(1)}, bf16[128,512]{1,0:T(8,128)(2,1)S(1)}, u32[]{:S(2)}, u32[]{:S(2)}) %collective-permute-start) | collective-permute-done | bytes 131104 | tf_op jit(solution)/shard_map/ppermute | solution.py:509
  49.9 1.4 %all-to-all-done.1.msg_ref = bf16[64,16,512]{2,1,0:T(8,128)(2,1)S(1)} async-done(((bf16[64,16,512]{2,1,0:T(8,128)(2,1)}), bf16[64,16,512]{2,1,0:T(8,128)(2,1)S(1)}, u32[]{:S(2)}, u32[]{:S(2)}) %all-to-all-start.1) | async-done | bytes 1048608 | tf_op jit(solution)/shard_map/all_to_all | solution.py:510
  51.4 0.5 score.1
  51.9 3.7 %collective-permute-start.1 = (bf16[528,128]{1,0:T(8,128)(2,1)S(1)}, bf16[528,128]{1,0:T(8,128)(2,1)S(1)}, u32[]{:S(2)}, u32[]{:S(2)}) collective-permute-start(bf16[528,128]{1,0:T(8,128)(2,1)S(1)} %get-tuple-element.24), channel_id=1, source_target_pairs={{0,8},{8,0},{16,24},{24,16},{32,40},{40,32},{48,56},{56,48},{64,72... | collective-permute-start | bytes 405512 | tf_op jit(solution)/shard_map/ppermute | solution.py:512
  55.6 2.4 %collective-permute-done.1.swap_ref = bf16[528,128]{1,0:T(8,128)(2,1)S(1)} collective-permute-done((bf16[528,128]{1,0:T(8,128)(2,1)S(1)}, bf16[528,128]{1,0:T(8,128)(2,1)S(1)}, u32[]{:S(2)}, u32[]{:S(2)}) %collective-permute-start.1) | collective-permute-done | bytes 135200 | tf_op jit(solution)/shard_map/ppermute | solution.py:512
  58.0 0.0 copy-done
  58.0 0.5 words.1
  58.5 9.1 %all_to_all.20 = bf16[4,208,128]{2,1,0:T(8,128)(2,1)S(1)} all-to-all(bf16[4,208,128]{2,1,0:T(8,128)(2,1)S(1)} %words.1), channel_id=1, replica_groups={{0,2,4,6},{1,3,5,7},{8,10,12,14},{9,11,13,15},{16,18,20,22},{17,19,21,2..., dimensions={0} | all-to-all | bytes 425984 | tf_op jit(solution)/shard_map/all_to_all | solution.py:514
  67.6 7.6 %all_gather.3.all_ref = bf16[8,208,128]{2,1,0:T(8,128)(2,1)S(1)} all-gather(bf16[4,208,128]{2,1,0:T(8,128)(2,1)S(1)} %all_to_all.20), channel_id=1, replica_groups={{0,1},{2,3},{4,5},{6,7},{8,9},{10,11},{12,13},{14,15},{16,17},{18,19},{..., dimensions={0}, use_global_device_ids=true | all-gather | bytes 638976 | tf_op jit(solution)/shard_map/all_gather | solution.py:518
  75.1 3.9 %pick.1 = (bf16[512,4,384]{2,1,0:T(4,128)(2,1)S(1)}, bf16[512,4,128]{2,1,0:T(4,128)(2,1)S(1)}, f32[1,128]{1,0:T(1,128)}, f32[1,128]{1,0:T(1,128)}, s32[1,1]{1,0:T(1,128)}) custom-call(f32[512,128]{1,0:T(8,128)S(1)} %get-tuple-element.23.exps_ref, bf16[528,128]{1,0:T(8,128)(2,1)S(1)} %collective-permute-done.1.swap_ref, ...), custom_call_target="tpu_custom_call" | custom-call | tf_op jit(solution)/shard_map/pick/pallas_call | solution.py:397
  79.7 0.0 copy-start.2
  79.7 53.9 %all_to_all.21.panel_ref = bf16[512,4,384]{2,1,0:T(4,128)(2,1)S(1)} all-to-all(bf16[512,4,384]{2,1,0:T(4,128)(2,1)S(1)} %get-tuple-element.27), channel_id=1, replica_groups=mesh['state'=64,'seq'=8] {'state','seq'}, dimensions={0} | all-to-all | bytes 3145728 | tf_op jit(solution)/shard_map/all_to_all | solution.py:524
  133.5 0.0 copy-done.2
  133.5 4.8 %chain.1 = f32[1,1]{1,0:T(1,128)} custom-call(s32[1,128]{1,0:T(1,128)S(1)} %copy-done.2, bf16[512,4,384]{2,1,0:T(4,128)(2,1)S(1)} %all_to_all.21.panel_ref, bf16[512,4,128]{2,1,0:T(4,128)(2,1)S(1)} %get-tuple-element.32.spare_ref), custom_call_target="tpu_custom_call" | custom-call | tf_op jit(solution)/shard_map/chain/pallas_call | solution.py:485
  (1 shorter events, 0.0 us)
Async XLA Ops:
  6.7 17.3 %copy-start.1 = (bf16[128,512]{1,0:T(8,128)(2,1)S(1)}, bf16[128,512]{1,0:T(8,128)(2,1)}, u32[]{:S(2)}) copy-start(bf16[128,512]{1,0:T(8,128)(2,1)} %get-tuple-element.22.own_ref) | copy-start | bytes 393220
  6.7 51.3 %copy-start = (bf16[128,512]{1,0:T(8,128)(2,1)S(1)}, bf16[128,512]{1,0:T(8,128)(2,1)}, u32[]{:S(2)}) copy-start(bf16[128,512]{1,0:T(8,128)(2,1)} %get-tuple-element.25.emit_ref) | copy-start | bytes 393220
  6.7 44.7 %all-to-all-start.1 = ((bf16[64,16,512]{2,1,0:T(8,128)(2,1)}), bf16[64,16,512]{2,1,0:T(8,128)(2,1)S(1)}, u32[]{:S(2)}, u32[]{:S(2)}) async-start(bf16[64,16,512]{2,1,0:T(8,128)(2,1)} %get-tuple-element.21), calls=%async_computation.1 | async-start | bytes 2097152 | tf_op jit(solution)/shard_map/all_to_all | solution.py:510
  24.0 26.0 %collective-permute-start = (bf16[128,512]{1,0:T(8,128)(2,1)S(1)}, bf16[128,512]{1,0:T(8,128)(2,1)S(1)}, u32[]{:S(2)}, u32[]{:S(2)}) collective-permute-start(bf16[128,512]{1,0:T(8,128)(2,1)S(1)} %copy-done.1), channel_id=1, source_target_pairs={{0,8},{8,0},{16,24},{24,16},{32,40},{40,32},{48,56},{56,48},{64,72... | collective-permute-start | bytes 393224 | tf_op jit(solution)/shard_map/ppermute | solution.py:509
  51.9 6.1 %collective-permute-start.1 = (bf16[528,128]{1,0:T(8,128)(2,1)S(1)}, bf16[528,128]{1,0:T(8,128)(2,1)S(1)}, u32[]{:S(2)}, u32[]{:S(2)}) collective-permute-start(bf16[528,128]{1,0:T(8,128)(2,1)S(1)} %get-tuple-element.24), channel_id=1, source_target_pairs={{0,8},{8,0},{16,24},{24,16},{32,40},{40,32},{48,56},{56,48},{64,72... | collective-permute-start | bytes 405512 | tf_op jit(solution)/shard_map/ppermute | solution.py:512
  79.7 53.9 %copy-start.2 = (s32[1,128]{1,0:T(1,128)S(1)}, s32[1,128]{1,0:T(1,128)}, u32[]{:S(2)}) copy-start(s32[1,128]{1,0:T(1,128)} %get-tuple-element.20.slot_ref) | copy-start | bytes 1540

commit v9 on v8

--- a/solution.py
+++ b/solution.py
@@ -279,7 +279,7 @@
 
 def words(msg, emit_kept, z_part, swapped):
     outs = [((4, XROWS, LANES), bf16)]
-    scratch = [((512, LANES), f32)] * 2
+    scratch = [((576, LANES), f32)] * 2
     return call(words_kernel, "words", outs, scratch, msg, emit_kept, z_part, swapped)[0]
 
 
@@ -406,12 +406,12 @@
         in_specs=[vmem] * 3,
         out_specs=(vmem,) * 5,
         scratch_shapes=[
-            pltpu.VMEM((1024, LANES), f32),
+            pltpu.VMEM((1032, LANES), f32),
             pltpu.VMEM((256, 512), bf16),
             pltpu.VMEM((768, 256), bf16),
             pltpu.VMEM((2048, 256), bf16),
             pltpu.VMEM((2048, 768), bf16),
-            pltpu.VMEM((8192, LANES), f32),
+            pltpu.VMEM((8200, LANES), f32),
         ],
         compiler_params=pltpu.CompilerParams(vmem_limit_bytes=40 * 1024 * 1024),
         name="pick",
@@ -488,7 +488,7 @@
         in_specs=[pl.BlockSpec(memory_space=pltpu.SMEM), vmem, vmem],
         out_specs=vmem,
         scratch_shapes=[
-            pltpu.VMEM((SLOTS * 4096, LANES), f32),
+            pltpu.VMEM((SLOTS * 4096 + 64, LANES), f32),
             pltpu.VMEM((length, KW, LANES), bf16),
             pltpu.VMEM((length // 2, KW, LANES), bf16),
             pltpu.VMEM((2 * length, LANES), f32),

time: 139 us -> 139 us (level)
  no operation moved by 1% of the time
where the time goes in v9:
time: 139 us; the launch traced here: 138 us
  blocking collectives  70.5 us (51%)
  waiting for transfers between devices  26.9 us (19%)
  starting transfers between devices  23.9 us (17%)
  Pallas kernels  15.7 us (11%)
    all_to_all x1, blocking collectives, exchange(): lax.all_to_all(value, ('state', 'seq'), split_axis=0, concat_axis=0, tile...  53.9 us
    ppermute x1, waiting for transfers between devices, local(): other = lax.ppermute(out_kept, 'state', pairs)  23 us
    all_to_all x1, starting transfers between devices, local(): lax.all_to_all(msg, 'state', split_axis=0, concat_axis=0, tiled=True)  17.3 us
    all_to_all x1, blocking collectives, local(): lax.all_to_all(mine, 'seq', split_axis=0, concat_axis=0, tiled=True, axis...  9.09 us
    all_gather x1, blocking collectives, local(): lax.all_gather(along_x, 'seq', axis=0, tiled=True, axis_index_groups=[[0,...  7.59 us
    pallas_call x1, Pallas kernels, prep(): pl.pallas_call(prep_kernel, out_shape=(jax.ShapeDtypeStruct((SHARDS, ROWS...  6.01 us
    pallas_call x1, Pallas kernels, chain(): pl.pallas_call(chain_kernel, out_shape=jax.ShapeDtypeStruct((1, 1), f32),...  4.84 us
    pallas_call x1, Pallas kernels, pick(): pl.pallas_call(pick_kernel, out_shape=(jax.ShapeDtypeStruct((512, 4, SENT...  3.87 us
  transfers between devices with their start and end apart: 3, of which 3 were waited for; matrix products, arithmetic and copies ran while one was open for 0% of the time, Pallas kernels for 0%

profile of v9, /device:TPU:1, one launch (start us, length us, event | category | flops | bytes accessed | tf_op | source)
XLA Modules:
  0.0 138.4 jit_solution(2415882750800977413)
XLA Ops:
  0.6 6.0 %prep.1 = (bf16[64,16,512]{2,1,0:T(8,128)(2,1)}, bf16[128,512]{1,0:T(8,128)(2,1)}, bf16[128,512]{1,0:T(8,128)(2,1)}, s32[1,128]{1,0:T(1,128)}) custom-call(s32[2,128]{1,0:T(2,128)} %bitcast.8, s32[1,128]{1,0:T(1,128)} %tokens_hbm.1, s32[1,128]{1,0:T(1,128)} %tokens_hbm.1, s32[1024,128]{1,0:T(8,128)} %bitcast.7, s32[1,128]{1,0:T(1,128)} %bitcast.9, ...), custom_call_target="tpu_custom_call" | custom-call | tf_op jit(solution)/shard_map/prep/pallas_call | solution.py:165
  6.7 0.0 copy-start.1
  6.7 0.0 copy-start
  6.7 17.3 %all-to-all-start.1 = ((bf16[64,16,512]{2,1,0:T(8,128)(2,1)}), bf16[64,16,512]{2,1,0:T(8,128)(2,1)S(1)}, u32[]{:S(2)}, u32[]{:S(2)}) async-start(bf16[64,16,512]{2,1,0:T(8,128)(2,1)} %get-tuple-element.21), calls=%async_computation.1 | async-start | bytes 2097152 | tf_op jit(solution)/shard_map/all_to_all | solution.py:510
  24.0 0.0 copy-done.1
  24.0 2.9 %collective-permute-start = (bf16[128,512]{1,0:T(8,128)(2,1)S(1)}, bf16[128,512]{1,0:T(8,128)(2,1)S(1)}, u32[]{:S(2)}, u32[]{:S(2)}) collective-permute-start(bf16[128,512]{1,0:T(8,128)(2,1)S(1)} %copy-done.1), channel_id=1, source_target_pairs={{0,8},{8,0},{16,24},{24,16},{32,40},{40,32},{48,56},{56,48},{64,72... | collective-permute-start | bytes 393224 | tf_op jit(solution)/shard_map/ppermute | solution.py:509
  26.9 23.0 %collective-permute-done.other_ref = bf16[128,512]{1,0:T(8,128)(2,1)S(1)} collective-permute-done((bf16[128,512]{1,0:T(8,128)(2,1)S(1)}, bf16[128,512]{1,0:T(8,128)(2,1)S(1)}, u32[]{:S(2)}, u32[]{:S(2)}) %collective-permute-start) | collective-permute-done | bytes 131104 | tf_op jit(solution)/shard_map/ppermute | solution.py:509
  49.9 1.4 %all-to-all-done.1.msg_ref = bf16[64,16,512]{2,1,0:T(8,128)(2,1)S(1)} async-done(((bf16[64,16,512]{2,1,0:T(8,128)(2,1)}), bf16[64,16,512]{2,1,0:T(8,128)(2,1)S(1)}, u32[]{:S(2)}, u32[]{:S(2)}) %all-to-all-start.1) | async-done | bytes 1048608 | tf_op jit(solution)/shard_map/all_to_all | solution.py:510
  51.4 0.5 score.1
  51.9 3.7 %collective-permute-start.1 = (bf16[528,128]{1,0:T(8,128)(2,1)S(1)}, bf16[528,128]{1,0:T(8,128)(2,1)S(1)}, u32[]{:S(2)}, u32[]{:S(2)}) collective-permute-start(bf16[528,128]{1,0:T(8,128)(2,1)S(1)} %get-tuple-element.24), channel_id=1, source_target_pairs={{0,8},{8,0},{16,24},{24,16},{32,40},{40,32},{48,56},{56,48},{64,72... | collective-permute-start | bytes 405512 | tf_op jit(solution)/shard_map/ppermute | solution.py:512
  55.6 2.4 %collective-permute-done.1.swap_ref = bf16[528,128]{1,0:T(8,128)(2,1)S(1)} collective-permute-done((bf16[528,128]{1,0:T(8,128)(2,1)S(1)}, bf16[528,128]{1,0:T(8,128)(2,1)S(1)}, u32[]{:S(2)}, u32[]{:S(2)}) %collective-permute-start.1) | collective-permute-done | bytes 135200 | tf_op jit(solution)/shard_map/ppermute | solution.py:512
  58.0 0.0 copy-done
  58.0 0.5 words.1
  58.5 9.1 %all_to_all.20 = bf16[4,208,128]{2,1,0:T(8,128)(2,1)S(1)} all-to-all(bf16[4,208,128]{2,1,0:T(8,128)(2,1)S(1)} %words.1), channel_id=1, replica_groups={{0,2,4,6},{1,3,5,7},{8,10,12,14},{9,11,13,15},{16,18,20,22},{17,19,21,2..., dimensions={0} | all-to-all | bytes 425984 | tf_op jit(solution)/shard_map/all_to_all | solution.py:514
  67.6 7.6 %all_gather.3.all_ref = bf16[8,208,128]{2,1,0:T(8,128)(2,1)S(1)} all-gather(bf16[4,208,128]{2,1,0:T(8,128)(2,1)S(1)} %all_to_all.20), channel_id=1, replica_groups={{0,1},{2,3},{4,5},{6,7},{8,9},{10,11},{12,13},{14,15},{16,17},{18,19},{..., dimensions={0}, use_global_device_ids=true | all-gather | bytes 638976 | tf_op jit(solution)/shard_map/all_gather | solution.py:518
  75.1 3.9 %pick.1 = (bf16[512,4,384]{2,1,0:T(4,128)(2,1)S(1)}, bf16[512,4,128]{2,1,0:T(4,128)(2,1)S(1)}, f32[1,128]{1,0:T(1,128)}, f32[1,128]{1,0:T(1,128)}, s32[1,1]{1,0:T(1,128)}) custom-call(f32[512,128]{1,0:T(8,128)S(1)} %get-tuple-element.23.exps_ref, bf16[528,128]{1,0:T(8,128)(2,1)S(1)} %collective-permute-done.1.swap_ref, ...), custom_call_target="tpu_custom_call" | custom-call | tf_op jit(solution)/shard_map/pick/pallas_call | solution.py:397
  79.7 0.0 copy-start.2
  79.7 53.9 %all_to_all.21.panel_ref = bf16[512,4,384]{2,1,0:T(4,128)(2,1)S(1)} all-to-all(bf16[512,4,384]{2,1,0:T(4,128)(2,1)S(1)} %get-tuple-element.27), channel_id=1, replica_groups=mesh['state'=64,'seq'=8] {'state','seq'}, dimensions={0} | all-to-all | bytes 3145728 | tf_op jit(solution)/shard_map/all_to_all | solution.py:524
  133.5 0.0 copy-done.2
  133.5 4.8 %chain.1 = f32[1,1]{1,0:T(1,128)} custom-call(s32[1,128]{1,0:T(1,128)S(1)} %copy-done.2, bf16[512,4,384]{2,1,0:T(4,128)(2,1)S(1)} %all_to_all.21.panel_ref, bf16[512,4,128]{2,1,0:T(4,128)(2,1)S(1)} %get-tuple-element.32.spare_ref), custom_call_target="tpu_custom_call" | custom-call | tf_op jit(solution)/shard_map/chain/pallas_call | solution.py:485
  (1 shorter events, 0.0 us)
Async XLA Ops:
  6.7 17.3 %copy-start.1 = (bf16[128,512]{1,0:T(8,128)(2,1)S(1)}, bf16[128,512]{1,0:T(8,128)(2,1)}, u32[]{:S(2)}) copy-start(bf16[128,512]{1,0:T(8,128)(2,1)} %get-tuple-element.22.own_ref) | copy-start | bytes 393220
  6.7 51.3 %copy-start = (bf16[128,512]{1,0:T(8,128)(2,1)S(1)}, bf16[128,512]{1,0:T(8,128)(2,1)}, u32[]{:S(2)}) copy-start(bf16[128,512]{1,0:T(8,128)(2,1)} %get-tuple-element.25.emit_ref) | copy-start | bytes 393220
  6.7 44.7 %all-to-all-start.1 = ((bf16[64,16,512]{2,1,0:T(8,128)(2,1)}), bf16[64,16,512]{2,1,0:T(8,128)(2,1)S(1)}, u32[]{:S(2)}, u32[]{:S(2)}) async-start(bf16[64,16,512]{2,1,0:T(8,128)(2,1)} %get-tuple-element.21), calls=%async_computation.1 | async-start | bytes 2097152 | tf_op jit(solution)/shard_map/all_to_all | solution.py:510
  24.0 26.0 %collective-permute-start = (bf16[128,512]{1,0:T(8,128)(2,1)S(1)}, bf16[128,512]{1,0:T(8,128)(2,1)S(1)}, u32[]{:S(2)}, u32[]{:S(2)}) collective-permute-start(bf16[128,512]{1,0:T(8,128)(2,1)S(1)} %copy-done.1), channel_id=1, source_target_pairs={{0,8},{8,0},{16,24},{24,16},{32,40},{40,32},{48,56},{56,48},{64,72... | collective-permute-start | bytes 393224 | tf_op jit(solution)/shard_map/ppermute | solution.py:509
  51.9 6.1 %collective-permute-start.1 = (bf16[528,128]{1,0:T(8,128)(2,1)S(1)}, bf16[528,128]{1,0:T(8,128)(2,1)S(1)}, u32[]{:S(2)}, u32[]{:S(2)}) collective-permute-start(bf16[528,128]{1,0:T(8,128)(2,1)S(1)} %get-tuple-element.24), channel_id=1, source_target_pairs={{0,8},{8,0},{16,24},{24,16},{32,40},{40,32},{48,56},{56,48},{64,72... | collective-permute-start | bytes 405512 | tf_op jit(solution)/shard_map/ppermute | solution.py:512
  79.7 53.9 %copy-start.2 = (s32[1,128]{1,0:T(1,128)S(1)}, s32[1,128]{1,0:T(1,128)}, u32[]{:S(2)}) copy-start(s32[1,128]{1,0:T(1,128)} %get-tuple-element.20.slot_ref) | copy-start | bytes 1540
